TPU v7x, 32 devices: a whole 2x2x4 slice. The times are simulated.
32 devices in a mesh: exp: 16 (over z, y, x), head: 2 (over core).
Axes of the slice: x: 2, y: 2, z: 4, core: 2. Of those that a mesh axis runs over, the one named last changes fastest.
Arguments:
- block_input: bfloat16 [10240, 1024], P(('exp', 'head')), may hold values from -6 to 6
- dispatch: int32 [8192], P(('exp', 'head')), may hold values from 0 to 319, as said below
- lengths: int32 [16, 5], P('exp'), may hold values from 64 to 256, as said below
- ln1_gain: float32 [1024], replicated, may hold values from 0.5 to 1.5
- ln1_bias: float32 [1024], replicated, may hold values from -2 to 2
- ln2_gain: float32 [1024], replicated, may hold values from 0.5 to 1.5
- ln2_bias: float32 [1024], replicated, may hold values from -2 to 2
- w_qkv: bfloat16 [3, 1024, 1024], P(None, None, 'head'), may hold values from -0.1875 to 0.1875
- w_out: bfloat16 [1024, 1024], P('head'), may hold values from -1.5 to 1.5
- w_up: bfloat16 [16, 1024, 4096], P('exp', None, 'head'), may hold values from -0.1875 to 0.1875
- w_down: bfloat16 [16, 4096, 1024], P('exp', 'head'), may hold values from -0.09375 to 0.09375
- grad_output: bfloat16 [10240, 1024], P(('exp', 'head')), may hold values from -6 to 6
Outputs:
- block_output: bfloat16 [10240, 1024], P(('exp', 'head'))
- grad_input: float32 [10240, 1024], P(('exp', 'head'))
- grad_ln1_gain: float32 [1024], replicated
- grad_ln1_bias: float32 [1024], replicated
- grad_ln2_gain: float32 [1024], replicated
- grad_ln2_bias: float32 [1024], replicated
- grad_w_qkv: float32 [3, 1024, 1024], P(None, None, 'head')
- grad_w_out: float32 [1024, 1024], P('head')
- grad_w_up: float32 [16, 1024, 4096], P('exp', None, 'head')
- grad_w_down: float32 [16, 4096, 1024], P('exp', 'head')
Inputs may be any that keep to these rules, and one draw needn't show every extreme that they name: `dispatch`: on each device's 256 tokens the values are distinct; value d sends the token to expert-order device d // 10, and the values one device sends to one destination are that destination's block start plus 0, 1, 2 and so on without gaps. In every draw one destination gets 10 tokens from every device. `lengths`: each row holds one sequence of 256 tokens, neither first nor last, and four sequences of 64 tokens.
All inputs are finite; a program needn't handle non-finite values.
Results may differ from a plain program's by a relative error of at most 0.015.
Values may be sent and summed in bfloat16 or wider, within the bound.
No kernel may reach another device: no remote copies, remote signals or barrier semaphores. Data moves between devices by JAX's collectives and lax.ppermute only.
A program may use at most 128 MiB of HBM per device.

v0:
```python
import functools
import math

import jax
import jax.numpy as jnp
from jax import lax
from jax.experimental import pallas as pl
from jax.experimental.pallas import tpu as pltpu
from jax.sharding import PartitionSpec as P

HEAD_DIM = 64
EPS = 1e-05
BF16 = jnp.bfloat16
F32 = jnp.float32
MIB = 1024 * 1024
EMPTY = 1e30


def dot(left, right):
    return lax.dot_general(left, right, (((1,), (0,)), ((), ())), preferred_element_type=F32)


def dot_nt(left, right):
    return lax.dot_general(left, right, (((1,), (1,)), ((), ())), preferred_element_type=F32)


def dot_tn(left, right):
    return lax.dot_general(left, right, (((0,), (0,)), ((), ())), preferred_element_type=F32)


def normalise(rows):
    mean = jnp.mean(rows, axis=1, keepdims=True)
    centred = rows - mean
    inverse = lax.rsqrt(jnp.mean(centred * centred, axis=1, keepdims=True) + EPS)
    return centred * inverse, inverse


def norm_back(upstream, normed, inverse, gain):
    scaled = upstream * gain
    first = jnp.mean(scaled, axis=1, keepdims=True)
    second = jnp.mean(scaled * normed, axis=1, keepdims=True)
    return inverse * (scaled - first - normed * second)


def pack(out_ref, rows, slot_of, cap, fill):
    total, width = out_ref.shape[0], rows.shape[1]
    place = lax.broadcasted_iota(jnp.int32, (total, slot_of.shape[1]), 0)
    first = (place >> 3) * cap
    sub = lax.broadcasted_iota(jnp.int32, (total, 128), 0) & 7
    piece = width // 8

    def placed(target):
        hit = (slot_of == target).astype(F32)
        moved = dot(hit.astype(BF16), rows)
        if fill:
            moved = moved + (1.0 - jnp.sum(hit, axis=1, keepdims=True)) * EMPTY
        return moved

    whole = cap // 8
    for group in range(whole):
        moved = placed(first + (place & 7) + group * 8)
        out_ref[:, group * width : (group + 1) * width] = moved.astype(BF16)
    for left in range(cap % 8):
        moved = placed(first + whole * 8 + left)
        folded = moved[:, :piece]
        for s in range(1, 8):
            folded = jnp.where(sub == s, moved[:, s * piece : (s + 1) * piece], folded)
        start = whole * width + left * piece
        out_ref[:, start : start + piece] = folded.astype(BF16)


def unpack(packed_ref, slot_of, cap, width):
    total = packed_ref.shape[0]
    place = lax.broadcasted_iota(jnp.int32, (slot_of.shape[0], total), 1)
    first = (place >> 3) * cap
    piece = width // 8
    sub = lax.broadcasted_iota(jnp.int32, (total, piece), 0) & 7
    whole = cap // 8
    rows = None
    for group in range(whole):
        hit = (slot_of == first + (place & 7) + group * 8).astype(BF16)
        part = dot(hit, packed_ref[:, group * width : (group + 1) * width])
        rows = part if rows is None else rows + part
    for left in range(cap % 8):
        start = whole * width + left * piece
        folded = packed_ref[:, start : start + piece].astype(F32)
        spread = jnp.concatenate(
            [jnp.where(sub == s, folded, 0.0).astype(BF16) for s in range(8)], axis=1
        )
        hit = (slot_of == first + whole * 8 + left).astype(BF16)
        part = dot(hit, spread)
        rows = part if rows is None else rows + part
    return rows


def slots_down(count):
    return lax.broadcasted_iota(jnp.int32, (count, 1), 0)


def norm1_kernel(x_ref, gain_ref, bias_ref, out_ref, *, cap):
    normed, _ = normalise(x_ref[...].astype(F32))
    rows = (normed * gain_ref[...] + bias_ref[...]).astype(BF16)
    slot_of = lax.broadcasted_iota(jnp.int32, (1, rows.shape[0]), 1)
    pack(out_ref, rows, slot_of, cap, False)


def gather_kernel(packed_ref, dispatch_ref, out_ref, *, cap):
    out_ref[...] = unpack(packed_ref, dispatch_ref[...], cap, out_ref.shape[1]).astype(BF16)


def two_heads(rows):
    lane = lax.broadcasted_iota(jnp.int32, rows.shape, 1)
    clear = jnp.zeros_like(rows)
    return jnp.concatenate(
        [jnp.where(lane < HEAD_DIM, rows, clear), jnp.where(lane < HEAD_DIM, clear, rows)], axis=0
    )


def started(source, target, sem):
    copy = pltpu.make_async_copy(source, target, sem)
    copy.start()
    return copy


def segments(lengths_ref, places):
    seg = jnp.zeros(places.shape, jnp.int32)
    end = 0
    for index in range(lengths_ref.shape[1]):
        end = end + lengths_ref[0, index]
        seg = seg + (places >= end).astype(jnp.int32)
    return seg


def attend_kernel(
    where_ref,
    lengths_ref,
    own_ref,
    other_ref,
    w_qkv_far,
    w_out_far,
    own_far,
    input_far,
    qkv_far,
    context_far,
    logsum_far,
    kept_ref,
    sent_ref,
    w_qkv_ref,
    w_out_ref,
    input_ref,
    qkv_ref,
    context_ref,
    logsum_ref,
    sems,
    *,
    step,
    reach,
    scale,
):
    weights = [
        started(w_qkv_far.at[which], w_qkv_ref.at[which], sems.at[which]) for which in range(3)
    ]
    last_weight = started(w_out_far, w_out_ref, sems.at[3])
    leaving = [started(own_ref, own_far, sems.at[4])]
    half = own_ref.shape[0]
    span = 2 * half
    here = where_ref[0]
    own_start = pl.multiple_of(here * half, half)
    other_start = pl.multiple_of((1 - here) * half, half)
    input_ref[pl.ds(own_start, half), :] = own_ref[...]
    input_ref[pl.ds(other_start, half), :] = other_ref[...]
    leaving.append(started(input_ref, input_far, sems.at[5]))
    for which in range(3):
        weights[which].wait()
        qkv_ref[which] = dot(input_ref[...], w_qkv_ref[which]).astype(BF16)
    leaving.append(started(qkv_ref, qkv_far, sems.at[6]))
    heads = qkv_ref.shape[2] // HEAD_DIM
    for start in range(0, span, step):
        stop = start + step
        low = max(0, start - reach)
        shape = (step, stop - low)
        query_at = lax.broadcasted_iota(jnp.int32, shape, 0) + start
        key_at = lax.broadcasted_iota(jnp.int32, shape, 1) + low
        allowed = (segments(lengths_ref, query_at) == segments(lengths_ref, key_at)) & (
            key_at <= query_at
        )
        allowed = jnp.concatenate([allowed.astype(F32)] * heads, axis=0) > 0.5
        lane = lax.broadcasted_iota(jnp.int32, (step, 2 * HEAD_DIM), 1)
        pairs = [
            slice(at, at + 2 * HEAD_DIM) for at in range(0, heads * HEAD_DIM, 2 * HEAD_DIM)
        ]
        scores = jnp.concatenate(
            [
                dot_nt(two_heads(qkv_ref[0, start:stop, columns]), qkv_ref[1, low:stop, columns])
                for columns in pairs
            ],
            axis=0,
        )
        scores = jnp.where(allowed, scores * scale, -1e30)
        top = jnp.max(scores, axis=1, keepdims=True)
        expo = jnp.exp(scores - top)
        total = jnp.sum(expo, axis=1, keepdims=True)
        probs = (expo * (1.0 / total)).astype(BF16)
        logsum = top + jnp.log(total)
        logsums = jnp.zeros((step, 128), F32)
        logsum_lane = lax.broadcasted_iota(jnp.int32, (step, 128), 1)
        for head in range(heads):
            mine = logsum[head * step : (head + 1) * step]
            logsums = jnp.where(logsum_lane == head, mine, logsums)
        for at, columns in enumerate(pairs):
            both = dot(
                probs[2 * at * step : 2 * (at + 1) * step], qkv_ref[2, low:stop, columns]
            )
            context_ref[start:stop, columns] = jnp.where(
                lane < HEAD_DIM, both[:step], both[step:]
            ).astype(BF16)
        logsum_ref[:, start:stop] = logsums.T
    leaving.append(started(context_ref, context_far, sems.at[7]))
    leaving.append(started(logsum_ref, logsum_far, sems.at[8]))
    last_weight.wait()
    sent_ref[...] = dot(context_ref[pl.ds(other_start, half), :], w_out_ref[...]).astype(BF16)
    kept_ref[...] = dot(context_ref[pl.ds(own_start, half), :], w_out_ref[...])
    for copy in leaving:
        copy.wait()


def scatter_kernel(kept_ref, came_ref, dispatch_ref, out_ref, *, cap, fill):
    rows = (kept_ref[...] + came_ref[...].astype(F32)).astype(BF16)
    pack(out_ref, rows, dispatch_ref[...], cap, fill)


def norm2_kernel(
    packed_ref, x_ref, grad_ref, gain_ref, bias_ref, resid_ref, h2_ref, up_ref, valid_ref, *, cap
):
    count, width = x_ref.shape
    moved = unpack(packed_ref, slots_down(count), cap, width)
    valid = (moved[:, :1] < 0.5 * EMPTY).astype(F32)
    resid = x_ref[...].astype(F32) + jnp.where(moved < 0.5 * EMPTY, moved, 0.0)
    resid_ref[...] = resid
    normed, _ = normalise(resid)
    h2_ref[...] = (normed * gain_ref[...] + bias_ref[...]).astype(BF16)
    up_ref[...] = (grad_ref[...].astype(F32) * valid).astype(BF16)
    valid_ref[...] = jnp.broadcast_to(valid, valid_ref.shape)


def gelu_and_slope(pre):
    root = math.sqrt(2.0 / math.pi)
    square = pre * pre
    bent = jnp.tanh(pre * (root + (root * 0.044715) * square))
    half = 0.5 + 0.5 * bent
    slope = half + (0.5 * pre) * (1.0 - bent * bent) * (root + (3.0 * 0.044715 * root) * square)
    return pre * half, slope


def expert_kernel(
    h2_ref,
    h2_other_ref,
    up_ref,
    up_other_ref,
    w_up_ref,
    w_down_ref,
    hidden_ref,
    dpre_ref,
    dh2_kept_ref,
    dh2_sent_ref,
    branch_kept_ref,
    branch_sent_ref,
    rows_ref,
    grads_ref,
    dh2_ref,
    branch_ref,
):
    count = h2_ref.shape[0]

    @pl.when(pl.program_id(0) == 0)
    def _():
        rows_ref[:count] = h2_ref[...]
        rows_ref[count:] = h2_other_ref[...]
        grads_ref[:count] = up_ref[...]
        grads_ref[count:] = up_other_ref[...]
        dh2_ref[...] = jnp.zeros_like(dh2_ref)
        branch_ref[...] = jnp.zeros_like(branch_ref)

    w_up, w_down = w_up_ref[...], w_down_ref[...]
    pre = dot(rows_ref[...], w_up)
    gelu, slope = gelu_and_slope(pre)
    hidden = gelu.astype(BF16)
    hidden_ref[...] = hidden
    dpre = (dot_nt(grads_ref[...], w_down) * slope).astype(BF16)
    dpre_ref[...] = dpre
    dh2_ref[...] += dot_nt(dpre, w_up)
    branch_ref[...] += dot(hidden, w_down)

    @pl.when(pl.program_id(0) == pl.num_programs(0) - 1)
    def _():
        dh2_kept_ref[...] = dh2_ref[:count]
        dh2_sent_ref[...] = dh2_ref[count:].astype(BF16)
        branch_kept_ref[...] = branch_ref[:count].astype(BF16)
        branch_sent_ref[...] = branch_ref[count:].astype(BF16)


def store_sums(sums_ref, upstream, normed):
    for which, total in enumerate((upstream * normed, upstream)):
        total = jnp.sum(total, axis=0, keepdims=True)
        pieces = total.shape[1] // 128
        for at in range(pieces):
            row = which * pieces + at
            sums_ref[row : row + 1] = total[:, at * 128 : (at + 1) * 128]


def norm2_back_kernel(
    kept_ref, came_ref, resid_ref, grad_ref, gain_ref, dresid_ref, packed_ref, sums_ref, *, cap
):
    dh2 = kept_ref[...] + came_ref[...].astype(F32)
    normed, inverse = normalise(resid_ref[...])
    dresid = grad_ref[...].astype(F32) + norm_back(dh2, normed, inverse, gain_ref[...])
    dresid_ref[...] = dresid
    slot_of = lax.broadcasted_iota(jnp.int32, (1, dh2.shape[0]), 1)
    pack(packed_ref, dresid.astype(BF16), slot_of, cap, False)
    store_sums(sums_ref, dh2, normed)


def out_grad_kernel(where_ref, own_ref, other_ref, context_far, dattn_ref, *rest):
    piece_fars, (context_ref, grad_ref, piece_ref, sems) = rest[:4], rest[4:]
    arriving = started(context_far, context_ref, sems.at[4])
    half = own_ref.shape[0]
    here = where_ref[0]
    dattn_ref[pl.ds(pl.multiple_of(here * half, half), half), :] = own_ref[...]
    dattn_ref[pl.ds(pl.multiple_of((1 - here) * half, half), half), :] = other_ref[...]
    arriving.wait()
    grad_ref[...] = dot_tn(context_ref[...], dattn_ref[...])
    width = grad_ref.shape[1]
    quarter = grad_ref.shape[0] // 4
    owners = piece_ref.shape[1]
    rows = quarter // owners
    leaving = []
    for step in (1, 2, 3, 0):
        first = (where_ref[1] ^ step) * quarter
        for owner in range(owners):
            start = pl.multiple_of(first + owner * rows, rows)
            block = grad_ref[pl.ds(start, rows), :]
            piece_ref[step, owner] = jnp.concatenate(
                [block[:, at : at + 128] for at in range(0, width, 128)], axis=0
            ).astype(BF16)
        leaving.append(started(piece_ref.at[step], piece_fars[step], sems.at[step]))
    for copy in leaving:
        copy.wait()


def attend_back_kernel(
    where_ref,
    lengths_ref,
    dattn_ref,
    qkv_far,
    context_far,
    logsum_far,
    w_qkv_far,
    w_out_far,
    kept_ref,
    sent_ref,
    *rest,
    step,
    reach,
    scale,
):
    dvalue_fars, dkq_fars = rest[:4], rest[4:8]
    dcontext_ref, inner_ref, dquery_ref, dqkv_ref = rest[8:12]
    qkv_ref, context_ref, logsum_ref, w_qkv_ref, w_out_ref, sems = rest[12:]
    arriving = [
        started(source, target, sems.at[at])
        for at, (source, target) in enumerate(
            (
                (w_out_far, w_out_ref),
                (context_far, context_ref),
                (qkv_far, qkv_ref),
                (logsum_far, logsum_ref),
                (w_qkv_far, w_qkv_ref),
            )
        )
    ]
    half = kept_ref.shape[0]
    span = 2 * half
    here = where_ref[0]
    own_start = pl.multiple_of(here * half, half)
    other_start = pl.multiple_of((1 - here) * half, half)
    arriving[0].wait()
    dcontext = dot_nt(dattn_ref[...], w_out_ref[...]).astype(BF16)
    dcontext_ref[...] = dcontext
    arriving[1].wait()
    arriving[2].wait()
    arriving[3].wait()
    heads = qkv_ref.shape[2] // HEAD_DIM
    columns_all = qkv_ref.shape[2]
    product = dcontext.astype(F32) * context_ref[...].astype(F32)
    coarse = product.astype(BF16)
    fine = (product - coarse.astype(F32)).astype(BF16)
    of_head = (
        lax.broadcasted_iota(jnp.int32, (16, columns_all), 1) // HEAD_DIM
        == lax.broadcasted_iota(jnp.int32, (16, columns_all), 0)
    ).astype(BF16)
    inner_ref[...] = dot_nt(of_head, coarse) + dot_nt(of_head, fine)
    dquery_ref[...] = jnp.zeros_like(dquery_ref)
    for start in range(0, span, step):
        stop = start + step
        high = min(span, stop + reach)
        shape = (step, high - start)
        key_at = lax.broadcasted_iota(jnp.int32, shape, 0) + start
        query_at = lax.broadcasted_iota(jnp.int32, shape, 1) + start
        allowed = (segments(lengths_ref, query_at) == segments(lengths_ref, key_at)) & (
            key_at <= query_at
        )
        allowed = jnp.concatenate([allowed.astype(F32)] * heads, axis=0) > 0.5
        lane = lax.broadcasted_iota(jnp.int32, (step, 2 * HEAD_DIM), 1)
        pairs = [
            slice(at, at + 2 * HEAD_DIM) for at in range(0, heads * HEAD_DIM, 2 * HEAD_DIM)
        ]
        keys = [two_heads(qkv_ref[1, start:stop, columns]) for columns in pairs]

        def by_head(ref, start=start, high=high):
            return jnp.concatenate(
                [
                    jnp.broadcast_to(ref[head : head + 1, start:high], (step, high - start))
                    for head in range(heads)
                ],
                axis=0,
            )

        scores = jnp.concatenate(
            [
                dot_nt(keys[at], qkv_ref[0, start:high, columns])
                for at, columns in enumerate(pairs)
            ],
            axis=0,
        )
        probs = jnp.exp(jnp.where(allowed, scores * scale - by_head(logsum_ref), -1e30))
        dprobs = jnp.concatenate(
            [
                dot_nt(two_heads(qkv_ref[2, start:stop, columns]), dcontext_ref[start:high, columns])
                for columns in pairs
            ],
            axis=0,
        )
        dscores = (probs * (dprobs - by_head(inner_ref))).astype(BF16)
        probs = probs.astype(BF16)
        for at, columns in enumerate(pairs):
            mine = slice(2 * at * step, 2 * (at + 1) * step)
            dvalues = dot(probs[mine], dcontext_ref[start:high, columns])
            dkeys = dot(dscores[mine], qkv_ref[0, start:high, columns])
            dquery_ref[start:high, columns] += dot_tn(dscores[mine], keys[at])
            dqkv_ref[1, start:stop, columns] = (
                jnp.where(lane < HEAD_DIM, dkeys[:step], dkeys[step:]) * scale
            ).astype(BF16)
            dqkv_ref[2, start:stop, columns] = jnp.where(
                lane < HEAD_DIM, dvalues[:step], dvalues[step:]
            ).astype(BF16)
    dqkv_ref[0] = (dquery_ref[...] * scale).astype(BF16)

    quarter = columns_all // 4
    leaving = []
    for kind, at in ((2, 1), (2, 2), (2, 3), (1, 1), (0, 1), (1, 2), (0, 2), (1, 3), (0, 3), (2, 0), (1, 0), (0, 0)):
        first = pl.multiple_of((where_ref[1] ^ at) * quarter, quarter)
        target = dvalue_fars[at] if kind == 2 else dkq_fars[at].at[1 - kind]
        leaving.append(
            started(dqkv_ref.at[kind, :, pl.ds(first, quarter)], target, sems.at[5 + kind * 4 + at])
        )
    arriving[4].wait()

    def back_rows(start):
        total = dot_nt(dqkv_ref[0, pl.ds(start, half), :], w_qkv_ref[0])
        total = total + dot_nt(dqkv_ref[1, pl.ds(start, half), :], w_qkv_ref[1])
        return total + dot_nt(dqkv_ref[2, pl.ds(start, half), :], w_qkv_ref[2])

    sent_ref[...] = back_rows(other_start).astype(BF16)
    kept_ref[...] = back_rows(own_start)
    for copy in leaving:
        copy.wait()


def token_grad(where_ref, grad_refs, index, input_ref, own_refs, other_refs):
    half = own_refs[0].shape[0]
    own_start = pl.multiple_of(where_ref[0] * half, half)
    other_start = pl.multiple_of((1 - where_ref[0]) * half, half)

    def rows(ref, start, count):
        return ref[pl.ds(start, count), :] if index is None else ref[index, pl.ds(start, count), :]

    total = dot_tn(rows(grad_refs[0], 0, 2 * half), input_ref[...])
    for grad_ref, own_ref, other_ref in zip(grad_refs[1:], own_refs, other_refs):
        total = total + dot_tn(rows(grad_ref, own_start, half), own_ref[...])
        total = total + dot_tn(rows(grad_ref, other_start, half), other_ref[...])
    return total.T


def store_halves(where_ref, bit, half_refs, load, at):
    rows = at.stop - at.start
    for side, half_ref in enumerate(half_refs):
        mine = ((where_ref[2] >> bit) & 1) ^ side
        for index in range(half_ref.shape[0]):
            half_ref[index, at] = load(2 * index + mine, rows).astype(BF16)


def value_grad_kernel(where_ref, *refs):
    grad_refs, input_ref, own_refs, other_refs = refs[0:4], refs[4], refs[5:8], refs[8:11]
    out_refs, half_refs, total_ref = refs[11:15], refs[15:17], refs[17]
    total_ref[...] = token_grad(where_ref, grad_refs, None, input_ref, own_refs, other_refs)
    rows = half_refs[0].shape[1] // 2
    store_halves(
        where_ref, 0, half_refs,
        lambda owner, rows: sum(ref[owner].astype(F32) for ref in out_refs), slice(0, rows),
    )
    store_halves(
        where_ref, 0, half_refs,
        lambda owner, rows: total_ref[pl.ds(pl.multiple_of(owner * rows, rows), rows), :],
        slice(rows, 2 * rows),
    )


def key_query_grad_kernel(where_ref, *refs):
    grad_refs, input_ref, own_refs, other_refs = refs[0:4], refs[4], refs[5:8], refs[8:11]
    half_refs, total_ref = refs[11:13], refs[13]
    rows = half_refs[0].shape[1] // 2
    for index in range(2):
        total_ref[...] = token_grad(where_ref, grad_refs, index, input_ref, own_refs, other_refs)
        store_halves(
            where_ref, 0, half_refs,
            lambda owner, rows: total_ref[pl.ds(pl.multiple_of(owner * rows, rows), rows), :],
            slice(index * rows, (index + 1) * rows),
        )


def add_kernel(where_ref, kept_ref, came_ref, *half_refs, bit):
    store_halves(
        where_ref, bit, half_refs,
        lambda owner, rows: kept_ref[owner].astype(F32) + came_ref[owner].astype(F32),
        slice(0, kept_ref.shape[1]),
    )


def last_add_kernel(kept_ref, came_ref, out_ref):
    out_ref[...] = (kept_ref[0].astype(F32) + came_ref[0].astype(F32)).astype(BF16)


def split_store(out_ref, start, value):
    rows = value.shape[0]
    coarse = value.astype(BF16)
    out_ref[start : start + rows] = coarse
    out_ref[start + rows : start + 2 * rows] = (value - coarse.astype(F32)).astype(BF16)


def last_add_sums_kernel(kept_ref, came_ref, *refs):
    out_ref = refs[4]
    rows = kept_ref.shape[1]
    out_ref[:rows] = (kept_ref[0].astype(F32) + came_ref[0].astype(F32)).astype(BF16)
    sums = jnp.concatenate([refs[0][...] + refs[1][...], refs[2][...] + refs[3][...]], axis=0)
    split_store(out_ref, rows, sums)


def split_sum(refs, start, stop):
    rows = (stop - start) // 2
    return sum(
        ref[start : start + rows].astype(F32) + ref[start + rows : stop].astype(F32)
        for ref in refs
    )


def stack_kernel(own_ref, came_ref, out_ref, *, sums):
    rows = own_ref.shape[0] - sums
    out_ref[:rows] = own_ref[:rows]
    out_ref[rows : 2 * rows] = came_ref[:rows]
    if sums:
        split_store(out_ref, 2 * rows, split_sum((own_ref, came_ref), rows, rows + sums))


def place_rows(where_ref, digits, at):
    bits = 2 * (digits - 1)
    return where_ref[2] ^ sum(((at >> bit) & 1) << (bits - 1 - bit) for bit in range(bits))


def each_piece(where_ref, refs, digits, rows, use):
    owners = 4 ** (digits - 1)
    for step in range(4):
        column = where_ref[1] ^ step
        for at in range(owners):
            owner = place_rows(where_ref, digits, at)
            first = at * 2 * rows

            def load(low, high, first=first, step=step):
                if step < 3:
                    return refs[step][first + low : first + high]
                middle = refs[3].shape[0]
                start, stop = first + low, first + high
                if stop <= middle:
                    return refs[3][start:stop]
                if start >= middle:
                    return refs[4][start - middle : stop - middle]
                return jnp.concatenate([refs[3][start:middle], refs[4][: stop - middle]], axis=0)

            use(column, owner, load)


def finish_out_value_kernel(where_ref, *refs, digits):
    qkv_ref, out_ref = refs[5:]
    width = qkv_ref.shape[1]
    rows = width // 4 ** (digits - 1)
    few = rows * 128 // width

    def use(column, owner, load):
        start = pl.multiple_of(column * 128 + owner * few, few)
        out_ref[pl.ds(start, few), :] = jnp.concatenate(
            [load(at, at + few).astype(F32) for at in range(0, rows, few)], axis=1
        )
        lanes = pl.ds(pl.multiple_of(column * 128, 128), 128)
        qkv_ref[0, pl.ds(pl.multiple_of(owner * rows, rows), rows), lanes] = load(
            rows, 2 * rows
        ).astype(F32)

    each_piece(where_ref, refs[:5], digits, rows, use)


def finish_key_query_kernel(where_ref, *refs, digits, sums):
    qkv_ref, sums_ref = refs[6:]
    width = qkv_ref.shape[1]
    rows = width // 4 ** (digits - 1)

    def use(column, owner, load):
        lanes = pl.ds(pl.multiple_of(column * 128, 128), 128)
        down = pl.ds(pl.multiple_of(owner * rows, rows), rows)
        qkv_ref[1, down, lanes] = load(0, rows).astype(F32)
        qkv_ref[0, down, lanes] = load(rows, 2 * rows).astype(F32)

    each_piece(where_ref, refs[:5], digits, rows, use)
    total = refs[0].shape[0]
    half = refs[4].shape[0]
    sums_ref[...] = split_sum(refs[:3], total - sums, total) + split_sum(
        refs[4:5], half - sums, half
    )


def expert_grad_kernel(rows_ref, grads_ref, hidden_ref, dpre_ref, up_ref, down_ref, turned_ref):
    @pl.when(pl.program_id(0) == 0)
    def _():
        turned_ref[...] = rows_ref[...].T

    up_ref[...] = dot(turned_ref[...], dpre_ref[...])
    down_ref[...] = dot_tn(hidden_ref[...], grads_ref[...])


def norm1_back_kernel(packed_ref, x_ref, dresid_ref, gain_ref, out_ref, sums_ref, *, cap):
    count, width = x_ref.shape
    dh1 = unpack(packed_ref, slots_down(count), cap, width)
    normed, inverse = normalise(x_ref[...].astype(F32))
    out_ref[...] = dresid_ref[...] + norm_back(dh1, normed, inverse, gain_ref[...])
    store_sums(sums_ref, dh1, normed)


VMEM = pl.BlockSpec(memory_space=pltpu.VMEM)
SMEM = pl.BlockSpec(memory_space=pltpu.SMEM)


def after(value, *others):
    return lax.optimization_barrier((value, *others))[0]


def far(value):
    return pltpu.with_memory_space_constraint(value, pltpu.HBM)


def call(kernel, name, outs, args, flops, scalars=0, scratch=(), limit=16, away=(), out_away=(), raw=(), out_raw=()):
    shapes = [
        pltpu.HBM(shape, kind)
        if at in out_away or at in out_raw
        else jax.ShapeDtypeStruct(shape, kind)
        for at, (shape, kind) in enumerate(outs)
    ]

    def spec(at, away, raw):
        if at in raw:
            return pl.BlockSpec(memory_space=pltpu.HBM)
        return pl.BlockSpec() if at in away else VMEM

    size = sum(math.prod(a.shape) * a.dtype.itemsize for a in (*args, *shapes))
    return pl.pallas_call(
        kernel,
        name=name,
        out_shape=shapes,
        in_specs=[
            SMEM if at < scalars else spec(at, away, raw) for at in range(len(args))
        ],
        out_specs=[spec(at, out_away, out_raw) for at in range(len(outs))],
        scratch_shapes=list(scratch),
        cost_estimate=pl.CostEstimate(flops=flops, bytes_accessed=size, transcendentals=0),
        compiler_params=pltpu.CompilerParams(vmem_limit_bytes=limit * MIB),
    )(*[far(value) if at in away or at in raw else value for at, value in enumerate(args)])


def expert(h2, h2_other, upstream, upstream_other, w_up, w_down):
    count, width = h2.shape
    units = w_up.shape[1]
    tile = min(512, units)
    shapes = [
        ((2 * count, units), BF16),
        ((2 * count, units), BF16),
        ((count, width), F32),
        ((count, width), BF16),
        ((count, width), BF16),
        ((count, width), BF16),
        ((2 * count, width), BF16),
        ((2 * count, width), BF16),
    ]
    stay = (2, 3)
    both = pl.BlockSpec((2 * count, width), lambda j: (0, 0))
    rows = pl.BlockSpec((count, width), lambda j: (0, 0))
    by_unit = pl.BlockSpec((2 * count, tile), lambda j: (0, j))
    return pl.pallas_call(
        expert_kernel,
        name="expert",
        grid=(units // tile,),
        out_shape=[
            jax.ShapeDtypeStruct(shape, kind) if at in stay else pltpu.HBM(shape, kind)
            for at, (shape, kind) in enumerate(shapes)
        ],
        in_specs=[rows] * 4
        + [
            pl.BlockSpec((width, tile), lambda j: (0, j)),
            pl.BlockSpec((tile, width), lambda j: (j, 0)),
        ],
        out_specs=[by_unit, by_unit, rows, rows, rows, rows, both, both],
        scratch_shapes=[
            pltpu.VMEM((2 * count, width), F32),
            pltpu.VMEM((2 * count, width), F32),
        ],
        cost_estimate=pl.CostEstimate(
            flops=16 * count * width * units, bytes_accessed=16 * MIB, transcendentals=0
        ),
        compiler_params=pltpu.CompilerParams(vmem_limit_bytes=40 * MIB),
    )(h2, h2_other, upstream, upstream_other, far(w_up), far(w_down))


def expert_grads(rows, grads, hidden, dpre):
    count, width = rows.shape
    units = hidden.shape[1]
    tile = min(512, units)
    whole = pl.BlockSpec((count, width), lambda j: (0, 0))
    by_unit = pl.BlockSpec((count, tile), lambda j: (0, j))
    return pl.pallas_call(
        expert_grad_kernel,
        name="expert_grads",
        grid=(units // tile,),
        out_shape=[pltpu.HBM((width, units), F32), pltpu.HBM((units, width), F32)],
        in_specs=[whole] * 2 + [by_unit] * 2,
        out_specs=[
            pl.BlockSpec((width, tile), lambda j: (0, j)),
            pl.BlockSpec((tile, width), lambda j: (j, 0)),
        ],
        scratch_shapes=[pltpu.VMEM((width, count), BF16)],
        cost_estimate=pl.CostEstimate(
            flops=4 * count * width * units, bytes_accessed=24 * MIB, transcendentals=0
        ),
        compiler_params=pltpu.CompilerParams(vmem_limit_bytes=40 * MIB),
    )(far(rows), far(grads), far(hidden), far(dpre))


def flip(value, axis, bit):
    size = lax.axis_size(axis)
    return lax.ppermute(value, axis, [(i, i ^ bit) for i in range(size)])


def to_others(values, digit):
    return [
        flip(values[m] if isinstance(values, (list, tuple)) else values, "exp", m << (2 * digit))
        for m in range(1, 4)
    ]


def after_all(values, *others):
    return list(lax.optimization_barrier((*values, *others))[: len(values)])


def sum_and_spread(first, second, where, digits, sums, extra, finish):
    bits = 2 * (digits - 1)

    def across(value, bit):
        return flip(value, "exp", 4 << bit)

    def add(halves, came, bit, sums=None):
        owners, rows, columns = came.shape
        if bit + 1 < bits:
            return call(
                functools.partial(add_kernel, bit=bit + 1), "add",
                [((owners // 2, rows, columns), BF16)] * 2, [where, halves[0], came], 0, scalars=1,
                away=(1,), out_away=(0,),
            )
        if sums is None:
            return call(
                last_add_kernel, "last_add", [((rows, columns), BF16)], [halves[0], came], 0,
                away=(0,),
            )
        return call(
            last_add_sums_kernel, "last_add_sums", [((rows + extra, columns), BF16)],
            [halves[0], came, *sums], 0, away=(0,),
        )

    def stack(own, came, sums):
        rows, columns = own.shape
        return call(
            functools.partial(stack_kernel, sums=sums), "stack",
            [((2 * rows - sums, columns), BF16)], [own, came], 0,
        )[0]

    def steps(halves, sums, extra):
        for bit in range(bits):
            came = yield halves[1], [across(halves[1], bit)]
            halves = add(halves, came[0], bit, sums)
        total = halves[0]
        for bit in reversed(range(bits)):
            came = yield total, [across(total, bit)]
            total = stack(total, came[0], extra)
        by_x, by_y = yield total, [flip(total, "exp", 1), flip(total, "exp", 2)]
        middle = total.shape[0] // 2
        sent = [by_y[:middle], by_x[middle:]]
        halves = yield sent[0], [flip(sent[0], "exp", 1), flip(sent[1], "exp", 2)]
        yield None, [total, by_x, by_y, *halves]

    lines, states, last = [steps(first, None, 0), None], [None, None], None
    states[0] = next(lines[0])
    for at, line in enumerate([0] + [0, 1] * (2 * bits + 1) + [1]):
        if at == 1:
            pieces = second(last)
            lines[1], last = steps(pieces, sums, extra), pieces[1]
            states[1] = next(lines[1])
        came = states[line][1]
        states[line] = lines[line].send(came if last is None else after_all(came, last))
        last = states[line][0]
        if line == 0 and last is None:
            finished = finish(states[0][1])
            last = finished[1]
    return finished, states[1][1]


def on_device(
    block_input,
    dispatch,
    lengths,
    ln1_gain,
    ln1_bias,
    ln2_gain,
    ln2_bias,
    w_qkv,
    w_out,
    w_up,
    w_down,
    grad_output,
):
    slots, width = block_input.shape
    seq_rows = dispatch.shape[0]
    n_exp = lax.axis_size("exp")
    devices = n_exp * lax.axis_size("head")
    cap = slots // devices
    span = 2 * seq_rows
    columns = w_qkv.shape[2]
    scale = 1.0 / math.sqrt(HEAD_DIM)
    digits = (n_exp.bit_length() - 1) // 2
    place = lax.axis_index("exp")
    where = jnp.stack(
        [lax.axis_index("head"), place & 3, place >> 2]
    ).astype(jnp.int32)
    step = 128
    reach = 3 * seq_rows // 4
    packed = ((devices * 8, cap * 128), BF16)
    moving = 2 * devices * 8 * max(slots, seq_rows) * width * 3
    gain1, bias1 = ln1_gain.reshape(1, width), ln1_bias.reshape(1, width)
    gain2, bias2 = ln2_gain.reshape(1, width), ln2_bias.reshape(1, width)
    down, along = dispatch.reshape(seq_rows, 1), dispatch.reshape(1, seq_rows)

    def exchange(value):
        value = value.reshape(devices, 8, cap * 128)
        value = lax.all_to_all(value, ("exp", "head"), split_axis=0, concat_axis=0, tiled=True)
        return value.reshape(devices * 8, cap * 128)

    def cross(value):
        return flip(value, "head", 1)

    (h1,) = call(
        functools.partial(norm1_kernel, cap=cap), "norm1", [packed],
        [block_input, gain1, bias1], moving, away=(0, 1, 2),
    )
    arrived = exchange(h1)
    (own,) = call(
        functools.partial(gather_kernel, cap=cap), "gather1", [((seq_rows, width), BF16)],
        [arrived, down], moving,
    )
    other = cross(own)
    own_copy, inputs, qkv, context, logsum, attn_kept, attn_sent = call(
        functools.partial(attend_kernel, step=step, reach=reach, scale=scale),
        "attend",
        [
            ((seq_rows, width), BF16),
            ((span, width), BF16),
            ((3, span, columns), BF16),
            ((span, columns), BF16),
            ((128, span), F32),
            ((seq_rows, width), F32),
            ((seq_rows, width), BF16),
        ],
        [where, lengths, own, other, w_qkv, w_out],
        2 * span * width * columns * 4 + 16 * span * span * columns,
        scalars=2,
        limit=24,
        raw=(4, 5),
        out_raw=range(5),
        scratch=[
            pltpu.VMEM((3, width, columns), BF16),
            pltpu.VMEM((columns, width), BF16),
            pltpu.VMEM((span, width), BF16),
            pltpu.VMEM((3, span, columns), BF16),
            pltpu.VMEM((span, columns), BF16),
            pltpu.VMEM((128, span), F32),
            pltpu.SemaphoreType.DMA((9,)),
        ],
    )
    (sent,) = call(
        functools.partial(scatter_kernel, cap=cap, fill=True), "scatter1", [packed],
        [attn_kept, cross(attn_sent), along], moving,
    )
    attn_back = exchange(sent)
    near_own = after(own_copy, sent)
    by_x, by_y = flip(near_own, "exp", 1), flip(near_own, "exp", 2)
    by_xy = flip(after(own_copy, attn_back), "exp", 3)
    attn_back = after(attn_back, by_x, by_y)
    resid, h2, upstream, valid = call(
        functools.partial(norm2_kernel, cap=cap),
        "norm2",
        [((slots, width), F32), ((slots, width), BF16), ((slots, width), BF16), ((slots, 128), F32)],
        [attn_back, block_input, grad_output, gain2, bias2],
        moving,
    )
    h2_other, upstream_other = cross(h2), cross(upstream)
    hidden, dpre, dh2_kept, dh2_sent, branch_kept, branch_sent, rows_all, grads_all = expert(
        h2, h2_other, upstream, upstream_other, w_up[0], w_down[0]
    )
    dh2_sent = after(dh2_sent, by_xy)
    dresid, sent, sums2 = call(
        functools.partial(norm2_back_kernel, cap=cap),
        "norm2_back",
        [((slots, width), F32), packed, ((width // 64, 128), F32)],
        [dh2_kept, cross(dh2_sent), resid, grad_output, gain2],
        moving,
    )
    arrived = exchange(sent)
    plane_own = [after(rows, sent) for rows in (by_x, by_y, by_xy)]
    plane_other = [cross(rows) for rows in plane_own]
    hidden = after(hidden, sent)
    grad_up, grad_down = expert_grads(rows_all, grads_all, hidden, dpre)
    arrived, grad_up, grad_down, *plane_other = lax.optimization_barrier(
        (arrived, grad_up, grad_down, *plane_other)
    )
    branch = branch_kept.astype(F32) + cross(branch_sent).astype(F32)
    result = (resid + valid[:, :1] * branch).astype(BF16)
    (own,) = call(
        functools.partial(gather_kernel, cap=cap), "gather2", [((seq_rows, width), BF16)],
        [arrived, down], moving,
    )
    other = cross(own)
    piece = 4 * width // n_exp
    dattn, *out_pieces = call(
        out_grad_kernel,
        "out_grad",
        [((span, width), BF16), *[((n_exp // 4, piece, 128), BF16)] * 4],
        [where, own, other, context],
        2 * span * width * columns,
        scalars=1,
        scratch=[
            pltpu.VMEM((span, columns), BF16),
            pltpu.VMEM((columns, width), F32),
            pltpu.VMEM((4, n_exp // 4, piece, 128), BF16),
            pltpu.SemaphoreType.DMA((5,)),
        ],
        raw=(3,),
        out_raw=range(1, 5),
    )
    out_parts = [out_pieces[0], *to_others(out_pieces, 0)]
    du_kept, du_sent, *parts = call(
        functools.partial(attend_back_kernel, step=step, reach=reach, scale=scale),
        "attend_back",
        [
            ((seq_rows, width), F32),
            ((seq_rows, width), BF16),
            *[((span, 128), BF16)] * 4,
            *[((2, span, 128), BF16)] * 4,
        ],
        [where, lengths, dattn, qkv, context, logsum, w_qkv, w_out],
        2 * span * width * columns * 4 + 40 * span * span * columns,
        scalars=2,
        limit=24,
        raw=range(3, 8),
        out_raw=range(2, 10),
        scratch=[
            pltpu.VMEM((span, columns), BF16),
            pltpu.VMEM((16, span), F32),
            pltpu.VMEM((span, columns), F32),
            pltpu.VMEM((3, span, columns), BF16),
            pltpu.VMEM((3, span, columns), BF16),
            pltpu.VMEM((span, columns), BF16),
            pltpu.VMEM((128, span), F32),
            pltpu.VMEM((3, width, columns), BF16),
            pltpu.VMEM((columns, width), BF16),
            pltpu.SemaphoreType.DMA((17,)),
        ],
    )
    du_sent, *parts = after_all([du_sent, *parts], *out_parts[1:])
    value_parts = [parts[0], *to_others(parts[:4], 0)]
    key_query_parts = [parts[4], *to_others(after_all(parts[4:], *value_parts[1:]), 0)]
    (sent,) = call(
        functools.partial(scatter_kernel, cap=cap, fill=False), "scatter2", [packed],
        [du_kept, cross(du_sent), along], moving,
    )
    arrived = exchange(after(sent, *value_parts[1:]))
    input_grad, sums1 = call(
        functools.partial(norm1_back_kernel, cap=cap),
        "norm1_back",
        [((slots, width), F32), ((width // 64, 128), F32)],
        [arrived, block_input, dresid, gain1],
        moving,
        away=(1, 2, 3),
        out_away=(0,),
    )
    tokens = [inputs, *plane_own, *plane_other]
    split = [((n_exp // 8, 2 * piece, 128), BF16)] * 2
    product = 8 * span * width * 128
    out_value = call(
        value_grad_kernel, "value_grad", split, [where, *value_parts, *tokens, *out_parts],
        product, scalars=1, scratch=[pltpu.VMEM((width, 128), F32)], away=(1, *range(5, 13)),
        out_away=(0,),
    )

    def key_query(last):
        came = after_all(key_query_parts[1:], last)
        return call(
            key_query_grad_kernel, "key_query_grad", split,
            [where, key_query_parts[0], *came, *tokens], 2 * product, scalars=1,
            scratch=[pltpu.VMEM((width, 128), F32)], away=(1, *range(5, 12)), out_away=(0,),
        )

    sums = [sums1, cross(sums1), sums2, cross(sums2)]
    extra = 4 * sums1.shape[0]
    whole_qkv = pltpu.HBM((3, width, columns), F32)
    finish = pl.pallas_call(
        functools.partial(finish_out_value_kernel, digits=digits),
        name="finish_out_value",
        grid=(1,),
        out_shape=[whole_qkv, pltpu.HBM((columns, width), F32)],
        in_specs=[SMEM] + [VMEM] * 5,
        out_specs=[
            pl.BlockSpec((1, width, columns), lambda i: (2, 0, 0)),
            pl.BlockSpec((columns, width), lambda i: (0, 0)),
        ],
        cost_estimate=pl.CostEstimate(flops=0, bytes_accessed=6 * MIB, transcendentals=0),
        compiler_params=pltpu.CompilerParams(vmem_limit_bytes=40 * MIB),
    )
    (grad_qkv, grad_out), key_query = sum_and_spread(
        out_value, key_query, where, digits, sums, extra, lambda parts: finish(where, *parts)
    )
    grad_qkv, sums = pl.pallas_call(
        functools.partial(finish_key_query_kernel, digits=digits, sums=extra),
        name="finish_key_query",
        grid=(1,),
        out_shape=[whole_qkv, jax.ShapeDtypeStruct((extra // 2, 128), F32)],
        in_specs=[SMEM] + [VMEM] * 5 + [pl.BlockSpec(memory_space=pltpu.HBM)],
        out_specs=[
            pl.BlockSpec((2, width, columns), lambda i: (0, 0, 0)),
            pl.BlockSpec((extra // 2, 128), lambda i: (0, 0)),
        ],
        input_output_aliases={6: 0},
        cost_estimate=pl.CostEstimate(flops=0, bytes_accessed=6 * MIB, transcendentals=0),
        compiler_params=pltpu.CompilerParams(vmem_limit_bytes=40 * MIB),
    )(where, *key_query, grad_qkv)
    sums = sums.reshape(4, width)
    return (
        result,
        input_grad,
        sums[0],
        sums[1],
        sums[2],
        sums[3],
        grad_qkv,
        grad_out,
        grad_up[None],
        grad_down[None],
    )


def solution(mesh):
    placed = (
        P(("exp", "head"), None),
        P(("exp", "head")),
        P("exp", None),
        P(),
        P(),
        P(),
        P(),
        P(None, None, "head"),
        P("head", None),
        P("exp", None, "head"),
        P("exp", "head", None),
        P(("exp", "head"), None),
    )
    return jax.shard_map(
        on_device,
        mesh=mesh,
        in_specs=placed,
        out_specs=(
            P(("exp", "head"), None),
            P(("exp", "head"), None),
            P(),
            P(),
            P(),
            P(),
            P(None, None, "head"),
            P("head", None),
            P("exp", None, "head"),
            P("exp", "head", None),
        ),
        check_vma=False,
    )
```

profile of v0, /device:TPU:0, one launch (start us, length us, event | category | flops | bytes accessed | tf_op | source)
XLA Modules:
  0.0 252.1 jit_solution(15806884930818947194)
XLA Ops:
  0.7 3.3 %norm1.1 = bf16[256,1280]{1,0:T(8,128)(2,1)} custom-call(bf16[320,1024]{1,0:T(8,128)(2,1)} %x_ref.5, f32[1,1024]{1,0:T(1,128)} %bitcast.39, f32[1,1024]{1,0:T(1,128)} %bitcast.43), custom_call_target="tpu_custom_call" | custom-call | flops 503316480 | bytes 1318912 | tf_op jit(solution)/shard_map/norm1/pallas_call | solution.py:682
  4.0 7.3 %all-to-all-start = ((bf16[32,8,1280]{2,1,0:T(8,128)(2,1)}), bf16[32,8,1280]{2,1,0:T(8,128)(2,1)S(1)}, u32[]{:S(2)}, u32[]{:S(2)}) async-start(bf16[32,8,1280]{2,1,0:T(8,128)(2,1)} %bitcast.5), calls=%async_computation | async-start | bytes 1310720 | tf_op jit(solution)/shard_map/all_to_all | solution.py:877
  11.5 17.7 %all-to-all-done = bf16[32,8,1280]{2,1,0:T(8,128)(2,1)S(1)} async-done(((bf16[32,8,1280]{2,1,0:T(8,128)(2,1)}), bf16[32,8,1280]{2,1,0:T(8,128)(2,1)S(1)}, u32[]{:S(2)}, u32[]{:S(2)}) %all-to-all-start) | async-done | bytes 655392 | tf_op jit(solution)/shard_map/all_to_all | solution.py:877
  30.1 1.8 collective-permute-done.other_ref
  31.8 8.1 %attend.1 = (bf16[256,1024]{1,0:T(8,128)(2,1)}, bf16[512,1024]{1,0:T(8,128)(2,1)}, bf16[3,512,512]{2,1,0:T(8,128)(2,1)}, bf16[512,512]{1,0:T(8,128)(2,1)}, f32[1...) custom-call(s32[3]{0:T(128)S(1)} %pad_add_fusion.where_ref, s32[1,5]{1,0:T(1,128)S(1)} %copy-done.8, ...), custom_call_target="tpu_custom_call" | custom-call | flops 4294967296 | bytes 10747936 | tf_op jit(solution)/shard_map/attend/pallas_call | solution.py:682
  40.1 1.8 collective-permute-done.1.came_ref
  41.9 1.5 scatter1.1
  43.4 3.7 %all-to-all-start.1 = ((bf16[32,8,1280]{2,1,0:T(8,128)(2,1)}), bf16[32,8,1280]{2,1,0:T(8,128)(2,1)S(1)}, u32[]{:S(2)}, u32[]{:S(2)}) async-start(bf16[32,8,1280]{2,1,0:T(8,128)(2,1)} %bitcast.9), calls=%async_computation.1 | async-start | bytes 1310720 | tf_op jit(solution)/shard_map/all_to_all | solution.py:877
  47.1 1.7 collective-permute-start.3
  48.8 1.5 collective-permute-start.2
  50.3 17.8 %collective-permute-done.3.refs_6_ = bf16[256,1024]{1,0:T(8,128)(2,1)S(1)} collective-permute-done((bf16[256,1024]{1,0:T(8,128)(2,1)S(1)}, bf16[256,1024]{1,0:T(8,128)(2,1)S(1)}, u32[]{:S(2)}, u32[]{:S(2)}) %collective-permute-start.3) | collective-permute-done | bytes 524320 | tf_op jit(solution)/shard_map/ppermute | solution.py:765
  68.9 1.2 norm2.1
  70.7 1.3 collective-permute-start.7
  73.2 16.6 %expert.1 = (bf16[640,2048]{1,0:T(8,128)(2,1)}, bf16[640,2048]{1,0:T(8,128)(2,1)}, f32[320,1024]{1,0:T(8,128)S(1)}, bf16[320,1024]{1,0:T(8,128)(2,1)S(1)}, bf16[...) custom-call(bf16[320,1024]{1,0:T(8,128)(2,1)S(1)} %get-tuple-element.11, ...), custom_call_target="tpu_custom_call" | custom-call | flops 10737418240 | bytes 16777216 | tf_op jit(solution)/shard_map/expert/pallas_call | solution.py:714
  90.1 2.0 collective-permute-done.8.came_ref
  92.1 2.9 %norm2_back.1 = (f32[320,1024]{1,0:T(8,128)S(1)}, bf16[256,1280]{1,0:T(8,128)(2,1)}, f32[16,128]{1,0:T(8,128)S(1)}) custom-call(f32[320,1024]{1,0:T(8,128)S(1)} %get-tuple-element.119.kept_ref, bf16[320,1024]{1,0:T(8,128)(2,1)S(1)} %collective-permute-done.8.came_ref, f32[320,1024]{1,0:T(8,128)S(1)} %get-tuple-element.113.resid_ref, ...), custom_call_target="tpu_custom_call" | custom-call | flops 503316480 | bytes 5910528 | tf_op jit(solution)/shard_map/norm2_back/pallas_call | solution.py:682
  95.0 1.1 copy-done.2
  96.1 4.8 %all-to-all-start.2 = ((bf16[32,8,1280]{2,1,0:T(8,128)(2,1)}), bf16[32,8,1280]{2,1,0:T(8,128)(2,1)S(1)}, u32[]{:S(2)}, u32[]{:S(2)}) async-start(bf16[32,8,1280]{2,1,0:T(8,128)(2,1)} %bitcast.15), calls=%async_computation.2 | async-start | bytes 1310720 | tf_op jit(solution)/shard_map/all_to_all | solution.py:877
  101.5 11.6 %expert_grads.1 = (f32[1024,2048]{1,0:T(8,128)}, f32[2048,1024]{1,0:T(8,128)}) custom-call(bf16[640,1024]{1,0:T(8,128)(2,1)} %get-tuple-element.124.rows_ref, bf16[640,1024]{1,0:T(8,128)(2,1)} %get-tuple-element.125.grads_ref, bf16[640,2048]{1,0:T(8,128)(2,1)} %get-tuple-element.127.hidden_ref, bf16[640,2048]{1,0:T(8,128)(2,1)} %get-tuple-element.128.dpre_ref), custom_call_target="tpu_custom_call" | custom-call | flops 5368709120 | bytes 25165824 | tf_op jit(solution)/shard_map/expert_grads/pallas_call | solution.py:745
  114.7 3.8 %all-to-all-done.2 = bf16[32,8,1280]{2,1,0:T(8,128)(2,1)S(1)} async-done(((bf16[32,8,1280]{2,1,0:T(8,128)(2,1)}), bf16[32,8,1280]{2,1,0:T(8,128)(2,1)S(1)}, u32[]{:S(2)}, u32[]{:S(2)}) %all-to-all-start.2) | async-done | bytes 655392 | tf_op jit(solution)/shard_map/all_to_all | solution.py:877
  119.3 1.8 collective-permute-done.12.other_ref
  121.1 3.4 %out_grad.1 = (bf16[512,1024]{1,0:T(8,128)(2,1)S(1)}, bf16[4,256,128]{2,1,0:T(8,128)(2,1)}, bf16[4,256,128]{2,1,0:T(8,128)(2,1)}, bf16[4,256,128]{2,1,0:T(8,128)(2,1)}, bf16[4,256,128]{2,1,0:T(8,128)(2,1)}) custom-call(s32[3]{0:T(128)S(1)} %pad_add_fusion.where_ref, bf16[256,1024]{1,0:T(8,128)(2,1)S(1)} %gather2.1.own_ref, ...), custom_call_target="tpu_custom_call" | custom-call | flops 536870912 | bytes 3670028 | tf_op jit(solution)/shard_map/out_grad/pallas_call | solution.py:682
  124.5 1.4 collective-permute-start.13
  126.0 1.5 collective-permute-start.14
  128.1 8.9 %attend_back.1 = (f32[256,1024]{1,0:T(8,128)S(1)}, bf16[256,1024]{1,0:T(8,128)(2,1)S(1)}, bf16[512,128]{1,0:T(8,128)(2,1)}, bf16[512,128]{1,0:T(8,128)(2,1)}, bf...) custom-call(s32[3]{0:T(128)S(1)} %pad_add_fusion.where_ref, ...), custom_call_target="tpu_custom_call" | custom-call | flops 7516192768 | bytes 10747936 | tf_op jit(solution)/shard_map/attend_back/pallas_call | solution.py:682
  137.0 3.0 %collective-permute-done.14.refs_13_ = bf16[4,256,128]{2,1,0:T(8,128)(2,1)S(1)} collective-permute-done((bf16[4,256,128]{2,1,0:T(8,128)(2,1)}, bf16[4,256,128]{2,1,0:T(8,128)(2,1)S(1)}, u32[]{:S(2)}, u32[]{:S(2)}) %collective-permute-start.14) | collective-permute-done | bytes 262176 | tf_op jit(solution)/shard_map/ppermute | solution.py:765
  140.0 1.0 collective-permute-start.17
  142.0 1.6 collective-permute-start.19
  143.5 1.4 scatter2.1
  145.0 1.6 collective-permute-done.17.refs_1_
  147.3 2.4 collective-permute-done.19.refs_3_
  149.7 3.2 %all-to-all-start.3 = ((bf16[32,8,1280]{2,1,0:T(8,128)(2,1)}), bf16[32,8,1280]{2,1,0:T(8,128)(2,1)S(1)}, u32[]{:S(2)}, u32[]{:S(2)}) async-start(bf16[32,8,1280]{2,1,0:T(8,128)(2,1)} %bitcast.17), calls=%async_computation.3 | async-start | bytes 1310720 | tf_op jit(solution)/shard_map/all_to_all | solution.py:877
  153.0 4.0 %value_grad.1 = (bf16[2,512,128]{2,1,0:T(8,128)(2,1)}, bf16[2,512,128]{2,1,0:T(8,128)(2,1)S(1)}) custom-call(s32[3]{0:T(128)S(1)} %pad_add_fusion.where_ref, bf16[512,128]{1,0:T(8,128)(2,1)} %get-tuple-element.166.refs_0_, bf16[512,128]{1,0:T(8,128)(2,1)S(1)} %collective-permute-done.17.refs_1_, bf16[512,128]{1,0:T(8,128)(2,1)S(1)} %collective-permute-done.18.refs_2_, ...), custom_call_target="tpu_custom_call" | custom-call | flops 536870912 | bytes 6291468 | tf_op jit(solution)/shard_map/value_grad/pallas_call | solution.py:682
  157.0 1.5 collective-permute-start.23
  158.5 1.5 collective-permute-start.20
  160.0 1.5 collective-permute-start.21
  162.0 9.7 %collective-permute-done.23.came_ref = bf16[2,512,128]{2,1,0:T(8,128)(2,1)S(1)} collective-permute-done((bf16[2,512,128]{2,1,0:T(8,128)(2,1)S(1)}, bf16[2,512,128]{2,1,0:T(8,128)(2,1)S(1)}, u32[]{:S(2)}, u32[]{:S(2)}) %collective-permute-start.23) | collective-permute-done | bytes 262176 | tf_op jit(solution)/shard_map/ppermute | solution.py:765
  171.7 1.7 add.17
  173.4 2.4 collective-permute-start.25
  176.2 4.4 %key_query_grad.1 = (bf16[2,512,128]{2,1,0:T(8,128)(2,1)}, bf16[2,512,128]{2,1,0:T(8,128)(2,1)S(1)}) custom-call(s32[3]{0:T(128)S(1)} %pad_add_fusion.where_ref, bf16[2,512,128]{2,1,0:T(8,128)(2,1)} %get-tuple-element.159.refs_0_, bf16[2,512,128]{2,1,0:T(8,128)(2,1)S(1)} %collective-permute-done.20.refs_1_, ...), custom_call_target="tpu_custom_call" | custom-call | flops 1073741824 | bytes 5767180 | tf_op jit(solution)/shard_map/key_query_grad/pallas_call | solution.py:682
  180.7 1.1 collective-permute-start.24
  181.9 0.9 last_add.1.own_ref
  182.9 1.7 collective-permute-start.27
  184.6 5.7 %collective-permute-done.24.came_ref = bf16[2,512,128]{2,1,0:T(8,128)(2,1)S(1)} collective-permute-done((bf16[2,512,128]{2,1,0:T(8,128)(2,1)S(1)}, bf16[2,512,128]{2,1,0:T(8,128)(2,1)S(1)}, u32[]{:S(2)}, u32[]{:S(2)}) %collective-permute-start.24) | collective-permute-done | bytes 262176 | tf_op jit(solution)/shard_map/ppermute | solution.py:765
  190.3 1.7 add.18
  192.0 1.2 collective-permute-start.31
  193.1 2.1 collective-permute-start.26
  195.3 3.9 %norm1_back.1 = (f32[320,1024]{1,0:T(8,128)}, f32[16,128]{1,0:T(8,128)S(1)}) custom-call(bf16[256,1280]{1,0:T(8,128)(2,1)S(1)} %bitcast.29, bf16[320,1024]{1,0:T(8,128)(2,1)} %x_ref.5, f32[320,1024]{1,0:T(8,128)} %copy-done.2, f32[1,1024]{1,0:T(1,128)} %bitcast.40), custom_call_target="tpu_custom_call" | custom-call | flops 503316480 | bytes 3944448 | tf_op jit(solution)/shard_map/norm1_back/pallas_call | solution.py:682
  200.5 0.9 last_add_sums.1.own_ref
  201.5 1.0 collective-permute-start.34
  202.5 3.3 %collective-permute-start.33 = (bf16[2048,128]{1,0:T(8,128)(2,1)S(1)}, bf16[2048,128]{1,0:T(8,128)(2,1)S(1)}, u32[]{:S(2)}, u32[]{:S(2)}) collective-permute-start(bf16[2048,128]{1,0:T(8,128)(2,1)S(1)} %stack.21.refs_0_), channel_id=1, source_target_pairs={{0,2},{2,0},{4,6},{6,4},{8,10},{10,8},{12,14},{14,12},{16,18},{18,... | collective-permute-start | bytes 1572872 | tf_op jit(solution)/shard_map/ppermute | solution.py:765
  205.8 2.2 collective-permute-start.30
  207.9 6.2 %collective-permute-done.30.came_ref = bf16[576,128]{1,0:T(8,128)(2,1)S(1)} collective-permute-done((bf16[576,128]{1,0:T(8,128)(2,1)S(1)}, bf16[576,128]{1,0:T(8,128)(2,1)S(1)}, u32[]{:S(2)}, u32[]{:S(2)}) %collective-permute-start.30) | collective-permute-done | bytes 147488 | tf_op jit(solution)/shard_map/ppermute | solution.py:765
  214.3 1.4 collective-permute-done.34.refs_2_
  216.6 4.2 %collective-permute-done.32.came_ref = bf16[1088,128]{1,0:T(8,128)(2,1)S(1)} collective-permute-done((bf16[1088,128]{1,0:T(8,128)(2,1)S(1)}, bf16[1088,128]{1,0:T(8,128)(2,1)S(1)}, u32[]{:S(2)}, u32[]{:S(2)}) %collective-permute-start.32) | collective-permute-done | bytes 278560 | tf_op jit(solution)/shard_map/ppermute | solution.py:765
  221.4 1.4 collective-permute-start.35
  223.3 1.8 collective-permute-start.37
  225.2 10.8 %collective-permute-done.38.refs_4_ = bf16[1024,128]{1,0:T(8,128)(2,1)S(1)} collective-permute-done((bf16[1024,128]{1,0:T(8,128)(2,1)S(1)}, bf16[1024,128]{1,0:T(8,128)(2,1)S(1)}, u32[]{:S(2)}, u32[]{:S(2)}) %collective-permute-start.38) | collective-permute-done | bytes 262176 | tf_op jit(solution)/shard_map/ppermute | solution.py:765
  236.0 2.5 collective-permute-done.37.refs_3_
  238.5 2.9 %finish_out_value.1 = (f32[3,1024,512]{2,1,0:T(8,128)}, f32[512,1024]{1,0:T(8,128)}) custom-call(s32[3]{0:T(128)S(1)} %pad_add_fusion.where_ref, bf16[2048,128]{1,0:T(8,128)(2,1)S(1)} %stack.21.refs_0_, bf16[2048,128]{1,0:T(8,128)(2,1)S(1)} %collective-permute-done.33.refs_1_, bf16[2048,128]{1,0:T(8,128)(2,1)S(1)} %collective-permute-done.34.refs_2_, ...), custom_call_target="tpu_custom_call" | custom-call | bytes 6291456 | tf_op jit(solution)/shard_map/finish_out_value/pallas_call | solution.py:1061
  241.9 1.7 collective-permute-start.39
  243.7 1.1 add_convert_fusion
  244.8 3.2 %collective-permute-done.40.refs_4_ = bf16[1056,128]{1,0:T(8,128)(2,1)S(1)} collective-permute-done((bf16[1056,128]{1,0:T(8,128)(2,1)S(1)}, bf16[1056,128]{1,0:T(8,128)(2,1)S(1)}, u32[]{:S(2)}, u32[]{:S(2)}) %collective-permute-start.40) | collective-permute-done | bytes 270368 | tf_op jit(solution)/shard_map/ppermute | solution.py:765
  248.4 3.1 %finish_key_query.1 = (f32[3,1024,512]{2,1,0:T(8,128)}, f32[32,128]{1,0:T(8,128)S(1)}) custom-call(s32[3]{0:T(128)S(1)} %pad_add_fusion.where_ref, bf16[2112,128]{1,0:T(8,128)(2,1)S(1)} %stack.23.refs_0_, bf16[2112,128]{1,0:T(8,128)(2,1)S(1)} %collective-permute-done.35.refs_1_, ...), custom_call_target="tpu_custom_call", output_to_operand_aliasing={{0}: (6, {})} | custom-call | bytes 6291456 | tf_op jit(solution)/shard_map/finish_key_query/pallas_call | solution.py:1063
  (102 shorter events, 15.7 us)
Async XLA Ops:
  0.6 10.7 %copy-start.6 = (s32[256]{0:T(256)S(1)}, s32[256]{0:T(256)}, u32[]{:S(2)}) copy-start(s32[256]{0:T(256)} %param.13) | copy-start | bytes 3076
  4.0 25.2 %all-to-all-start = ((bf16[32,8,1280]{2,1,0:T(8,128)(2,1)}), bf16[32,8,1280]{2,1,0:T(8,128)(2,1)S(1)}, u32[]{:S(2)}, u32[]{:S(2)}) async-start(bf16[32,8,1280]{2,1,0:T(8,128)(2,1)} %bitcast.5), calls=%async_computation | async-start | bytes 1310720 | tf_op jit(solution)/shard_map/all_to_all | solution.py:877
  11.3 20.5 %copy-start.8 = (s32[1,5]{1,0:T(1,128)S(1)}, s32[1,5]{1,0:T(1,128)}, u32[]{:S(2)}) copy-start(s32[1,5]{1,0:T(1,128)} %lengths_ref.3) | copy-start | bytes 64
  11.5 28.5 %copy-start.3 = (s32[256,1]{1,0:T(8,128)}, s32[256,1]{1,0:T(8,128)S(1)}, u32[]{:S(2)}) copy-start(s32[256,1]{1,0:T(8,128)S(1)} %copy.23.dispatch_ref) | copy-start | bytes 3076
  29.8 2.0 collective-permute-start
  39.9 2.0 collective-permute-start.1
  41.9 27.0 %copy-start = (bf16[320,1024]{1,0:T(8,128)(2,1)S(1)}, bf16[320,1024]{1,0:T(8,128)(2,1)}, u32[]{:S(2)}) copy-start(bf16[320,1024]{1,0:T(8,128)(2,1)} %x_ref.5) | copy-start | bytes 1966084
  41.9 27.0 %copy-start.1 = (bf16[320,1024]{1,0:T(8,128)(2,1)S(1)}, bf16[320,1024]{1,0:T(8,128)(2,1)}, u32[]{:S(2)}) copy-start(bf16[320,1024]{1,0:T(8,128)(2,1)} %grad_ref.3) | copy-start | bytes 1966084
  41.9 27.0 %copy-start.5 = (f32[1024]{0:T(1024)S(1)}, f32[1024]{0:T(1024)}, u32[]{:S(2)}) copy-start(f32[1024]{0:T(1024)} %param.17) | copy-start | bytes 12292
  41.9 27.0 %copy-start.7 = (f32[1024]{0:T(1024)S(1)}, f32[1024]{0:T(1024)}, u32[]{:S(2)}) copy-start(f32[1024]{0:T(1024)} %param.18) | copy-start | bytes 12292
  43.4 3.7 %copy-start.17 = (bf16[256,1024]{1,0:T(8,128)(2,1)S(1)}, bf16[256,1024]{1,0:T(8,128)(2,1)}, u32[]{:S(2)}) copy-start(bf16[256,1024]{1,0:T(8,128)(2,1)} %get-tuple-element.121) | copy-start | bytes 1572868
  43.4 25.4 %all-to-all-start.1 = ((bf16[32,8,1280]{2,1,0:T(8,128)(2,1)}), bf16[32,8,1280]{2,1,0:T(8,128)(2,1)S(1)}, u32[]{:S(2)}, u32[]{:S(2)}) async-start(bf16[32,8,1280]{2,1,0:T(8,128)(2,1)} %bitcast.9), calls=%async_computation.1 | async-start | bytes 1310720 | tf_op jit(solution)/shard_map/all_to_all | solution.py:877
  47.1 20.9 %collective-permute-start.3 = (bf16[256,1024]{1,0:T(8,128)(2,1)S(1)}, bf16[256,1024]{1,0:T(8,128)(2,1)S(1)}, u32[]{:S(2)}, u32[]{:S(2)}) collective-permute-start(bf16[256,1024]{1,0:T(8,128)(2,1)S(1)} %copy-done.17), channel_id=1, source_target_pairs={{0,4},{2,6},{4,0},{6,2},{8,12},{10,14},{12,8},{14,10},{16,20},{18,... | collective-permute-start | bytes 1572872 | tf_op jit(solution)/shard_map/ppermute | solution.py:765
  48.8 20.1 %collective-permute-start.2 = (bf16[256,1024]{1,0:T(8,128)(2,1)S(1)}, bf16[256,1024]{1,0:T(8,128)(2,1)}, u32[]{:S(2)}, u32[]{:S(2)}) collective-permute-start(bf16[256,1024]{1,0:T(8,128)(2,1)S(1)} %copy-done.17), channel_id=1, source_target_pairs={{0,2},{2,0},{4,6},{6,4},{8,10},{10,8},{12,14},{14,12},{16,18},{18,... | collective-permute-start | bytes 1572872 | tf_op jit(solution)/shard_map/ppermute | solution.py:765
  70.1 2.2 collective-permute-start.4
  70.2 3.0 %collective-permute-start.5 = (bf16[320,1024]{1,0:T(8,128)(2,1)S(1)}, bf16[320,1024]{1,0:T(8,128)(2,1)S(1)}, u32[]{:S(2)}, u32[]{:S(2)}) collective-permute-start(bf16[320,1024]{1,0:T(8,128)(2,1)S(1)} %get-tuple-element.116.up_ref), channel_id=1, source_target_pairs={{0,1},{1,0},{2,3},{3,2},{4,5},{5,4},{6,7},{7,6},{8,9},{9,8},{10,11... | collective-permute-start | bytes 1966088 | tf_op jit(solution)/shard_map/ppermute | solution.py:765
  70.7 19.2 %collective-permute-start.7 = (bf16[256,1024]{1,0:T(8,128)(2,1)}, bf16[256,1024]{1,0:T(8,128)(2,1)S(1)}, u32[]{:S(2)}, u32[]{:S(2)}) collective-permute-start(bf16[256,1024]{1,0:T(8,128)(2,1)} %get-tuple-element.121), channel_id=1, source_target_pairs={{0,6},{2,4},{4,2},{6,0},{8,14},{10,12},{12,10},{14,8},{16,22},{18,... | collective-permute-start | bytes 1572872 | tf_op jit(solution)/shard_map/ppermute | solution.py:765
  89.9 5.1 %copy-start.11 = (bf16[256,1024]{1,0:T(8,128)(2,1)}, bf16[256,1024]{1,0:T(8,128)(2,1)S(1)}, u32[]{:S(2)}) copy-start(bf16[256,1024]{1,0:T(8,128)(2,1)S(1)} %collective-permute-done.7.refs_7_) | copy-start | bytes 1572868
  89.9 2.2 collective-permute-start.8
  95.0 1.1 copy-start.2
  96.1 4.9 %copy-start.10 = (bf16[256,1024]{1,0:T(8,128)(2,1)S(1)}, bf16[256,1024]{1,0:T(8,128)(2,1)}, u32[]{:S(2)}) copy-start(bf16[256,1024]{1,0:T(8,128)(2,1)} %copy-done.9) | copy-start | bytes 1572868
  96.1 5.4 %copy-start.12 = (bf16[256,1024]{1,0:T(8,128)(2,1)S(1)}, bf16[256,1024]{1,0:T(8,128)(2,1)}, u32[]{:S(2)}) copy-start(bf16[256,1024]{1,0:T(8,128)(2,1)} %copy-done.11) | copy-start | bytes 1572868
  96.1 22.5 %all-to-all-start.2 = ((bf16[32,8,1280]{2,1,0:T(8,128)(2,1)}), bf16[32,8,1280]{2,1,0:T(8,128)(2,1)S(1)}, u32[]{:S(2)}, u32[]{:S(2)}) async-start(bf16[32,8,1280]{2,1,0:T(8,128)(2,1)} %bitcast.15), calls=%async_computation.2 | async-start | bytes 1310720 | tf_op jit(solution)/shard_map/all_to_all | solution.py:877
  100.8 12.3 %collective-permute-start.9 = (bf16[256,1024]{1,0:T(8,128)(2,1)}, bf16[256,1024]{1,0:T(8,128)(2,1)S(1)}, u32[]{:S(2)}, u32[]{:S(2)}) collective-permute-start(bf16[256,1024]{1,0:T(8,128)(2,1)} %collective-permute-done.2.refs_5_), channel_id=1, source_target_pairs={{0,1},{1,0},{2,3},{3,2},{4,5},{5,4},{6,7},{7,6},{8,9},{9,8},{10,11... | collective-permute-start | bytes 1572872 | tf_op jit(solution)/shard_map/ppermute | solution.py:765
  100.9 12.2 %collective-permute-start.10 = (bf16[256,1024]{1,0:T(8,128)(2,1)S(1)}, bf16[256,1024]{1,0:T(8,128)(2,1)S(1)}, u32[]{:S(2)}, u32[]{:S(2)}) collective-permute-start(bf16[256,1024]{1,0:T(8,128)(2,1)S(1)} %copy-done.10), channel_id=1, source_target_pairs={{0,1},{1,0},{2,3},{3,2},{4,5},{5,4},{6,7},{7,6},{8,9},{9,8},{10,11... | collective-permute-start | bytes 1572872 | tf_op jit(solution)/shard_map/ppermute | solution.py:765
  101.4 13.3 %collective-permute-start.11 = (bf16[256,1024]{1,0:T(8,128)(2,1)S(1)}, bf16[256,1024]{1,0:T(8,128)(2,1)}, u32[]{:S(2)}, u32[]{:S(2)}) collective-permute-start(bf16[256,1024]{1,0:T(8,128)(2,1)S(1)} %copy-done.12), channel_id=1, source_target_pairs={{0,1},{1,0},{2,3},{3,2},{4,5},{5,4},{6,7},{7,6},{8,9},{9,8},{10,11... | collective-permute-start | bytes 1572872 | tf_op jit(solution)/shard_map/ppermute | solution.py:765
  101.5 17.0 %copy-start.4 = (s32[256,1]{1,0:T(8,128)S(1)}, s32[256,1]{1,0:T(8,128)}, u32[]{:S(2)}) copy-start(s32[256,1]{1,0:T(8,128)} %copy-done.3) | copy-start | bytes 3076
  113.9 0.8 copy-start.14
  119.2 2.0 collective-permute-start.12
  124.5 12.5 %collective-permute-start.13 = (bf16[4,256,128]{2,1,0:T(8,128)(2,1)}, bf16[4,256,128]{2,1,0:T(8,128)(2,1)S(1)}, u32[]{:S(2)}, u32[]{:S(2)}) collective-permute-start(bf16[4,256,128]{2,1,0:T(8,128)(2,1)} %get-tuple-element.149), channel_id=1, source_target_pairs={{0,2},{2,0},{4,6},{6,4},{8,10},{10,8},{12,14},{14,12},{16,18},{18,... | collective-permute-start | bytes 786440 | tf_op jit(solution)/shard_map/ppermute | solution.py:765
  126.0 14.1 %collective-permute-start.14 = (bf16[4,256,128]{2,1,0:T(8,128)(2,1)}, bf16[4,256,128]{2,1,0:T(8,128)(2,1)S(1)}, u32[]{:S(2)}, u32[]{:S(2)}) collective-permute-start(bf16[4,256,128]{2,1,0:T(8,128)(2,1)} %get-tuple-element.150), channel_id=1, source_target_pairs={{0,4},{2,6},{4,0},{6,2},{8,12},{10,14},{12,8},{14,10},{16,20},{18,... | collective-permute-start | bytes 786440 | tf_op jit(solution)/shard_map/ppermute | solution.py:765
  127.5 12.6 %collective-permute-start.15 = (bf16[4,256,128]{2,1,0:T(8,128)(2,1)}, bf16[4,256,128]{2,1,0:T(8,128)(2,1)S(1)}, u32[]{:S(2)}, u32[]{:S(2)}) collective-permute-start(bf16[4,256,128]{2,1,0:T(8,128)(2,1)} %get-tuple-element.151), channel_id=1, source_target_pairs={{0,6},{2,4},{4,2},{6,0},{8,14},{10,12},{12,10},{14,8},{16,22},{18,... | collective-permute-start | bytes 786440 | tf_op jit(solution)/shard_map/ppermute | solution.py:765
  140.0 3.5 %collective-permute-start.16 = (bf16[256,1024]{1,0:T(8,128)(2,1)S(1)}, bf16[256,1024]{1,0:T(8,128)(2,1)S(1)}, u32[]{:S(2)}, u32[]{:S(2)}) collective-permute-start(bf16[256,1024]{1,0:T(8,128)(2,1)S(1)} %get-tuple-element.152), channel_id=1, source_target_pairs={{0,1},{1,0},{2,3},{3,2},{4,5},{5,4},{6,7},{7,6},{8,9},{9,8},{10,11... | collective-permute-start | bytes 1572872 | tf_op jit(solution)/shard_map/ppermute | solution.py:765
  140.0 6.5 %collective-permute-start.17 = (bf16[512,128]{1,0:T(8,128)(2,1)}, bf16[512,128]{1,0:T(8,128)(2,1)S(1)}, u32[]{:S(2)}, u32[]{:S(2)}) collective-permute-start(bf16[512,128]{1,0:T(8,128)(2,1)} %get-tuple-element.153), channel_id=1, source_target_pairs={{0,2},{2,0},{4,6},{6,4},{8,10},{10,8},{12,14},{14,12},{16,18},{18,... | collective-permute-start | bytes 393224 | tf_op jit(solution)/shard_map/ppermute | solution.py:765
  141.1 6.2 %collective-permute-start.18 = (bf16[512,128]{1,0:T(8,128)(2,1)}, bf16[512,128]{1,0:T(8,128)(2,1)S(1)}, u32[]{:S(2)}, u32[]{:S(2)}) collective-permute-start(bf16[512,128]{1,0:T(8,128)(2,1)} %get-tuple-element.154), channel_id=1, source_target_pairs={{0,4},{2,6},{4,0},{6,2},{8,12},{10,14},{12,8},{14,10},{16,20},{18,... | collective-permute-start | bytes 393224 | tf_op jit(solution)/shard_map/ppermute | solution.py:765
  142.0 7.8 %collective-permute-start.19 = (bf16[512,128]{1,0:T(8,128)(2,1)}, bf16[512,128]{1,0:T(8,128)(2,1)S(1)}, u32[]{:S(2)}, u32[]{:S(2)}) collective-permute-start(bf16[512,128]{1,0:T(8,128)(2,1)} %get-tuple-element.155), channel_id=1, source_target_pairs={{0,6},{2,4},{4,2},{6,0},{8,14},{10,12},{12,10},{14,8},{16,22},{18,... | collective-permute-start | bytes 393224 | tf_op jit(solution)/shard_map/ppermute | solution.py:765
  149.7 45.6 %all-to-all-start.3 = ((bf16[32,8,1280]{2,1,0:T(8,128)(2,1)}), bf16[32,8,1280]{2,1,0:T(8,128)(2,1)S(1)}, u32[]{:S(2)}, u32[]{:S(2)}) async-start(bf16[32,8,1280]{2,1,0:T(8,128)(2,1)} %bitcast.17), calls=%async_computation.3 | async-start | bytes 1310720 | tf_op jit(solution)/shard_map/all_to_all | solution.py:877
  153.0 5.5 %copy-start.20 = (bf16[2,512,128]{2,1,0:T(8,128)(2,1)S(1)}, bf16[2,512,128]{2,1,0:T(8,128)(2,1)}, u32[]{:S(2)}) copy-start(bf16[2,512,128]{2,1,0:T(8,128)(2,1)} %get-tuple-element.163) | copy-start | bytes 786436
  153.0 7.0 %copy-start.19 = (bf16[2,512,128]{2,1,0:T(8,128)(2,1)S(1)}, bf16[2,512,128]{2,1,0:T(8,128)(2,1)}, u32[]{:S(2)}) copy-start(bf16[2,512,128]{2,1,0:T(8,128)(2,1)} %get-tuple-element.164) | copy-start | bytes 786436
  153.0 8.4 %copy-start.18 = (bf16[2,512,128]{2,1,0:T(8,128)(2,1)S(1)}, bf16[2,512,128]{2,1,0:T(8,128)(2,1)}, u32[]{:S(2)}) copy-start(bf16[2,512,128]{2,1,0:T(8,128)(2,1)} %get-tuple-element.165) | copy-start | bytes 786436
  157.0 14.8 %collective-permute-start.23 = (bf16[2,512,128]{2,1,0:T(8,128)(2,1)S(1)}, bf16[2,512,128]{2,1,0:T(8,128)(2,1)S(1)}, u32[]{:S(2)}, u32[]{:S(2)}) collective-permute-start(bf16[2,512,128]{2,1,0:T(8,128)(2,1)S(1)} %get-tuple-element.173), channel_id=1, source_target_pairs={{0,8},{2,10},{4,12},{6,14},{8,0},{10,2},{12,4},{14,6},{16,24},{18,... | collective-permute-start | bytes 786440 | tf_op jit(solution)/shard_map/ppermute | solution.py:765
  158.5 17.3 %collective-permute-start.20 = (bf16[2,512,128]{2,1,0:T(8,128)(2,1)S(1)}, bf16[2,512,128]{2,1,0:T(8,128)(2,1)S(1)}, u32[]{:S(2)}, u32[]{:S(2)}) collective-permute-start(bf16[2,512,128]{2,1,0:T(8,128)(2,1)S(1)} %copy-done.20), channel_id=1, source_target_pairs={{0,2},{2,0},{4,6},{6,4},{8,10},{10,8},{12,14},{14,12},{16,18},{18,... | collective-permute-start | bytes 786440 | tf_op jit(solution)/shard_map/ppermute | solution.py:765
  160.0 16.3 %collective-permute-start.21 = (bf16[2,512,128]{2,1,0:T(8,128)(2,1)S(1)}, bf16[2,512,128]{2,1,0:T(8,128)(2,1)S(1)}, u32[]{:S(2)}, u32[]{:S(2)}) collective-permute-start(bf16[2,512,128]{2,1,0:T(8,128)(2,1)S(1)} %copy-done.19), channel_id=1, source_target_pairs={{0,4},{2,6},{4,0},{6,2},{8,12},{10,14},{12,8},{14,10},{16,20},{18,... | collective-permute-start | bytes 786440 | tf_op jit(solution)/shard_map/ppermute | solution.py:765
  161.4 14.8 %collective-permute-start.22 = (bf16[2,512,128]{2,1,0:T(8,128)(2,1)S(1)}, bf16[2,512,128]{2,1,0:T(8,128)(2,1)S(1)}, u32[]{:S(2)}, u32[]{:S(2)}) collective-permute-start(bf16[2,512,128]{2,1,0:T(8,128)(2,1)S(1)} %copy-done.18), channel_id=1, source_target_pairs={{0,6},{2,4},{4,2},{6,0},{8,14},{10,12},{12,10},{14,8},{16,22},{18,... | collective-permute-start | bytes 786440 | tf_op jit(solution)/shard_map/ppermute | solution.py:765
  173.4 8.5 %collective-permute-start.25 = (bf16[1,512,128]{2,1,0:T(8,128)(2,1)S(1)}, bf16[1,512,128]{2,1,0:T(8,128)(2,1)S(1)}, u32[]{:S(2)}, u32[]{:S(2)}) collective-permute-start(bf16[1,512,128]{2,1,0:T(8,128)(2,1)S(1)} %get-tuple-element.174), channel_id=1, source_target_pairs={{0,16},{2,18},{4,20},{6,22},{8,24},{10,26},{12,28},{14,30},{16,0},... | collective-permute-start | bytes 393224 | tf_op jit(solution)/shard_map/ppermute | solution.py:765
  180.7 9.6 %collective-permute-start.24 = (bf16[2,512,128]{2,1,0:T(8,128)(2,1)S(1)}, bf16[2,512,128]{2,1,0:T(8,128)(2,1)S(1)}, u32[]{:S(2)}, u32[]{:S(2)}) collective-permute-start(bf16[2,512,128]{2,1,0:T(8,128)(2,1)S(1)} %get-tuple-element.179), channel_id=1, source_target_pairs={{0,8},{2,10},{4,12},{6,14},{8,0},{10,2},{12,4},{14,6},{16,24},{18,... | collective-permute-start | bytes 786440 | tf_op jit(solution)/shard_map/ppermute | solution.py:765
  182.9 9.1 %collective-permute-start.27 = (bf16[512,128]{1,0:T(8,128)(2,1)S(1)}, bf16[512,128]{1,0:T(8,128)(2,1)S(1)}, u32[]{:S(2)}, u32[]{:S(2)}) collective-permute-start(bf16[512,128]{1,0:T(8,128)(2,1)S(1)} %last_add.1.own_ref), channel_id=1, source_target_pairs={{0,16},{2,18},{4,20},{6,22},{8,24},{10,26},{12,28},{14,30},{16,0},... | collective-permute-start | bytes 393224 | tf_op jit(solution)/shard_map/ppermute | solution.py:765
  192.0 9.5 %collective-permute-start.31 = (bf16[1024,128]{1,0:T(8,128)(2,1)S(1)}, bf16[1024,128]{1,0:T(8,128)(2,1)S(1)}, u32[]{:S(2)}, u32[]{:S(2)}) collective-permute-start(bf16[1024,128]{1,0:T(8,128)(2,1)S(1)} %stack.20.own_ref), channel_id=1, source_target_pairs={{0,8},{2,10},{4,12},{6,14},{8,0},{10,2},{12,4},{14,6},{16,24},{18,... | collective-permute-start | bytes 786440 | tf_op jit(solution)/shard_map/ppermute | solution.py:765
  193.1 6.5 %collective-permute-start.26 = (bf16[1,512,128]{2,1,0:T(8,128)(2,1)S(1)}, bf16[1,512,128]{2,1,0:T(8,128)(2,1)S(1)}, u32[]{:S(2)}, u32[]{:S(2)}) collective-permute-start(bf16[1,512,128]{2,1,0:T(8,128)(2,1)S(1)} %get-tuple-element.184), channel_id=1, source_target_pairs={{0,16},{2,18},{4,20},{6,22},{8,24},{10,26},{12,28},{14,30},{16,0},... | collective-permute-start | bytes 393224 | tf_op jit(solution)/shard_map/ppermute | solution.py:765
  195.3 4.4 %collective-permute-start.29 = (f32[16,128]{1,0:T(8,128)S(1)}, f32[16,128]{1,0:T(8,128)S(1)}, u32[]{:S(2)}, u32[]{:S(2)}) collective-permute-start(f32[16,128]{1,0:T(8,128)S(1)} %get-tuple-element.188.refs_2_), channel_id=1, source_target_pairs={{0,1},{1,0},{2,3},{3,2},{4,5},{5,4},{6,7},{7,6},{8,9},{9,8},{10,11... | collective-permute-start | bytes 24584 | tf_op jit(solution)/shard_map/ppermute | solution.py:765
  199.1 15.1 %copy-start.16 = (bf16[320,1024]{1,0:T(8,128)(2,1)S(1)}, bf16[320,1024]{1,0:T(8,128)(2,1)}, u32[]{:S(2)}) copy-start(bf16[320,1024]{1,0:T(8,128)(2,1)} %get-tuple-element.118) | copy-start | bytes 1966084
  199.2 1.3 collective-permute-start.28
  201.5 14.2 %collective-permute-start.34 = (bf16[2048,128]{1,0:T(8,128)(2,1)S(1)}, bf16[2048,128]{1,0:T(8,128)(2,1)S(1)}, u32[]{:S(2)}, u32[]{:S(2)}) collective-permute-start(bf16[2048,128]{1,0:T(8,128)(2,1)S(1)} %stack.21.refs_0_), channel_id=1, source_target_pairs={{0,4},{2,6},{4,0},{6,2},{8,12},{10,14},{12,8},{14,10},{16,20},{18,... | collective-permute-start | bytes 1572872 | tf_op jit(solution)/shard_map/ppermute | solution.py:765
  202.5 14.1 %collective-permute-start.33 = (bf16[2048,128]{1,0:T(8,128)(2,1)S(1)}, bf16[2048,128]{1,0:T(8,128)(2,1)S(1)}, u32[]{:S(2)}, u32[]{:S(2)}) collective-permute-start(bf16[2048,128]{1,0:T(8,128)(2,1)S(1)} %stack.21.refs_0_), channel_id=1, source_target_pairs={{0,2},{2,0},{4,6},{6,4},{8,10},{10,8},{12,14},{14,12},{16,18},{18,... | collective-permute-start | bytes 1572872 | tf_op jit(solution)/shard_map/ppermute | solution.py:765
  205.8 8.3 %collective-permute-start.30 = (bf16[576,128]{1,0:T(8,128)(2,1)S(1)}, bf16[576,128]{1,0:T(8,128)(2,1)S(1)}, u32[]{:S(2)}, u32[]{:S(2)}) collective-permute-start(bf16[576,128]{1,0:T(8,128)(2,1)S(1)} %last_add_sums.1.own_ref), channel_id=1, source_target_pairs={{0,16},{2,18},{4,20},{6,22},{8,24},{10,26},{12,28},{14,30},{16,0},... | collective-permute-start | bytes 442376 | tf_op jit(solution)/shard_map/ppermute | solution.py:765
  214.2 6.6 %collective-permute-start.32 = (bf16[1088,128]{1,0:T(8,128)(2,1)S(1)}, bf16[1088,128]{1,0:T(8,128)(2,1)S(1)}, u32[]{:S(2)}, u32[]{:S(2)}) collective-permute-start(bf16[1088,128]{1,0:T(8,128)(2,1)S(1)} %stack.22.own_ref), channel_id=1, source_target_pairs={{0,8},{2,10},{4,12},{6,14},{8,0},{10,2},{12,4},{14,6},{16,24},{18,... | collective-permute-start | bytes 835592 | tf_op jit(solution)/shard_map/ppermute | solution.py:765
  214.3 29.4 %collective-permute-start.6 = (bf16[320,1024]{1,0:T(8,128)(2,1)S(1)}, bf16[320,1024]{1,0:T(8,128)(2,1)S(1)}, u32[]{:S(2)}, u32[]{:S(2)}) collective-permute-start(bf16[320,1024]{1,0:T(8,128)(2,1)S(1)} %copy-done.16), channel_id=1, source_target_pairs={{0,1},{1,0},{2,3},{3,2},{4,5},{5,4},{6,7},{7,6},{8,9},{9,8},{10,11... | collective-permute-start | bytes 1966088 | tf_op jit(solution)/shard_map/ppermute | solution.py:765
  220.8 20.6 %collective-permute-start.36 = (bf16[2112,128]{1,0:T(8,128)(2,1)S(1)}, bf16[2112,128]{1,0:T(8,128)(2,1)S(1)}, u32[]{:S(2)}, u32[]{:S(2)}) collective-permute-start(bf16[2112,128]{1,0:T(8,128)(2,1)S(1)} %stack.23.refs_0_), channel_id=1, source_target_pairs={{0,4},{2,6},{4,0},{6,2},{8,12},{10,14},{12,8},{14,10},{16,20},{18,... | collective-permute-start | bytes 1622024 | tf_op jit(solution)/shard_map/ppermute | solution.py:765
  221.4 20.1 %collective-permute-start.35 = (bf16[2112,128]{1,0:T(8,128)(2,1)S(1)}, bf16[2112,128]{1,0:T(8,128)(2,1)S(1)}, u32[]{:S(2)}, u32[]{:S(2)}) collective-permute-start(bf16[2112,128]{1,0:T(8,128)(2,1)S(1)} %stack.23.refs_0_), channel_id=1, source_target_pairs={{0,2},{2,0},{4,6},{6,4},{8,10},{10,8},{12,14},{14,12},{16,18},{18,... | collective-permute-start | bytes 1622024 | tf_op jit(solution)/shard_map/ppermute | solution.py:765
  222.8 13.2 %collective-permute-start.38 = (bf16[1024,128]{1,0:T(8,128)(2,1)S(1)}, bf16[1024,128]{1,0:T(8,128)(2,1)S(1)}, u32[]{:S(2)}, u32[]{:S(2)}) collective-permute-start(bf16[1024,128]{1,0:T(8,128)(2,1)S(1)} %slice.33), channel_id=1, source_target_pairs={{0,4},{2,6},{4,0},{6,2},{8,12},{10,14},{12,8},{14,10},{16,20},{18,... | collective-permute-start | bytes 786440 | tf_op jit(solution)/shard_map/ppermute | solution.py:765
  223.3 15.2 %collective-permute-start.37 = (bf16[1024,128]{1,0:T(8,128)(2,1)S(1)}, bf16[1024,128]{1,0:T(8,128)(2,1)S(1)}, u32[]{:S(2)}, u32[]{:S(2)}) collective-permute-start(bf16[1024,128]{1,0:T(8,128)(2,1)S(1)} %slice.32), channel_id=1, source_target_pairs={{0,2},{2,0},{4,6},{6,4},{8,10},{10,8},{12,14},{14,12},{16,18},{18,... | collective-permute-start | bytes 786440 | tf_op jit(solution)/shard_map/ppermute | solution.py:765
  225.2 18.5 %copy-start.15 = (bf16[320,1024]{1,0:T(8,128)(2,1)S(1)}, bf16[320,1024]{1,0:T(8,128)(2,1)}, u32[]{:S(2)}) copy-start(bf16[320,1024]{1,0:T(8,128)(2,1)} %get-tuple-element.117) | copy-start | bytes 1966084
  241.5 6.5 %collective-permute-start.40 = (bf16[1056,128]{1,0:T(8,128)(2,1)S(1)}, bf16[1056,128]{1,0:T(8,128)(2,1)S(1)}, u32[]{:S(2)}, u32[]{:S(2)}) collective-permute-start(bf16[1056,128]{1,0:T(8,128)(2,1)S(1)} %slice.35), channel_id=1, source_target_pairs={{0,4},{2,6},{4,0},{6,2},{8,12},{10,14},{12,8},{14,10},{16,20},{18,... | collective-permute-start | bytes 811016 | tf_op jit(solution)/shard_map/ppermute | solution.py:765
  241.9 6.5 %collective-permute-start.39 = (bf16[1056,128]{1,0:T(8,128)(2,1)S(1)}, bf16[1056,128]{1,0:T(8,128)(2,1)S(1)}, u32[]{:S(2)}, u32[]{:S(2)}) collective-permute-start(bf16[1056,128]{1,0:T(8,128)(2,1)S(1)} %slice.34), channel_id=1, source_target_pairs={{0,2},{2,0},{4,6},{6,4},{8,10},{10,8},{12,14},{14,12},{16,18},{18,... | collective-permute-start | bytes 811016 | tf_op jit(solution)/shard_map/ppermute | solution.py:765
  (2 other events, 1.6 us)
where the time goes:
time: 253 us; the launch traced here: 252 us
  waiting for transfers between devices  102 us (40%)
  Pallas kernels  83.9 us (33%)
  starting transfers between devices  59.4 us (23%)
  local copies, waits for them, and re-layouts  4.49 us (2%)
    ppermute x41, waiting for transfers between devices, flip(): return lax.ppermute(value, axis, [(i, i ^ bit) for i in range(size)])  80.5 us
    pallas_call x21, Pallas kernels, call(): pl.pallas_call(kernel, name=name, out_shape=shapes, in_specs=[SMEM if at...  49.6 us
    ppermute x41, starting transfers between devices, flip(): return lax.ppermute(value, axis, [(i, i ^ bit) for i in range(size)])  40.4 us
    all_to_all x4, waiting for transfers between devices, exchange(): lax.all_to_all(value, ('exp', 'head'), split_axis=0, concat_axis=0, tiled...  21.6 us
    all_to_all x4, starting transfers between devices, exchange(): lax.all_to_all(value, ('exp', 'head'), split_axis=0, concat_axis=0, tiled...  19 us
    pallas_call x1, Pallas kernels, expert(): pl.pallas_call(expert_kernel, name='expert', grid=(units // tile,), out_s...  16.6 us
    pallas_call x1, Pallas kernels, expert_grads(): pl.pallas_call(expert_grad_kernel, name='expert_grads', grid=(units // ti...  11.6 us
  transfers between devices with their start and end apart: 45, of which 26 were waited for; matrix products, arithmetic and copies ran while one was open for 1% of the time, Pallas kernels for 23%

commit v1 on v0

--- a/solution.py
+++ b/solution.py
@@ -263,12 +263,9 @@
     dpre_ref,
     dh2_kept_ref,
     dh2_sent_ref,
-    branch_kept_ref,
-    branch_sent_ref,
     rows_ref,
     grads_ref,
     dh2_ref,
-    branch_ref,
 ):
     count = h2_ref.shape[0]
 
@@ -279,7 +276,6 @@
         grads_ref[:count] = up_ref[...]
         grads_ref[count:] = up_other_ref[...]
         dh2_ref[...] = jnp.zeros_like(dh2_ref)
-        branch_ref[...] = jnp.zeros_like(branch_ref)
 
     w_up, w_down = w_up_ref[...], w_down_ref[...]
     pre = dot(rows_ref[...], w_up)
@@ -289,14 +285,11 @@
     dpre = (dot_nt(grads_ref[...], w_down) * slope).astype(BF16)
     dpre_ref[...] = dpre
     dh2_ref[...] += dot_nt(dpre, w_up)
-    branch_ref[...] += dot(hidden, w_down)
 
     @pl.when(pl.program_id(0) == pl.num_programs(0) - 1)
     def _():
         dh2_kept_ref[...] = dh2_ref[:count]
         dh2_sent_ref[...] = dh2_ref[count:].astype(BF16)
-        branch_kept_ref[...] = branch_ref[:count].astype(BF16)
-        branch_sent_ref[...] = branch_ref[count:].astype(BF16)
 
 
 def store_sums(sums_ref, upstream, normed):
@@ -309,15 +302,28 @@
 
 
 def norm2_back_kernel(
-    kept_ref, came_ref, resid_ref, grad_ref, gain_ref, dresid_ref, packed_ref, sums_ref, *, cap
+    kept_ref,
+    came_ref,
+    resid_ref,
+    grad_ref,
+    gain_ref,
+    dresid_far,
+    packed_ref,
+    sums_ref,
+    dresid_ref,
+    sem,
+    *,
+    cap,
 ):
     dh2 = kept_ref[...] + came_ref[...].astype(F32)
     normed, inverse = normalise(resid_ref[...])
     dresid = grad_ref[...].astype(F32) + norm_back(dh2, normed, inverse, gain_ref[...])
     dresid_ref[...] = dresid
+    leaving = started(dresid_ref, dresid_far, sem)
     slot_of = lax.broadcasted_iota(jnp.int32, (1, dh2.shape[0]), 1)
     pack(packed_ref, dresid.astype(BF16), slot_of, cap, False)
     store_sums(sums_ref, dh2, normed)
+    leaving.wait()
 
 
 def out_grad_kernel(where_ref, own_ref, other_ref, context_far, dattn_ref, *rest):
@@ -645,6 +651,20 @@
     down_ref[...] = dot_tn(hidden_ref[...], grads_ref[...])
 
 
+def branch_kernel(hidden_ref, w_down_ref, kept_ref, sent_ref, branch_ref):
+    @pl.when(pl.program_id(0) == 0)
+    def _():
+        branch_ref[...] = jnp.zeros_like(branch_ref)
+
+    branch_ref[...] += dot(hidden_ref[...], w_down_ref[...])
+
+    @pl.when(pl.program_id(0) == pl.num_programs(0) - 1)
+    def _():
+        count = kept_ref.shape[0]
+        kept_ref[...] = branch_ref[:count].astype(BF16)
+        sent_ref[...] = branch_ref[count:].astype(BF16)
+
+
 def norm1_back_kernel(packed_ref, x_ref, dresid_ref, gain_ref, out_ref, sums_ref, *, cap):
     count, width = x_ref.shape
     dh1 = unpack(packed_ref, slots_down(count), cap, width)
@@ -701,8 +721,6 @@
         ((2 * count, units), BF16),
         ((2 * count, units), BF16),
         ((count, width), F32),
-        ((count, width), BF16),
-        ((count, width), BF16),
         ((count, width), BF16),
         ((2 * count, width), BF16),
         ((2 * count, width), BF16),
@@ -724,13 +742,12 @@
             pl.BlockSpec((width, tile), lambda j: (0, j)),
             pl.BlockSpec((tile, width), lambda j: (j, 0)),
         ],
-        out_specs=[by_unit, by_unit, rows, rows, rows, rows, both, both],
+        out_specs=[by_unit, by_unit, rows, rows, both, both],
         scratch_shapes=[
             pltpu.VMEM((2 * count, width), F32),
-            pltpu.VMEM((2 * count, width), F32),
         ],
         cost_estimate=pl.CostEstimate(
-            flops=16 * count * width * units, bytes_accessed=16 * MIB, transcendentals=0
+            flops=12 * count * width * units, bytes_accessed=16 * MIB, transcendentals=0
         ),
         compiler_params=pltpu.CompilerParams(vmem_limit_bytes=40 * MIB),
     )(h2, h2_other, upstream, upstream_other, far(w_up), far(w_down))
@@ -760,6 +777,29 @@
     )(far(rows), far(grads), far(hidden), far(dpre))
 
 
+def expert_branch(hidden, w_down):
+    count, units = hidden.shape
+    width = w_down.shape[1]
+    tile = min(512, units)
+    half = pl.BlockSpec((count // 2, width), lambda j: (0, 0))
+    return pl.pallas_call(
+        branch_kernel,
+        name="expert_branch",
+        grid=(units // tile,),
+        out_shape=[pltpu.HBM((count // 2, width), BF16)] * 2,
+        in_specs=[
+            pl.BlockSpec((count, tile), lambda j: (0, j)),
+            pl.BlockSpec((tile, width), lambda j: (j, 0)),
+        ],
+        out_specs=[half, half],
+        scratch_shapes=[pltpu.VMEM((count, width), F32)],
+        cost_estimate=pl.CostEstimate(
+            flops=2 * count * width * units, bytes_accessed=8 * MIB, transcendentals=0
+        ),
+        compiler_params=pltpu.CompilerParams(vmem_limit_bytes=20 * MIB),
+    )(far(hidden), far(w_down))
+
+
 def flip(value, axis, bit):
     size = lax.axis_size(axis)
     return lax.ppermute(value, axis, [(i, i ^ bit) for i in range(size)])
@@ -776,7 +816,7 @@
     return list(lax.optimization_barrier((*values, *others))[: len(values)])
 
 
-def sum_and_spread(first, second, where, digits, sums, extra, finish):
+def sum_and_spread(first, second, where, digits, sums, extra, finish, first_wait):
     bits = 2 * (digits - 1)
 
     def across(value, bit):
@@ -821,7 +861,7 @@
         halves = yield sent[0], [flip(sent[0], "exp", 1), flip(sent[1], "exp", 2)]
         yield None, [total, by_x, by_y, *halves]
 
-    lines, states, last = [steps(first, None, 0), None], [None, None], None
+    lines, states, last = [steps(first, None, 0), None], [None, None], first_wait
     states[0] = next(lines[0])
     for at, line in enumerate([0] + [0, 1] * (2 * bits + 1) + [1]):
         if at == 1:
@@ -923,10 +963,7 @@
         [attn_kept, cross(attn_sent), along], moving,
     )
     attn_back = exchange(sent)
-    near_own = after(own_copy, sent)
-    by_x, by_y = flip(near_own, "exp", 1), flip(near_own, "exp", 2)
     by_xy = flip(after(own_copy, attn_back), "exp", 3)
-    attn_back = after(attn_back, by_x, by_y)
     resid, h2, upstream, valid = call(
         functools.partial(norm2_kernel, cap=cap),
         "norm2",
@@ -935,7 +972,7 @@
         moving,
     )
     h2_other, upstream_other = cross(h2), cross(upstream)
-    hidden, dpre, dh2_kept, dh2_sent, branch_kept, branch_sent, rows_all, grads_all = expert(
+    hidden, dpre, dh2_kept, dh2_sent, rows_all, grads_all = expert(
         h2, h2_other, upstream, upstream_other, w_up[0], w_down[0]
     )
     dh2_sent = after(dh2_sent, by_xy)
@@ -945,17 +982,19 @@
         [((slots, width), F32), packed, ((width // 64, 128), F32)],
         [dh2_kept, cross(dh2_sent), resid, grad_output, gain2],
         moving,
+        out_raw=(0,),
+        scratch=[pltpu.VMEM((slots, width), F32), pltpu.SemaphoreType.DMA],
     )
     arrived = exchange(sent)
-    plane_own = [after(rows, sent) for rows in (by_x, by_y, by_xy)]
-    plane_other = [cross(rows) for rows in plane_own]
-    hidden = after(hidden, sent)
+    near_own, hidden, far_own = after_all([own_copy, hidden, by_xy], sent)
+    by_x, by_y = flip(near_own, "exp", 1), flip(near_own, "exp", 2)
+    far_other = cross(far_own)
     grad_up, grad_down = expert_grads(rows_all, grads_all, hidden, dpre)
-    arrived, grad_up, grad_down, *plane_other = lax.optimization_barrier(
-        (arrived, grad_up, grad_down, *plane_other)
-    )
-    branch = branch_kept.astype(F32) + cross(branch_sent).astype(F32)
-    result = (resid + valid[:, :1] * branch).astype(BF16)
+    arrived, grad_up, grad_down, by_x, by_y, far_other = lax.optimization_barrier(
+        (arrived, grad_up, grad_down, by_x, by_y, far_other)
+    )
+    plane_own = [by_x, by_y, far_own]
+    plane_other = [cross(by_x), cross(by_y), far_other]
     (own,) = call(
         functools.partial(gather_kernel, cap=cap), "gather2", [((seq_rows, width), BF16)],
         [arrived, down], moving,
@@ -1007,7 +1046,7 @@
             pltpu.SemaphoreType.DMA((17,)),
         ],
     )
-    du_sent, *parts = after_all([du_sent, *parts], *out_parts[1:])
+    du_sent, *parts = after_all([du_sent, *parts], *out_parts[1:], *plane_other)
     value_parts = [parts[0], *to_others(parts[:4], 0)]
     key_query_parts = [parts[4], *to_others(after_all(parts[4:], *value_parts[1:]), 0)]
     (sent,) = call(
@@ -1032,6 +1071,10 @@
         product, scalars=1, scratch=[pltpu.VMEM((width, 128), F32)], away=(1, *range(5, 13)),
         out_away=(0,),
     )
+    branch_kept, branch_sent = expert_branch(after(hidden, out_value[1]), w_down[0])
+    branch_came = cross(branch_sent)
+    branch = branch_kept.astype(F32) + branch_came.astype(F32)
+    result = (resid + valid[:, :1] * branch).astype(BF16)
 
     def key_query(last):
         came = after_all(key_query_parts[1:], last)
@@ -1058,7 +1101,8 @@
         compiler_params=pltpu.CompilerParams(vmem_limit_bytes=40 * MIB),
     )
     (grad_qkv, grad_out), key_query = sum_and_spread(
-        out_value, key_query, where, digits, sums, extra, lambda parts: finish(where, *parts)
+        out_value, key_query, where, digits, sums, extra, lambda parts: finish(where, *parts),
+        branch_sent,
     )
     grad_qkv, sums = pl.pallas_call(
         functools.partial(finish_key_query_kernel, digits=digits, sums=extra),

time: 253 us -> 248 us (0.980)
  waiting for transfers between devices: 102 us -> 77.4 us
  blocking collectives: 0 us -> 21.2 us
  Pallas kernels: 83.9 us -> 86.6 us
    all_to_all x0 -> x1, blocking collectives: none -> 21.2 us  [exchange(): lax.all_to_all(value, ('exp', 'head'), split_axis=0, concat_axis=0, tiled...]
    ppermute x41, waiting for transfers between devices: 80.5 us -> 59.7 us  [flip(): return lax.ppermute(value, axis, [(i, i ^ bit) for i in range(size)])]
    pallas_call x0 -> x1, Pallas kernels: none -> 6.91 us  [expert_branch(): pl.pallas_call(branch_kernel, name='expert_branch', grid=(units // tile,)...]
    all_to_all x4 -> x3, waiting for transfers between devices: 21.6 us -> 17.8 us  [exchange(): lax.all_to_all(value, ('exp', 'head'), split_axis=0, concat_axis=0, tiled...]
    pallas_call x1, Pallas kernels: 16.6 us -> 13.1 us  [expert(): pl.pallas_call(expert_kernel, name='expert', grid=(units // tile,), out_s...]
    all_to_all x4 -> x3, starting transfers between devices: 19 us -> 15.8 us  [exchange(): lax.all_to_all(value, ('exp', 'head'), split_axis=0, concat_axis=0, tiled...]
  transfers between devices with their start and end apart: 45 -> 44, of which waited for: 26 -> 23; matrix products, arithmetic and copies ran while one was open for 1% -> 1% of each run, Pallas kernels for 23% -> 27%
where the time goes in v1:
time: 248 us
  Pallas kernels  86.6 us (35%)
  waiting for transfers between devices  77.4 us (31%)
  starting transfers between devices  57 us (23%)
  blocking collectives  21.2 us (9%)
  local copies, waits for them, and re-layouts  2.95 us (1%)
    ppermute x41, waiting for transfers between devices, flip(): return lax.ppermute(value, axis, [(i, i ^ bit) for i in range(size)])  59.7 us
    pallas_call x21, Pallas kernels, call(): pl.pallas_call(kernel, name=name, out_shape=shapes, in_specs=[SMEM if at...  49.1 us
    ppermute x41, starting transfers between devices, flip(): return lax.ppermute(value, axis, [(i, i ^ bit) for i in range(size)])  41.2 us
    all_to_all x1, blocking collectives, exchange(): lax.all_to_all(value, ('exp', 'head'), split_axis=0, concat_axis=0, tiled...  21.2 us
    all_to_all x3, waiting for transfers between devices, exchange(): lax.all_to_all(value, ('exp', 'head'), split_axis=0, concat_axis=0, tiled...  17.8 us
    all_to_all x3, starting transfers between devices, exchange(): lax.all_to_all(value, ('exp', 'head'), split_axis=0, concat_axis=0, tiled...  15.8 us
    pallas_call x1, Pallas kernels, expert(): pl.pallas_call(expert_kernel, name='expert', grid=(units // tile,), out_s...  13.1 us
    pallas_call x1, Pallas kernels, expert_grads(): pl.pallas_call(expert_grad_kernel, name='expert_grads', grid=(units // ti...  11.6 us
  transfers between devices with their start and end apart: 44, of which 23 were waited for; matrix products, arithmetic and copies ran while one was open for 1% of the time, Pallas kernels for 27%

profile of v1, /device:TPU:0, one launch (start us, length us, event | category | flops | bytes accessed | tf_op | source)
XLA Modules:
  0.0 247.5 jit_solution(17940929316385279462)
XLA Ops:
  0.7 3.3 %norm1.1 = bf16[256,1280]{1,0:T(8,128)(2,1)} custom-call(bf16[320,1024]{1,0:T(8,128)(2,1)} %x_ref.5, f32[1,1024]{1,0:T(1,128)} %bitcast.40, f32[1,1024]{1,0:T(1,128)} %bitcast.45), custom_call_target="tpu_custom_call" | custom-call | flops 503316480 | bytes 1318912 | tf_op jit(solution)/shard_map/norm1/pallas_call | solution.py:702
  4.0 7.3 %all-to-all-start = ((bf16[32,8,1280]{2,1,0:T(8,128)(2,1)}), bf16[32,8,1280]{2,1,0:T(8,128)(2,1)S(1)}, u32[]{:S(2)}, u32[]{:S(2)}) async-start(bf16[32,8,1280]{2,1,0:T(8,128)(2,1)} %bitcast.5), calls=%async_computation | async-start | bytes 1310720 | tf_op jit(solution)/shard_map/all_to_all | solution.py:917
  11.5 17.8 %all-to-all-done = bf16[32,8,1280]{2,1,0:T(8,128)(2,1)S(1)} async-done(((bf16[32,8,1280]{2,1,0:T(8,128)(2,1)}), bf16[32,8,1280]{2,1,0:T(8,128)(2,1)S(1)}, u32[]{:S(2)}, u32[]{:S(2)}) %all-to-all-start) | async-done | bytes 655392 | tf_op jit(solution)/shard_map/all_to_all | solution.py:917
  30.1 1.8 collective-permute-done.other_ref
  31.8 8.2 %attend.1 = (bf16[256,1024]{1,0:T(8,128)(2,1)}, bf16[512,1024]{1,0:T(8,128)(2,1)}, bf16[3,512,512]{2,1,0:T(8,128)(2,1)}, bf16[512,512]{1,0:T(8,128)(2,1)}, f32[1...) custom-call(s32[3]{0:T(128)S(1)} %pad_add_fusion.where_ref, s32[1,5]{1,0:T(1,128)S(1)} %copy-done.5, ...), custom_call_target="tpu_custom_call" | custom-call | flops 4294967296 | bytes 10747936 | tf_op jit(solution)/shard_map/attend/pallas_call | solution.py:702
  40.2 1.8 collective-permute-done.1.came_ref
  42.7 21.2 %all_to_all.20 = bf16[32,8,1280]{2,1,0:T(8,128)(2,1)S(1)} all-to-all(bf16[32,8,1280]{2,1,0:T(8,128)(2,1)S(1)} %bitcast.31), channel_id=1, replica_groups=mesh['exp'=16,'head'=2] {'exp','head'}, dimensions={0} | all-to-all | bytes 1310720 | tf_op jit(solution)/shard_map/all_to_all | solution.py:917
  63.9 1.2 norm2.1
  65.7 2.3 collective-permute-start.4
  68.2 13.1 %expert.1 = (bf16[640,2048]{1,0:T(8,128)(2,1)}, bf16[640,2048]{1,0:T(8,128)(2,1)}, f32[320,1024]{1,0:T(8,128)S(1)}, bf16[320,1024]{1,0:T(8,128)(2,1)S(1)}, bf16[...) custom-call(bf16[320,1024]{1,0:T(8,128)(2,1)S(1)} %get-tuple-element.112.h2_ref, ...), custom_call_target="tpu_custom_call" | custom-call | flops 8053063680 | bytes 16777216 | tf_op jit(solution)/shard_map/expert/pallas_call | solution.py:732
  81.5 2.0 collective-permute-done.5.came_ref
  83.5 3.1 %norm2_back.1 = (f32[320,1024]{1,0:T(8,128)}, bf16[256,1280]{1,0:T(8,128)(2,1)}, f32[16,128]{1,0:T(8,128)S(1)}) custom-call(f32[320,1024]{1,0:T(8,128)S(1)} %get-tuple-element.116.kept_ref, bf16[320,1024]{1,0:T(8,128)(2,1)S(1)} %collective-permute-done.5.came_ref, f32[320,1024]{1,0:T(8,128)S(1)} %get-tuple-element.109.resid_ref, ...), custom_call_target="tpu_custom_call" | custom-call | flops 503316480 | bytes 5910528 | tf_op jit(solution)/shard_map/norm2_back/pallas_call | solution.py:702
  86.6 3.7 %all-to-all-start.2 = ((bf16[32,8,1280]{2,1,0:T(8,128)(2,1)}), bf16[32,8,1280]{2,1,0:T(8,128)(2,1)S(1)}, u32[]{:S(2)}, u32[]{:S(2)}) async-start(bf16[32,8,1280]{2,1,0:T(8,128)(2,1)} %bitcast.15), calls=%async_computation.2 | async-start | bytes 1310720 | tf_op jit(solution)/shard_map/all_to_all | solution.py:917
  90.4 1.6 collective-permute-start.7
  92.0 1.5 collective-permute-start.6
  93.4 11.6 %expert_grads.1 = (f32[1024,2048]{1,0:T(8,128)}, f32[2048,1024]{1,0:T(8,128)}) custom-call(bf16[640,1024]{1,0:T(8,128)(2,1)} %get-tuple-element.121.rows_ref, bf16[640,1024]{1,0:T(8,128)(2,1)} %get-tuple-element.122.grads_ref, bf16[640,2048]{1,0:T(8,128)(2,1)} %get-tuple-element.155.hidden_ref, bf16[640,2048]{1,0:T(8,128)(2,1)} %get-tuple-element.123.dpre_ref), custom_call_target="tpu_custom_call" | custom-call | flops 5368709120 | bytes 25165824 | tf_op jit(solution)/shard_map/expert_grads/pallas_call | solution.py:762
  105.0 6.2 %collective-permute-done.7.refs_6_ = bf16[256,1024]{1,0:T(8,128)(2,1)S(1)} collective-permute-done((bf16[256,1024]{1,0:T(8,128)(2,1)S(1)}, bf16[256,1024]{1,0:T(8,128)(2,1)S(1)}, u32[]{:S(2)}, u32[]{:S(2)}) %collective-permute-start.7) | collective-permute-done | bytes 524320 | tf_op jit(solution)/shard_map/ppermute | solution.py:805
  111.3 0.8 copy-done.7
  114.4 1.1 collective-permute-done.9.other_ref
  115.5 3.4 %out_grad.1 = (bf16[512,1024]{1,0:T(8,128)(2,1)S(1)}, bf16[4,256,128]{2,1,0:T(8,128)(2,1)}, bf16[4,256,128]{2,1,0:T(8,128)(2,1)}, bf16[4,256,128]{2,1,0:T(8,128)(2,1)}, bf16[4,256,128]{2,1,0:T(8,128)(2,1)}) custom-call(s32[3]{0:T(128)S(1)} %pad_add_fusion.where_ref, bf16[256,1024]{1,0:T(8,128)(2,1)S(1)} %gather2.1.own_ref, ...), custom_call_target="tpu_custom_call" | custom-call | flops 536870912 | bytes 3670028 | tf_op jit(solution)/shard_map/out_grad/pallas_call | solution.py:702
  118.9 1.5 collective-permute-start.10
  120.8 1.7 collective-permute-start.12
  122.4 8.9 %attend_back.1 = (f32[256,1024]{1,0:T(8,128)S(1)}, bf16[256,1024]{1,0:T(8,128)(2,1)S(1)}, bf16[512,128]{1,0:T(8,128)(2,1)}, bf16[512,128]{1,0:T(8,128)(2,1)}, bf...) custom-call(s32[3]{0:T(128)S(1)} %pad_add_fusion.where_ref, ...), custom_call_target="tpu_custom_call" | custom-call | flops 7516192768 | bytes 10747936 | tf_op jit(solution)/shard_map/attend_back/pallas_call | solution.py:702
  131.4 2.9 %collective-permute-done.11.refs_13_ = bf16[4,256,128]{2,1,0:T(8,128)(2,1)S(1)} collective-permute-done((bf16[4,256,128]{2,1,0:T(8,128)(2,1)}, bf16[4,256,128]{2,1,0:T(8,128)(2,1)S(1)}, u32[]{:S(2)}, u32[]{:S(2)}) %collective-permute-start.11) | collective-permute-done | bytes 262176 | tf_op jit(solution)/shard_map/ppermute | solution.py:805
  134.9 1.2 collective-permute-start.16
  136.1 1.8 collective-permute-start.17
  137.8 1.4 scatter2.1
  139.3 1.6 collective-permute-done.15.refs_1_
  140.8 2.7 %collective-permute-done.16.refs_2_ = bf16[512,128]{1,0:T(8,128)(2,1)S(1)} collective-permute-done((bf16[512,128]{1,0:T(8,128)(2,1)}, bf16[512,128]{1,0:T(8,128)(2,1)S(1)}, u32[]{:S(2)}, u32[]{:S(2)}) %collective-permute-start.16) | collective-permute-done | bytes 131104 | tf_op jit(solution)/shard_map/ppermute | solution.py:805
  143.5 4.8 %all-to-all-start.3 = ((bf16[32,8,1280]{2,1,0:T(8,128)(2,1)}), bf16[32,8,1280]{2,1,0:T(8,128)(2,1)S(1)}, u32[]{:S(2)}, u32[]{:S(2)}) async-start(bf16[32,8,1280]{2,1,0:T(8,128)(2,1)} %bitcast.17), calls=%async_computation.3 | async-start | bytes 1310720 | tf_op jit(solution)/shard_map/all_to_all | solution.py:917
  148.4 4.0 %value_grad.1 = (bf16[2,512,128]{2,1,0:T(8,128)(2,1)}, bf16[2,512,128]{2,1,0:T(8,128)(2,1)S(1)}) custom-call(s32[3]{0:T(128)S(1)} %pad_add_fusion.where_ref, bf16[512,128]{1,0:T(8,128)(2,1)} %get-tuple-element.148.refs_0_, bf16[512,128]{1,0:T(8,128)(2,1)S(1)} %collective-permute-done.15.refs_1_, bf16[512,128]{1,0:T(8,128)(2,1)S(1)} %collective-permute-done.16.refs_2_, ...), custom_call_target="tpu_custom_call" | custom-call | flops 536870912 | bytes 6291468 | tf_op jit(solution)/shard_map/value_grad/pallas_call | solution.py:702
  152.4 1.5 collective-permute-start.23
  153.9 1.5 collective-permute-start.20
  155.4 1.5 collective-permute-start.21
  157.4 6.9 %expert_branch.1 = (bf16[320,1024]{1,0:T(8,128)(2,1)}, bf16[320,1024]{1,0:T(8,128)(2,1)}) custom-call(bf16[640,2048]{1,0:T(8,128)(2,1)} %get-tuple-element.155.hidden_ref, bf16[2048,1024]{1,0:T(8,128)(2,1)} %bitcast.44), custom_call_target="tpu_custom_call" | custom-call | flops 2684354560 | bytes 8388608 | tf_op jit(solution)/shard_map/expert_branch/pallas_call | solution.py:785
  164.3 2.8 %collective-permute-done.23.came_ref = bf16[2,512,128]{2,1,0:T(8,128)(2,1)S(1)} collective-permute-done((bf16[2,512,128]{2,1,0:T(8,128)(2,1)S(1)}, bf16[2,512,128]{2,1,0:T(8,128)(2,1)S(1)}, u32[]{:S(2)}, u32[]{:S(2)}) %collective-permute-start.23) | collective-permute-done | bytes 262176 | tf_op jit(solution)/shard_map/ppermute | solution.py:805
  167.1 1.7 add.17
  168.8 2.4 collective-permute-start.25
  171.6 4.4 %key_query_grad.1 = (bf16[2,512,128]{2,1,0:T(8,128)(2,1)}, bf16[2,512,128]{2,1,0:T(8,128)(2,1)S(1)}) custom-call(s32[3]{0:T(128)S(1)} %pad_add_fusion.where_ref, bf16[2,512,128]{2,1,0:T(8,128)(2,1)} %get-tuple-element.163.refs_0_, bf16[2,512,128]{2,1,0:T(8,128)(2,1)S(1)} %collective-permute-done.20.refs_1_, ...), custom_call_target="tpu_custom_call" | custom-call | flops 1073741824 | bytes 5767180 | tf_op jit(solution)/shard_map/key_query_grad/pallas_call | solution.py:702
  176.0 1.1 collective-permute-start.24
  177.3 0.9 last_add.1.own_ref
  178.2 1.8 collective-permute-start.27
  180.0 5.7 %collective-permute-done.24.came_ref = bf16[2,512,128]{2,1,0:T(8,128)(2,1)S(1)} collective-permute-done((bf16[2,512,128]{2,1,0:T(8,128)(2,1)S(1)}, bf16[2,512,128]{2,1,0:T(8,128)(2,1)S(1)}, u32[]{:S(2)}, u32[]{:S(2)}) %collective-permute-start.24) | collective-permute-done | bytes 262176 | tf_op jit(solution)/shard_map/ppermute | solution.py:805
  185.7 1.6 add.18
  187.3 1.2 collective-permute-start.31
  188.5 2.1 collective-permute-start.26
  190.6 3.9 %norm1_back.1 = (f32[320,1024]{1,0:T(8,128)}, f32[16,128]{1,0:T(8,128)S(1)}) custom-call(bf16[256,1280]{1,0:T(8,128)(2,1)S(1)} %bitcast.29, bf16[320,1024]{1,0:T(8,128)(2,1)} %x_ref.5, f32[320,1024]{1,0:T(8,128)} %get-tuple-element.161.dresid_ref, f32[1,1024]{1,0:T(1,128)} %bitcast.41), custom_call_target="tpu_custom_call" | custom-call | flops 503316480 | bytes 3944448 | tf_op jit(solution)/shard_map/norm1_back/pallas_call | solution.py:702
  195.8 0.9 last_add_sums.1.own_ref
  196.8 1.0 collective-permute-start.34
  197.8 3.4 %collective-permute-start.33 = (bf16[2048,128]{1,0:T(8,128)(2,1)S(1)}, bf16[2048,128]{1,0:T(8,128)(2,1)S(1)}, u32[]{:S(2)}, u32[]{:S(2)}) collective-permute-start(bf16[2048,128]{1,0:T(8,128)(2,1)S(1)} %stack.21.refs_0_), channel_id=1, source_target_pairs={{0,2},{2,0},{4,6},{6,4},{8,10},{10,8},{12,14},{14,12},{16,18},{18,... | collective-permute-start | bytes 1572872 | tf_op jit(solution)/shard_map/ppermute | solution.py:805
  201.2 2.2 collective-permute-start.30
  203.3 6.2 %collective-permute-done.30.came_ref = bf16[576,128]{1,0:T(8,128)(2,1)S(1)} collective-permute-done((bf16[576,128]{1,0:T(8,128)(2,1)S(1)}, bf16[576,128]{1,0:T(8,128)(2,1)S(1)}, u32[]{:S(2)}, u32[]{:S(2)}) %collective-permute-start.30) | collective-permute-done | bytes 147488 | tf_op jit(solution)/shard_map/ppermute | solution.py:805
  209.7 1.3 collective-permute-done.34.refs_2_
  211.1 0.9 collective-permute-done.33.refs_1_
  212.0 4.2 %collective-permute-done.32.came_ref = bf16[1088,128]{1,0:T(8,128)(2,1)S(1)} collective-permute-done((bf16[1088,128]{1,0:T(8,128)(2,1)S(1)}, bf16[1088,128]{1,0:T(8,128)(2,1)S(1)}, u32[]{:S(2)}, u32[]{:S(2)}) %collective-permute-start.32) | collective-permute-done | bytes 278560 | tf_op jit(solution)/shard_map/ppermute | solution.py:805
  216.7 1.5 collective-permute-start.35
  218.7 1.7 collective-permute-start.37
  220.6 10.8 %collective-permute-done.38.refs_4_ = bf16[1024,128]{1,0:T(8,128)(2,1)S(1)} collective-permute-done((bf16[1024,128]{1,0:T(8,128)(2,1)S(1)}, bf16[1024,128]{1,0:T(8,128)(2,1)S(1)}, u32[]{:S(2)}, u32[]{:S(2)}) %collective-permute-start.38) | collective-permute-done | bytes 262176 | tf_op jit(solution)/shard_map/ppermute | solution.py:805
  231.4 2.5 %collective-permute-done.37.refs_3_ = bf16[1024,128]{1,0:T(8,128)(2,1)S(1)} collective-permute-done((bf16[1024,128]{1,0:T(8,128)(2,1)S(1)}, bf16[1024,128]{1,0:T(8,128)(2,1)S(1)}, u32[]{:S(2)}, u32[]{:S(2)}) %collective-permute-start.37) | collective-permute-done | bytes 262176 | tf_op jit(solution)/shard_map/ppermute | solution.py:805
  233.9 2.9 %finish_out_value.1 = (f32[3,1024,512]{2,1,0:T(8,128)}, f32[512,1024]{1,0:T(8,128)}) custom-call(s32[3]{0:T(128)S(1)} %pad_add_fusion.where_ref, bf16[2048,128]{1,0:T(8,128)(2,1)S(1)} %stack.21.refs_0_, bf16[2048,128]{1,0:T(8,128)(2,1)S(1)} %collective-permute-done.33.refs_1_, bf16[2048,128]{1,0:T(8,128)(2,1)S(1)} %collective-permute-done.34.refs_2_, ...), custom_call_target="tpu_custom_call" | custom-call | bytes 6291456 | tf_op jit(solution)/shard_map/finish_out_value/pallas_call | solution.py:1104
  237.3 1.7 collective-permute-start.39
  239.1 1.1 add_convert_fusion
  240.2 3.2 %collective-permute-done.40.refs_4_ = bf16[1056,128]{1,0:T(8,128)(2,1)S(1)} collective-permute-done((bf16[1056,128]{1,0:T(8,128)(2,1)S(1)}, bf16[1056,128]{1,0:T(8,128)(2,1)S(1)}, u32[]{:S(2)}, u32[]{:S(2)}) %collective-permute-start.40) | collective-permute-done | bytes 270368 | tf_op jit(solution)/shard_map/ppermute | solution.py:805
  243.8 3.1 %finish_key_query.1 = (f32[3,1024,512]{2,1,0:T(8,128)}, f32[32,128]{1,0:T(8,128)S(1)}) custom-call(s32[3]{0:T(128)S(1)} %pad_add_fusion.where_ref, bf16[2112,128]{1,0:T(8,128)(2,1)S(1)} %stack.23.refs_0_, bf16[2112,128]{1,0:T(8,128)(2,1)S(1)} %collective-permute-done.35.refs_1_, ...), custom_call_target="tpu_custom_call", output_to_operand_aliasing={{0}: (6, {})} | custom-call | bytes 6291456 | tf_op jit(solution)/shard_map/finish_key_query/pallas_call | solution.py:1107
  (98 shorter events, 11.5 us)
Async XLA Ops:
  0.6 10.7 %copy-start.3 = (s32[256]{0:T(256)S(1)}, s32[256]{0:T(256)}, u32[]{:S(2)}) copy-start(s32[256]{0:T(256)} %param.13) | copy-start | bytes 3076
  4.0 25.2 %all-to-all-start = ((bf16[32,8,1280]{2,1,0:T(8,128)(2,1)}), bf16[32,8,1280]{2,1,0:T(8,128)(2,1)S(1)}, u32[]{:S(2)}, u32[]{:S(2)}) async-start(bf16[32,8,1280]{2,1,0:T(8,128)(2,1)} %bitcast.5), calls=%async_computation | async-start | bytes 1310720 | tf_op jit(solution)/shard_map/all_to_all | solution.py:917
  11.3 20.5 %copy-start.5 = (s32[1,5]{1,0:T(1,128)S(1)}, s32[1,5]{1,0:T(1,128)}, u32[]{:S(2)}) copy-start(s32[1,5]{1,0:T(1,128)} %lengths_ref.3) | copy-start | bytes 64
  29.8 2.0 collective-permute-start
  40.0 2.0 collective-permute-start.1
  42.0 21.9 %copy-start = (bf16[320,1024]{1,0:T(8,128)(2,1)S(1)}, bf16[320,1024]{1,0:T(8,128)(2,1)}, u32[]{:S(2)}) copy-start(bf16[320,1024]{1,0:T(8,128)(2,1)} %x_ref.5) | copy-start | bytes 1966084
  42.0 21.9 %copy-start.1 = (bf16[320,1024]{1,0:T(8,128)(2,1)S(1)}, bf16[320,1024]{1,0:T(8,128)(2,1)}, u32[]{:S(2)}) copy-start(bf16[320,1024]{1,0:T(8,128)(2,1)} %grad_ref.3) | copy-start | bytes 1966084
  42.0 21.9 %copy-start.2 = (f32[1024]{0:T(1024)S(1)}, f32[1024]{0:T(1024)}, u32[]{:S(2)}) copy-start(f32[1024]{0:T(1024)} %param.17) | copy-start | bytes 12292
  42.0 21.9 %copy-start.4 = (f32[1024]{0:T(1024)S(1)}, f32[1024]{0:T(1024)}, u32[]{:S(2)}) copy-start(f32[1024]{0:T(1024)} %param.18) | copy-start | bytes 12292
  63.9 1.8 copy-start.15
  65.1 2.9 %collective-permute-start.2 = (bf16[320,1024]{1,0:T(8,128)(2,1)S(1)}, bf16[320,1024]{1,0:T(8,128)(2,1)S(1)}, u32[]{:S(2)}, u32[]{:S(2)}) collective-permute-start(bf16[320,1024]{1,0:T(8,128)(2,1)S(1)} %get-tuple-element.112.h2_ref), channel_id=1, source_target_pairs={{0,1},{1,0},{2,3},{3,2},{4,5},{5,4},{6,7},{7,6},{8,9},{9,8},{10,11... | collective-permute-start | bytes 1966088 | tf_op jit(solution)/shard_map/ppermute | solution.py:805
  65.3 3.0 %collective-permute-start.3 = (bf16[320,1024]{1,0:T(8,128)(2,1)S(1)}, bf16[320,1024]{1,0:T(8,128)(2,1)S(1)}, u32[]{:S(2)}, u32[]{:S(2)}) collective-permute-start(bf16[320,1024]{1,0:T(8,128)(2,1)S(1)} %get-tuple-element.113.up_ref), channel_id=1, source_target_pairs={{0,1},{1,0},{2,3},{3,2},{4,5},{5,4},{6,7},{7,6},{8,9},{9,8},{10,11... | collective-permute-start | bytes 1966088 | tf_op jit(solution)/shard_map/ppermute | solution.py:805
  65.7 15.6 %collective-permute-start.4 = (bf16[256,1024]{1,0:T(8,128)(2,1)S(1)}, bf16[256,1024]{1,0:T(8,128)(2,1)S(1)}, u32[]{:S(2)}, u32[]{:S(2)}) collective-permute-start(bf16[256,1024]{1,0:T(8,128)(2,1)S(1)} %copy-done.15), channel_id=1, source_target_pairs={{0,6},{2,4},{4,2},{6,0},{8,14},{10,12},{12,10},{14,8},{16,22},{18,... | collective-permute-start | bytes 1572872 | tf_op jit(solution)/shard_map/ppermute | solution.py:805
  81.3 12.2 %copy-start.6 = (bf16[256,1024]{1,0:T(8,128)(2,1)}, bf16[256,1024]{1,0:T(8,128)(2,1)S(1)}, u32[]{:S(2)}) copy-start(bf16[256,1024]{1,0:T(8,128)(2,1)S(1)} %collective-permute-done.4.refs_7_) | copy-start | bytes 1572868
  81.3 2.2 collective-permute-start.5
  86.6 26.3 %all-to-all-start.2 = ((bf16[32,8,1280]{2,1,0:T(8,128)(2,1)}), bf16[32,8,1280]{2,1,0:T(8,128)(2,1)S(1)}, u32[]{:S(2)}, u32[]{:S(2)}) async-start(bf16[32,8,1280]{2,1,0:T(8,128)(2,1)} %bitcast.15), calls=%async_computation.2 | async-start | bytes 1310720 | tf_op jit(solution)/shard_map/all_to_all | solution.py:917
  90.4 20.9 %collective-permute-start.7 = (bf16[256,1024]{1,0:T(8,128)(2,1)S(1)}, bf16[256,1024]{1,0:T(8,128)(2,1)S(1)}, u32[]{:S(2)}, u32[]{:S(2)}) collective-permute-start(bf16[256,1024]{1,0:T(8,128)(2,1)S(1)} %copy-done.15), channel_id=1, source_target_pairs={{0,4},{2,6},{4,0},{6,2},{8,12},{10,14},{12,8},{14,10},{16,20},{18,... | collective-permute-start | bytes 1572872 | tf_op jit(solution)/shard_map/ppermute | solution.py:805
  92.0 19.3 %collective-permute-start.6 = (bf16[256,1024]{1,0:T(8,128)(2,1)S(1)}, bf16[256,1024]{1,0:T(8,128)(2,1)S(1)}, u32[]{:S(2)}, u32[]{:S(2)}) collective-permute-start(bf16[256,1024]{1,0:T(8,128)(2,1)S(1)} %copy-done.15), channel_id=1, source_target_pairs={{0,2},{2,0},{4,6},{6,4},{8,10},{10,8},{12,14},{14,12},{16,18},{18,... | collective-permute-start | bytes 1572872 | tf_op jit(solution)/shard_map/ppermute | solution.py:805
  93.4 19.4 %collective-permute-start.8 = (bf16[256,1024]{1,0:T(8,128)(2,1)S(1)}, bf16[256,1024]{1,0:T(8,128)(2,1)}, u32[]{:S(2)}, u32[]{:S(2)}) collective-permute-start(bf16[256,1024]{1,0:T(8,128)(2,1)S(1)} %collective-permute-done.4.refs_7_), channel_id=1, source_target_pairs={{0,1},{1,0},{2,3},{3,2},{4,5},{5,4},{6,7},{7,6},{8,9},{9,8},{10,11... | collective-permute-start | bytes 1572872 | tf_op jit(solution)/shard_map/ppermute | solution.py:805
  111.3 0.8 copy-start.7
  112.1 0.8 copy-start.9
  112.9 1.0 copy-start.10
  112.9 1.2 copy-start.8
  113.5 2.0 collective-permute-start.9
  113.9 17.4 %collective-permute-start.13 = (bf16[256,1024]{1,0:T(8,128)(2,1)S(1)}, bf16[256,1024]{1,0:T(8,128)(2,1)S(1)}, u32[]{:S(2)}, u32[]{:S(2)}) collective-permute-start(bf16[256,1024]{1,0:T(8,128)(2,1)S(1)} %copy-done.10), channel_id=1, source_target_pairs={{0,1},{1,0},{2,3},{3,2},{4,5},{5,4},{6,7},{7,6},{8,9},{9,8},{10,11... | collective-permute-start | bytes 1572872 | tf_op jit(solution)/shard_map/ppermute | solution.py:805
  114.1 17.3 %collective-permute-start.14 = (bf16[256,1024]{1,0:T(8,128)(2,1)S(1)}, bf16[256,1024]{1,0:T(8,128)(2,1)S(1)}, u32[]{:S(2)}, u32[]{:S(2)}) collective-permute-start(bf16[256,1024]{1,0:T(8,128)(2,1)S(1)} %copy-done.8), channel_id=1, source_target_pairs={{0,1},{1,0},{2,3},{3,2},{4,5},{5,4},{6,7},{7,6},{8,9},{9,8},{10,11... | collective-permute-start | bytes 1572872 | tf_op jit(solution)/shard_map/ppermute | solution.py:805
  118.9 12.5 %collective-permute-start.10 = (bf16[4,256,128]{2,1,0:T(8,128)(2,1)}, bf16[4,256,128]{2,1,0:T(8,128)(2,1)S(1)}, u32[]{:S(2)}, u32[]{:S(2)}) collective-permute-start(bf16[4,256,128]{2,1,0:T(8,128)(2,1)} %get-tuple-element.142), channel_id=1, source_target_pairs={{0,2},{2,0},{4,6},{6,4},{8,10},{10,8},{12,14},{14,12},{16,18},{18,... | collective-permute-start | bytes 786440 | tf_op jit(solution)/shard_map/ppermute | solution.py:805
  120.4 13.9 %collective-permute-start.11 = (bf16[4,256,128]{2,1,0:T(8,128)(2,1)}, bf16[4,256,128]{2,1,0:T(8,128)(2,1)S(1)}, u32[]{:S(2)}, u32[]{:S(2)}) collective-permute-start(bf16[4,256,128]{2,1,0:T(8,128)(2,1)} %get-tuple-element.143), channel_id=1, source_target_pairs={{0,4},{2,6},{4,0},{6,2},{8,12},{10,14},{12,8},{14,10},{16,20},{18,... | collective-permute-start | bytes 786440 | tf_op jit(solution)/shard_map/ppermute | solution.py:805
  120.8 13.5 %collective-permute-start.12 = (bf16[4,256,128]{2,1,0:T(8,128)(2,1)}, bf16[4,256,128]{2,1,0:T(8,128)(2,1)S(1)}, u32[]{:S(2)}, u32[]{:S(2)}) collective-permute-start(bf16[4,256,128]{2,1,0:T(8,128)(2,1)} %get-tuple-element.144), channel_id=1, source_target_pairs={{0,6},{2,4},{4,2},{6,0},{8,14},{10,12},{12,10},{14,8},{16,22},{18,... | collective-permute-start | bytes 786440 | tf_op jit(solution)/shard_map/ppermute | solution.py:805
  131.4 12.2 %copy-start.11 = (bf16[256,1024]{1,0:T(8,128)(2,1)}, bf16[256,1024]{1,0:T(8,128)(2,1)S(1)}, u32[]{:S(2)}) copy-start(bf16[256,1024]{1,0:T(8,128)(2,1)S(1)} %collective-permute-done.13.refs_8_) | copy-start | bytes 1572868
  131.4 12.1 %copy-start.12 = (bf16[256,1024]{1,0:T(8,128)(2,1)}, bf16[256,1024]{1,0:T(8,128)(2,1)S(1)}, u32[]{:S(2)}) copy-start(bf16[256,1024]{1,0:T(8,128)(2,1)S(1)} %collective-permute-done.14.refs_9_) | copy-start | bytes 1572868
  134.3 3.5 %collective-permute-start.19 = (bf16[256,1024]{1,0:T(8,128)(2,1)S(1)}, bf16[256,1024]{1,0:T(8,128)(2,1)S(1)}, u32[]{:S(2)}, u32[]{:S(2)}) collective-permute-start(bf16[256,1024]{1,0:T(8,128)(2,1)S(1)} %get-tuple-element.159), channel_id=1, source_target_pairs={{0,1},{1,0},{2,3},{3,2},{4,5},{5,4},{6,7},{7,6},{8,9},{9,8},{10,11... | collective-permute-start | bytes 1572872 | tf_op jit(solution)/shard_map/ppermute | solution.py:805
  134.3 6.5 %collective-permute-start.15 = (bf16[512,128]{1,0:T(8,128)(2,1)}, bf16[512,128]{1,0:T(8,128)(2,1)S(1)}, u32[]{:S(2)}, u32[]{:S(2)}) collective-permute-start(bf16[512,128]{1,0:T(8,128)(2,1)} %get-tuple-element.149), channel_id=1, source_target_pairs={{0,2},{2,0},{4,6},{6,4},{8,10},{10,8},{12,14},{14,12},{16,18},{18,... | collective-permute-start | bytes 393224 | tf_op jit(solution)/shard_map/ppermute | solution.py:805
  134.9 8.6 %collective-permute-start.16 = (bf16[512,128]{1,0:T(8,128)(2,1)}, bf16[512,128]{1,0:T(8,128)(2,1)S(1)}, u32[]{:S(2)}, u32[]{:S(2)}) collective-permute-start(bf16[512,128]{1,0:T(8,128)(2,1)} %get-tuple-element.150), channel_id=1, source_target_pairs={{0,4},{2,6},{4,0},{6,2},{8,12},{10,14},{12,8},{14,10},{16,20},{18,... | collective-permute-start | bytes 393224 | tf_op jit(solution)/shard_map/ppermute | solution.py:805
  136.1 7.5 %collective-permute-start.17 = (bf16[512,128]{1,0:T(8,128)(2,1)}, bf16[512,128]{1,0:T(8,128)(2,1)S(1)}, u32[]{:S(2)}, u32[]{:S(2)}) collective-permute-start(bf16[512,128]{1,0:T(8,128)(2,1)} %get-tuple-element.151), channel_id=1, source_target_pairs={{0,6},{2,4},{4,2},{6,0},{8,14},{10,12},{12,10},{14,8},{16,22},{18,... | collective-permute-start | bytes 393224 | tf_op jit(solution)/shard_map/ppermute | solution.py:805
  143.5 47.1 %all-to-all-start.3 = ((bf16[32,8,1280]{2,1,0:T(8,128)(2,1)}), bf16[32,8,1280]{2,1,0:T(8,128)(2,1)S(1)}, u32[]{:S(2)}, u32[]{:S(2)}) async-start(bf16[32,8,1280]{2,1,0:T(8,128)(2,1)} %bitcast.17), calls=%async_computation.3 | async-start | bytes 1310720 | tf_op jit(solution)/shard_map/all_to_all | solution.py:917
  148.4 5.5 %copy-start.18 = (bf16[2,512,128]{2,1,0:T(8,128)(2,1)S(1)}, bf16[2,512,128]{2,1,0:T(8,128)(2,1)}, u32[]{:S(2)}) copy-start(bf16[2,512,128]{2,1,0:T(8,128)(2,1)} %get-tuple-element.167) | copy-start | bytes 786436
  148.4 7.0 %copy-start.17 = (bf16[2,512,128]{2,1,0:T(8,128)(2,1)S(1)}, bf16[2,512,128]{2,1,0:T(8,128)(2,1)}, u32[]{:S(2)}) copy-start(bf16[2,512,128]{2,1,0:T(8,128)(2,1)} %get-tuple-element.168) | copy-start | bytes 786436
  148.4 8.5 %copy-start.16 = (bf16[2,512,128]{2,1,0:T(8,128)(2,1)S(1)}, bf16[2,512,128]{2,1,0:T(8,128)(2,1)}, u32[]{:S(2)}) copy-start(bf16[2,512,128]{2,1,0:T(8,128)(2,1)} %get-tuple-element.169) | copy-start | bytes 786436
  152.4 14.7 %collective-permute-start.23 = (bf16[2,512,128]{2,1,0:T(8,128)(2,1)S(1)}, bf16[2,512,128]{2,1,0:T(8,128)(2,1)S(1)}, u32[]{:S(2)}, u32[]{:S(2)}) collective-permute-start(bf16[2,512,128]{2,1,0:T(8,128)(2,1)S(1)} %get-tuple-element.154), channel_id=1, source_target_pairs={{0,8},{2,10},{4,12},{6,14},{8,0},{10,2},{12,4},{14,6},{16,24},{18,... | collective-permute-start | bytes 786440 | tf_op jit(solution)/shard_map/ppermute | solution.py:805
  153.9 17.3 %collective-permute-start.20 = (bf16[2,512,128]{2,1,0:T(8,128)(2,1)S(1)}, bf16[2,512,128]{2,1,0:T(8,128)(2,1)S(1)}, u32[]{:S(2)}, u32[]{:S(2)}) collective-permute-start(bf16[2,512,128]{2,1,0:T(8,128)(2,1)S(1)} %copy-done.18), channel_id=1, source_target_pairs={{0,2},{2,0},{4,6},{6,4},{8,10},{10,8},{12,14},{14,12},{16,18},{18,... | collective-permute-start | bytes 786440 | tf_op jit(solution)/shard_map/ppermute | solution.py:805
  155.4 16.3 %collective-permute-start.21 = (bf16[2,512,128]{2,1,0:T(8,128)(2,1)S(1)}, bf16[2,512,128]{2,1,0:T(8,128)(2,1)S(1)}, u32[]{:S(2)}, u32[]{:S(2)}) collective-permute-start(bf16[2,512,128]{2,1,0:T(8,128)(2,1)S(1)} %copy-done.17), channel_id=1, source_target_pairs={{0,4},{2,6},{4,0},{6,2},{8,12},{10,14},{12,8},{14,10},{16,20},{18,... | collective-permute-start | bytes 786440 | tf_op jit(solution)/shard_map/ppermute | solution.py:805
  156.8 14.8 %collective-permute-start.22 = (bf16[2,512,128]{2,1,0:T(8,128)(2,1)S(1)}, bf16[2,512,128]{2,1,0:T(8,128)(2,1)S(1)}, u32[]{:S(2)}, u32[]{:S(2)}) collective-permute-start(bf16[2,512,128]{2,1,0:T(8,128)(2,1)S(1)} %copy-done.16), channel_id=1, source_target_pairs={{0,6},{2,4},{4,2},{6,0},{8,14},{10,12},{12,10},{14,8},{16,22},{18,... | collective-permute-start | bytes 786440 | tf_op jit(solution)/shard_map/ppermute | solution.py:805
  168.8 8.5 %collective-permute-start.25 = (bf16[1,512,128]{2,1,0:T(8,128)(2,1)S(1)}, bf16[1,512,128]{2,1,0:T(8,128)(2,1)S(1)}, u32[]{:S(2)}, u32[]{:S(2)}) collective-permute-start(bf16[1,512,128]{2,1,0:T(8,128)(2,1)S(1)} %get-tuple-element.172), channel_id=1, source_target_pairs={{0,16},{2,18},{4,20},{6,22},{8,24},{10,26},{12,28},{14,30},{16,0},... | collective-permute-start | bytes 393224 | tf_op jit(solution)/shard_map/ppermute | solution.py:805
  176.0 9.6 %collective-permute-start.24 = (bf16[2,512,128]{2,1,0:T(8,128)(2,1)S(1)}, bf16[2,512,128]{2,1,0:T(8,128)(2,1)S(1)}, u32[]{:S(2)}, u32[]{:S(2)}) collective-permute-start(bf16[2,512,128]{2,1,0:T(8,128)(2,1)S(1)} %get-tuple-element.177), channel_id=1, source_target_pairs={{0,8},{2,10},{4,12},{6,14},{8,0},{10,2},{12,4},{14,6},{16,24},{18,... | collective-permute-start | bytes 786440 | tf_op jit(solution)/shard_map/ppermute | solution.py:805
  178.2 9.1 %collective-permute-start.27 = (bf16[512,128]{1,0:T(8,128)(2,1)S(1)}, bf16[512,128]{1,0:T(8,128)(2,1)S(1)}, u32[]{:S(2)}, u32[]{:S(2)}) collective-permute-start(bf16[512,128]{1,0:T(8,128)(2,1)S(1)} %last_add.1.own_ref), channel_id=1, source_target_pairs={{0,16},{2,18},{4,20},{6,22},{8,24},{10,26},{12,28},{14,30},{16,0},... | collective-permute-start | bytes 393224 | tf_op jit(solution)/shard_map/ppermute | solution.py:805
  187.3 9.5 %collective-permute-start.31 = (bf16[1024,128]{1,0:T(8,128)(2,1)S(1)}, bf16[1024,128]{1,0:T(8,128)(2,1)S(1)}, u32[]{:S(2)}, u32[]{:S(2)}) collective-permute-start(bf16[1024,128]{1,0:T(8,128)(2,1)S(1)} %stack.20.own_ref), channel_id=1, source_target_pairs={{0,8},{2,10},{4,12},{6,14},{8,0},{10,2},{12,4},{14,6},{16,24},{18,... | collective-permute-start | bytes 786440 | tf_op jit(solution)/shard_map/ppermute | solution.py:805
  188.5 6.5 %collective-permute-start.26 = (bf16[1,512,128]{2,1,0:T(8,128)(2,1)S(1)}, bf16[1,512,128]{2,1,0:T(8,128)(2,1)S(1)}, u32[]{:S(2)}, u32[]{:S(2)}) collective-permute-start(bf16[1,512,128]{2,1,0:T(8,128)(2,1)S(1)} %get-tuple-element.182), channel_id=1, source_target_pairs={{0,16},{2,18},{4,20},{6,22},{8,24},{10,26},{12,28},{14,30},{16,0},... | collective-permute-start | bytes 393224 | tf_op jit(solution)/shard_map/ppermute | solution.py:805
  190.6 4.4 %collective-permute-start.29 = (f32[16,128]{1,0:T(8,128)S(1)}, f32[16,128]{1,0:T(8,128)S(1)}, u32[]{:S(2)}, u32[]{:S(2)}) collective-permute-start(f32[16,128]{1,0:T(8,128)S(1)} %get-tuple-element.186.refs_2_), channel_id=1, source_target_pairs={{0,1},{1,0},{2,3},{3,2},{4,5},{5,4},{6,7},{7,6},{8,9},{9,8},{10,11... | collective-permute-start | bytes 24584 | tf_op jit(solution)/shard_map/ppermute | solution.py:805
  194.5 15.2 %copy-start.14 = (bf16[320,1024]{1,0:T(8,128)(2,1)S(1)}, bf16[320,1024]{1,0:T(8,128)(2,1)}, u32[]{:S(2)}) copy-start(bf16[320,1024]{1,0:T(8,128)(2,1)} %get-tuple-element.157) | copy-start | bytes 1966084
  194.5 1.3 collective-permute-start.28
  196.8 14.2 %collective-permute-start.34 = (bf16[2048,128]{1,0:T(8,128)(2,1)S(1)}, bf16[2048,128]{1,0:T(8,128)(2,1)S(1)}, u32[]{:S(2)}, u32[]{:S(2)}) collective-permute-start(bf16[2048,128]{1,0:T(8,128)(2,1)S(1)} %stack.21.refs_0_), channel_id=1, source_target_pairs={{0,4},{2,6},{4,0},{6,2},{8,12},{10,14},{12,8},{14,10},{16,20},{18,... | collective-permute-start | bytes 1572872 | tf_op jit(solution)/shard_map/ppermute | solution.py:805
  197.8 14.2 %collective-permute-start.33 = (bf16[2048,128]{1,0:T(8,128)(2,1)S(1)}, bf16[2048,128]{1,0:T(8,128)(2,1)S(1)}, u32[]{:S(2)}, u32[]{:S(2)}) collective-permute-start(bf16[2048,128]{1,0:T(8,128)(2,1)S(1)} %stack.21.refs_0_), channel_id=1, source_target_pairs={{0,2},{2,0},{4,6},{6,4},{8,10},{10,8},{12,14},{14,12},{16,18},{18,... | collective-permute-start | bytes 1572872 | tf_op jit(solution)/shard_map/ppermute | solution.py:805
  201.2 8.3 %collective-permute-start.30 = (bf16[576,128]{1,0:T(8,128)(2,1)S(1)}, bf16[576,128]{1,0:T(8,128)(2,1)S(1)}, u32[]{:S(2)}, u32[]{:S(2)}) collective-permute-start(bf16[576,128]{1,0:T(8,128)(2,1)S(1)} %last_add_sums.1.own_ref), channel_id=1, source_target_pairs={{0,16},{2,18},{4,20},{6,22},{8,24},{10,26},{12,28},{14,30},{16,0},... | collective-permute-start | bytes 442376 | tf_op jit(solution)/shard_map/ppermute | solution.py:805
  209.6 6.6 %collective-permute-start.32 = (bf16[1088,128]{1,0:T(8,128)(2,1)S(1)}, bf16[1088,128]{1,0:T(8,128)(2,1)S(1)}, u32[]{:S(2)}, u32[]{:S(2)}) collective-permute-start(bf16[1088,128]{1,0:T(8,128)(2,1)S(1)} %stack.22.own_ref), channel_id=1, source_target_pairs={{0,8},{2,10},{4,12},{6,14},{8,0},{10,2},{12,4},{14,6},{16,24},{18,... | collective-permute-start | bytes 835592 | tf_op jit(solution)/shard_map/ppermute | solution.py:805
  209.7 29.4 %collective-permute-start.18 = (bf16[320,1024]{1,0:T(8,128)(2,1)S(1)}, bf16[320,1024]{1,0:T(8,128)(2,1)S(1)}, u32[]{:S(2)}, u32[]{:S(2)}) collective-permute-start(bf16[320,1024]{1,0:T(8,128)(2,1)S(1)} %copy-done.14), channel_id=1, source_target_pairs={{0,1},{1,0},{2,3},{3,2},{4,5},{5,4},{6,7},{7,6},{8,9},{9,8},{10,11... | collective-permute-start | bytes 1966088 | tf_op jit(solution)/shard_map/ppermute | solution.py:805
  216.2 20.6 %collective-permute-start.36 = (bf16[2112,128]{1,0:T(8,128)(2,1)S(1)}, bf16[2112,128]{1,0:T(8,128)(2,1)S(1)}, u32[]{:S(2)}, u32[]{:S(2)}) collective-permute-start(bf16[2112,128]{1,0:T(8,128)(2,1)S(1)} %stack.23.refs_0_), channel_id=1, source_target_pairs={{0,4},{2,6},{4,0},{6,2},{8,12},{10,14},{12,8},{14,10},{16,20},{18,... | collective-permute-start | bytes 1622024 | tf_op jit(solution)/shard_map/ppermute | solution.py:805
  216.7 20.1 %collective-permute-start.35 = (bf16[2112,128]{1,0:T(8,128)(2,1)S(1)}, bf16[2112,128]{1,0:T(8,128)(2,1)S(1)}, u32[]{:S(2)}, u32[]{:S(2)}) collective-permute-start(bf16[2112,128]{1,0:T(8,128)(2,1)S(1)} %stack.23.refs_0_), channel_id=1, source_target_pairs={{0,2},{2,0},{4,6},{6,4},{8,10},{10,8},{12,14},{14,12},{16,18},{18,... | collective-permute-start | bytes 1622024 | tf_op jit(solution)/shard_map/ppermute | solution.py:805
  218.2 13.2 %collective-permute-start.38 = (bf16[1024,128]{1,0:T(8,128)(2,1)S(1)}, bf16[1024,128]{1,0:T(8,128)(2,1)S(1)}, u32[]{:S(2)}, u32[]{:S(2)}) collective-permute-start(bf16[1024,128]{1,0:T(8,128)(2,1)S(1)} %slice.33), channel_id=1, source_target_pairs={{0,4},{2,6},{4,0},{6,2},{8,12},{10,14},{12,8},{14,10},{16,20},{18,... | collective-permute-start | bytes 786440 | tf_op jit(solution)/shard_map/ppermute | solution.py:805
  218.7 15.2 %collective-permute-start.37 = (bf16[1024,128]{1,0:T(8,128)(2,1)S(1)}, bf16[1024,128]{1,0:T(8,128)(2,1)S(1)}, u32[]{:S(2)}, u32[]{:S(2)}) collective-permute-start(bf16[1024,128]{1,0:T(8,128)(2,1)S(1)} %slice.32), channel_id=1, source_target_pairs={{0,2},{2,0},{4,6},{6,4},{8,10},{10,8},{12,14},{14,12},{16,18},{18,... | collective-permute-start | bytes 786440 | tf_op jit(solution)/shard_map/ppermute | solution.py:805
  220.6 18.5 %copy-start.13 = (bf16[320,1024]{1,0:T(8,128)(2,1)S(1)}, bf16[320,1024]{1,0:T(8,128)(2,1)}, u32[]{:S(2)}) copy-start(bf16[320,1024]{1,0:T(8,128)(2,1)} %get-tuple-element.156) | copy-start | bytes 1966084
  236.9 6.5 %collective-permute-start.40 = (bf16[1056,128]{1,0:T(8,128)(2,1)S(1)}, bf16[1056,128]{1,0:T(8,128)(2,1)S(1)}, u32[]{:S(2)}, u32[]{:S(2)}) collective-permute-start(bf16[1056,128]{1,0:T(8,128)(2,1)S(1)} %slice.35), channel_id=1, source_target_pairs={{0,4},{2,6},{4,0},{6,2},{8,12},{10,14},{12,8},{14,10},{16,20},{18,... | collective-permute-start | bytes 811016 | tf_op jit(solution)/shard_map/ppermute | solution.py:805
  237.3 6.5 %collective-permute-start.39 = (bf16[1056,128]{1,0:T(8,128)(2,1)S(1)}, bf16[1056,128]{1,0:T(8,128)(2,1)S(1)}, u32[]{:S(2)}, u32[]{:S(2)}) collective-permute-start(bf16[1056,128]{1,0:T(8,128)(2,1)S(1)} %slice.34), channel_id=1, source_target_pairs={{0,2},{2,0},{4,6},{6,4},{8,10},{10,8},{12,14},{14,12},{16,18},{18,... | collective-permute-start | bytes 811016 | tf_op jit(solution)/shard_map/ppermute | solution.py:805

commit v2 on v1

--- a/solution.py
+++ b/solution.py
@@ -582,9 +582,9 @@
     return where_ref[2] ^ sum(((at >> bit) & 1) << (bits - 1 - bit) for bit in range(bits))
 
 
-def each_piece(where_ref, refs, digits, rows, use):
+def each_piece(where_ref, refs, digits, rows, use, steps=range(4)):
     owners = 4 ** (digits - 1)
-    for step in range(4):
+    for step in steps:
         column = where_ref[1] ^ step
         for at in range(owners):
             owner = place_rows(where_ref, digits, at)
@@ -604,27 +604,50 @@
             use(column, owner, load)
 
 
-def finish_out_value_kernel(where_ref, *refs, digits):
-    qkv_ref, out_ref = refs[5:]
-    width = qkv_ref.shape[1]
+def out_value_pieces(where_ref, refs, digits, steps, value_ref, value_column, out_ref, out_first):
+    width = value_ref.shape[1]
     rows = width // 4 ** (digits - 1)
     few = rows * 128 // width
 
     def use(column, owner, load):
-        start = pl.multiple_of(column * 128 + owner * few, few)
+        start = pl.multiple_of(out_first(column) + owner * few, few)
         out_ref[pl.ds(start, few), :] = jnp.concatenate(
             [load(at, at + few).astype(F32) for at in range(0, rows, few)], axis=1
         )
-        lanes = pl.ds(pl.multiple_of(column * 128, 128), 128)
-        qkv_ref[0, pl.ds(pl.multiple_of(owner * rows, rows), rows), lanes] = load(
+        lanes = pl.ds(pl.multiple_of(value_column(column), 128), 128)
+        value_ref[0, pl.ds(pl.multiple_of(owner * rows, rows), rows), lanes] = load(
             rows, 2 * rows
         ).astype(F32)
 
-    each_piece(where_ref, refs[:5], digits, rows, use)
-
-
-def finish_key_query_kernel(where_ref, *refs, digits, sums):
-    qkv_ref, sums_ref = refs[6:]
+    each_piece(where_ref, refs, digits, rows, use, steps)
+
+
+def finish_out_value_near_kernel(where_ref, *refs, digits):
+    value_ref, out_ref = refs[3:]
+
+    def place(column):
+        return column * 128
+
+    out_value_pieces(where_ref, refs[:3], digits, range(3), value_ref, place, out_ref, place)
+
+
+def finish_out_value_far_kernel(where_ref, *refs, digits):
+    halves, (_, _, value_far, out_far, value_ref, out_ref, sems) = refs[:2], refs[2:]
+    out_value_pieces(
+        where_ref, (None, None, None, *halves), digits, range(3, 4),
+        value_ref, lambda column: 0, out_ref, lambda column: 0,
+    )
+    first = pl.ds(pl.multiple_of((where_ref[1] ^ 3) * 128, 128), 128)
+    leaving = [
+        started(value_ref, value_far.at[pl.ds(2, 1), :, first], sems.at[0]),
+        started(out_ref, out_far.at[first], sems.at[1]),
+    ]
+    for copy in leaving:
+        copy.wait()
+
+
+def finish_near_kernel(where_ref, *refs, digits, sums):
+    qkv_ref, sums_ref = refs[4:]
     width = qkv_ref.shape[1]
     rows = width // 4 ** (digits - 1)
 
@@ -634,12 +657,27 @@
         qkv_ref[1, down, lanes] = load(0, rows).astype(F32)
         qkv_ref[0, down, lanes] = load(rows, 2 * rows).astype(F32)
 
-    each_piece(where_ref, refs[:5], digits, rows, use)
+    each_piece(where_ref, refs[:3], digits, rows, use, range(3))
     total = refs[0].shape[0]
-    half = refs[4].shape[0]
-    sums_ref[...] = split_sum(refs[:3], total - sums, total) + split_sum(
-        refs[4:5], half - sums, half
-    )
+    sums_ref[...] = split_sum(refs[:3], total - sums, total)
+
+
+def finish_far_kernel(where_ref, *refs, digits, sums):
+    halves, near_sums_ref, _, qkv_far, sums_ref, total_ref, sem = refs[:2], *refs[2:]
+    width = total_ref.shape[1]
+    rows = width // 4 ** (digits - 1)
+
+    def use(column, owner, load):
+        down = pl.ds(pl.multiple_of(owner * rows, rows), rows)
+        total_ref[1, down, :] = load(0, rows).astype(F32)
+        total_ref[0, down, :] = load(rows, 2 * rows).astype(F32)
+
+    each_piece(where_ref, (None, None, None, *halves), digits, rows, use, range(3, 4))
+    lanes = pl.ds(pl.multiple_of((where_ref[1] ^ 3) * 128, 128), 128)
+    leaving = started(total_ref, qkv_far.at[pl.ds(0, 2), :, lanes], sem)
+    half = halves[1].shape[0]
+    sums_ref[...] = near_sums_ref[...] + split_sum(halves[1:], half - sums, half)
+    leaving.wait()
 
 
 def expert_grad_kernel(rows_ref, grads_ref, hidden_ref, dpre_ref, up_ref, down_ref, turned_ref):
@@ -816,7 +854,7 @@
     return list(lax.optimization_barrier((*values, *others))[: len(values)])
 
 
-def sum_and_spread(first, second, where, digits, sums, extra, finish, first_wait):
+def sum_and_spread(first, second, where, digits, sums, extra, finish_near, finish_far, first_wait, filler):
     bits = 2 * (digits - 1)
 
     def across(value, bit):
@@ -856,23 +894,28 @@
             came = yield total, [across(total, bit)]
             total = stack(total, came[0], extra)
         by_x, by_y = yield total, [flip(total, "exp", 1), flip(total, "exp", 2)]
+        if extra == 0:
+            near.extend(finish_near(total, by_x, by_y))
         middle = total.shape[0] // 2
         sent = [by_y[:middle], by_x[middle:]]
         halves = yield sent[0], [flip(sent[0], "exp", 1), flip(sent[1], "exp", 2)]
         yield None, [total, by_x, by_y, *halves]
 
-    lines, states, last = [steps(first, None, 0), None], [None, None], first_wait
+    near = []
+    lines, states, last, finished = [steps(first, None, 0), None], [None, None], first_wait, None
     states[0] = next(lines[0])
     for at, line in enumerate([0] + [0, 1] * (2 * bits + 1) + [1]):
         if at == 1:
             pieces = second(last)
             lines[1], last = steps(pieces, sums, extra), pieces[1]
             states[1] = next(lines[1])
-        came = states[line][1]
-        states[line] = lines[line].send(came if last is None else after_all(came, last))
+        ahead = [*near[1:], filler] if line == 0 and near else []
+        states[line] = lines[line].send(after_all(states[line][1], last, *ahead))
         last = states[line][0]
         if line == 0 and last is None:
-            finished = finish(states[0][1])
+            finished = finish_far(*states[0][1][3:], *near)
+            last = states[0][1][3]
+        elif finished is not None:
             last = finished[1]
     return finished, states[1][1]
 
@@ -1063,7 +1106,7 @@
         away=(1, 2, 3),
         out_away=(0,),
     )
-    tokens = [inputs, *plane_own, *plane_other]
+    tokens = [inputs, *after_all([*plane_own, *plane_other], du_sent)]
     split = [((n_exp // 8, 2 * piece, 128), BF16)] * 2
     product = 8 * span * width * 128
     out_value = call(
@@ -1087,37 +1130,67 @@
     sums = [sums1, cross(sums1), sums2, cross(sums2)]
     extra = 4 * sums1.shape[0]
     whole_qkv = pltpu.HBM((3, width, columns), F32)
-    finish = pl.pallas_call(
-        functools.partial(finish_out_value_kernel, digits=digits),
-        name="finish_out_value",
+    whole_out = pltpu.HBM((columns, width), F32)
+    in_place = pl.BlockSpec(memory_space=pltpu.HBM)
+    finish_near = pl.pallas_call(
+        functools.partial(finish_out_value_near_kernel, digits=digits),
+        name="finish_out_value_near",
         grid=(1,),
-        out_shape=[whole_qkv, pltpu.HBM((columns, width), F32)],
-        in_specs=[SMEM] + [VMEM] * 5,
+        out_shape=[whole_qkv, whole_out],
+        in_specs=[SMEM] + [VMEM] * 3,
         out_specs=[
             pl.BlockSpec((1, width, columns), lambda i: (2, 0, 0)),
             pl.BlockSpec((columns, width), lambda i: (0, 0)),
         ],
         cost_estimate=pl.CostEstimate(flops=0, bytes_accessed=6 * MIB, transcendentals=0),
-        compiler_params=pltpu.CompilerParams(vmem_limit_bytes=40 * MIB),
+        compiler_params=pltpu.CompilerParams(vmem_limit_bytes=20 * MIB),
+    )
+    finish_far = pl.pallas_call(
+        functools.partial(finish_out_value_far_kernel, digits=digits),
+        name="finish_out_value_far",
+        out_shape=[whole_qkv, whole_out],
+        in_specs=[SMEM] + [VMEM] * 2 + [in_place] * 2,
+        out_specs=[in_place] * 2,
+        scratch_shapes=[
+            pltpu.VMEM((1, width, 128), F32),
+            pltpu.VMEM((128, width), F32),
+            pltpu.SemaphoreType.DMA((2,)),
+        ],
+        input_output_aliases={3: 0, 4: 1},
+        cost_estimate=pl.CostEstimate(flops=0, bytes_accessed=2 * MIB, transcendentals=0),
+        compiler_params=pltpu.CompilerParams(vmem_limit_bytes=16 * MIB),
     )
     (grad_qkv, grad_out), key_query = sum_and_spread(
-        out_value, key_query, where, digits, sums, extra, lambda parts: finish(where, *parts),
-        branch_sent,
-    )
+        out_value, key_query, where, digits, sums, extra, functools.partial(finish_near, where),
+        functools.partial(finish_far, where), branch_sent, result,
+    )
+    sums_shape = jax.ShapeDtypeStruct((extra // 2, 128), F32)
     grad_qkv, sums = pl.pallas_call(
-        functools.partial(finish_key_query_kernel, digits=digits, sums=extra),
-        name="finish_key_query",
+        functools.partial(finish_near_kernel, digits=digits, sums=extra),
+        name="finish_near",
         grid=(1,),
-        out_shape=[whole_qkv, jax.ShapeDtypeStruct((extra // 2, 128), F32)],
-        in_specs=[SMEM] + [VMEM] * 5 + [pl.BlockSpec(memory_space=pltpu.HBM)],
+        out_shape=[whole_qkv, sums_shape],
+        in_specs=[SMEM] + [VMEM] * 3 + [in_place],
         out_specs=[
             pl.BlockSpec((2, width, columns), lambda i: (0, 0, 0)),
             pl.BlockSpec((extra // 2, 128), lambda i: (0, 0)),
         ],
-        input_output_aliases={6: 0},
+        input_output_aliases={4: 0},
         cost_estimate=pl.CostEstimate(flops=0, bytes_accessed=6 * MIB, transcendentals=0),
-        compiler_params=pltpu.CompilerParams(vmem_limit_bytes=40 * MIB),
-    )(where, *key_query, grad_qkv)
+        compiler_params=pltpu.CompilerParams(vmem_limit_bytes=20 * MIB),
+    )(where, *key_query[:3], grad_qkv)
+    halves = after_all(key_query[3:], sums)
+    grad_qkv, sums = pl.pallas_call(
+        functools.partial(finish_far_kernel, digits=digits, sums=extra),
+        name="finish_far",
+        out_shape=[whole_qkv, sums_shape],
+        in_specs=[SMEM] + [VMEM] * 3 + [in_place],
+        out_specs=[in_place, VMEM],
+        scratch_shapes=[pltpu.VMEM((2, width, 128), F32), pltpu.SemaphoreType.DMA],
+        input_output_aliases={4: 0},
+        cost_estimate=pl.CostEstimate(flops=0, bytes_accessed=2 * MIB, transcendentals=0),
+        compiler_params=pltpu.CompilerParams(vmem_limit_bytes=16 * MIB),
+    )(where, *halves, sums, grad_qkv)
     sums = sums.reshape(4, width)
     return (
         result,

time: 248 us -> 244 us (0.984)
  waiting for transfers between devices: 77.4 us -> 70.4 us
  Pallas kernels: 86.6 us -> 89.7 us
    ppermute x41, waiting for transfers between devices: 59.7 us -> 52.7 us  [flip(): return lax.ppermute(value, axis, [(i, i ^ bit) for i in range(size)])]
    pallas_call x2 -> x4, Pallas kernels: 6.06 us -> 9 us  [the longest x1 2.98 us: on_device(): pl.pallas_call(functools.partial(finish_near_kernel, digits=digits, sums=...]
  transfers between devices with their start and end apart: 44 -> 44, of which waited for: 23 -> 22; matrix products, arithmetic and copies ran while one was open for 1% -> 1% of each run, Pallas kernels for 27% -> 29%
where the time goes in v2:
time: 244 us; the launch traced here: 243 us
  Pallas kernels  89.7 us (37%)
  waiting for transfers between devices  70.4 us (29%)
  starting transfers between devices  57 us (23%)
  blocking collectives  21.2 us (9%)
  local copies, waits for them, and re-layouts  2.7 us (1%)
    ppermute x41, waiting for transfers between devices, flip(): return lax.ppermute(value, axis, [(i, i ^ bit) for i in range(size)])  52.7 us
    pallas_call x21, Pallas kernels, call(): pl.pallas_call(kernel, name=name, out_shape=shapes, in_specs=[SMEM if at...  49.1 us
    ppermute x41, starting transfers between devices, flip(): return lax.ppermute(value, axis, [(i, i ^ bit) for i in range(size)])  41.1 us
    all_to_all x1, blocking collectives, exchange(): lax.all_to_all(value, ('exp', 'head'), split_axis=0, concat_axis=0, tiled...  21.2 us
    all_to_all x3, waiting for transfers between devices, exchange(): lax.all_to_all(value, ('exp', 'head'), split_axis=0, concat_axis=0, tiled...  17.8 us
    all_to_all x3, starting transfers between devices, exchange(): lax.all_to_all(value, ('exp', 'head'), split_axis=0, concat_axis=0, tiled...  15.9 us
    pallas_call x1, Pallas kernels, expert(): pl.pallas_call(expert_kernel, name='expert', grid=(units // tile,), out_s...  13.1 us
    pallas_call x1, Pallas kernels, expert_grads(): pl.pallas_call(expert_grad_kernel, name='expert_grads', grid=(units // ti...  11.6 us
  transfers between devices with their start and end apart: 44, of which 22 were waited for; matrix products, arithmetic and copies ran while one was open for 1% of the time, Pallas kernels for 29%

profile of v2, /device:TPU:0, one launch (start us, length us, event | category | flops | bytes accessed | tf_op | source)
XLA Modules:
  0.0 243.2 jit_solution(4042496798826855990)
XLA Ops:
  0.7 3.3 %norm1.1 = bf16[256,1280]{1,0:T(8,128)(2,1)} custom-call(bf16[320,1024]{1,0:T(8,128)(2,1)} %x_ref.5, f32[1,1024]{1,0:T(1,128)} %bitcast.40, f32[1,1024]{1,0:T(1,128)} %bitcast.45), custom_call_target="tpu_custom_call" | custom-call | flops 503316480 | bytes 1318912 | tf_op jit(solution)/shard_map/norm1/pallas_call | solution.py:740
  4.0 7.3 %all-to-all-start = ((bf16[32,8,1280]{2,1,0:T(8,128)(2,1)}), bf16[32,8,1280]{2,1,0:T(8,128)(2,1)S(1)}, u32[]{:S(2)}, u32[]{:S(2)}) async-start(bf16[32,8,1280]{2,1,0:T(8,128)(2,1)} %bitcast.5), calls=%async_computation | async-start | bytes 1310720 | tf_op jit(solution)/shard_map/all_to_all | solution.py:960
  11.4 17.8 %all-to-all-done = bf16[32,8,1280]{2,1,0:T(8,128)(2,1)S(1)} async-done(((bf16[32,8,1280]{2,1,0:T(8,128)(2,1)}), bf16[32,8,1280]{2,1,0:T(8,128)(2,1)S(1)}, u32[]{:S(2)}, u32[]{:S(2)}) %all-to-all-start) | async-done | bytes 655392 | tf_op jit(solution)/shard_map/all_to_all | solution.py:960
  30.1 1.8 collective-permute-done.other_ref
  31.8 8.2 %attend.1 = (bf16[256,1024]{1,0:T(8,128)(2,1)}, bf16[512,1024]{1,0:T(8,128)(2,1)}, bf16[3,512,512]{2,1,0:T(8,128)(2,1)}, bf16[512,512]{1,0:T(8,128)(2,1)}, f32[1...) custom-call(s32[3]{0:T(128)S(1)} %pad_add_fusion.where_ref, s32[1,5]{1,0:T(1,128)S(1)} %copy-done.5, ...), custom_call_target="tpu_custom_call" | custom-call | flops 4294967296 | bytes 10747936 | tf_op jit(solution)/shard_map/attend/pallas_call | solution.py:740
  40.2 1.8 collective-permute-done.1.came_ref
  42.7 21.2 %all_to_all.20 = bf16[32,8,1280]{2,1,0:T(8,128)(2,1)S(1)} all-to-all(bf16[32,8,1280]{2,1,0:T(8,128)(2,1)S(1)} %bitcast.31), channel_id=1, replica_groups=mesh['exp'=16,'head'=2] {'exp','head'}, dimensions={0} | all-to-all | bytes 1310720 | tf_op jit(solution)/shard_map/all_to_all | solution.py:960
  63.9 1.2 norm2.1
  65.7 2.3 collective-permute-start.4
  68.2 13.1 %expert.1 = (bf16[640,2048]{1,0:T(8,128)(2,1)}, bf16[640,2048]{1,0:T(8,128)(2,1)}, f32[320,1024]{1,0:T(8,128)S(1)}, bf16[320,1024]{1,0:T(8,128)(2,1)S(1)}, bf16[...) custom-call(bf16[320,1024]{1,0:T(8,128)(2,1)S(1)} %get-tuple-element.124.h2_ref, ...), custom_call_target="tpu_custom_call" | custom-call | flops 8053063680 | bytes 16777216 | tf_op jit(solution)/shard_map/expert/pallas_call | solution.py:770
  81.5 2.0 collective-permute-done.5.came_ref
  83.5 3.1 %norm2_back.1 = (f32[320,1024]{1,0:T(8,128)}, bf16[256,1280]{1,0:T(8,128)(2,1)}, f32[16,128]{1,0:T(8,128)S(1)}) custom-call(f32[320,1024]{1,0:T(8,128)S(1)} %get-tuple-element.128.kept_ref, bf16[320,1024]{1,0:T(8,128)(2,1)S(1)} %collective-permute-done.5.came_ref, f32[320,1024]{1,0:T(8,128)S(1)} %get-tuple-element.121.resid_ref, ...), custom_call_target="tpu_custom_call" | custom-call | flops 503316480 | bytes 5910528 | tf_op jit(solution)/shard_map/norm2_back/pallas_call | solution.py:740
  86.6 3.7 %all-to-all-start.2 = ((bf16[32,8,1280]{2,1,0:T(8,128)(2,1)}), bf16[32,8,1280]{2,1,0:T(8,128)(2,1)S(1)}, u32[]{:S(2)}, u32[]{:S(2)}) async-start(bf16[32,8,1280]{2,1,0:T(8,128)(2,1)} %bitcast.15), calls=%async_computation.2 | async-start | bytes 1310720 | tf_op jit(solution)/shard_map/all_to_all | solution.py:960
  90.4 1.6 collective-permute-start.6
  92.0 1.5 collective-permute-start.7
  93.4 11.6 %expert_grads.1 = (f32[1024,2048]{1,0:T(8,128)}, f32[2048,1024]{1,0:T(8,128)}) custom-call(bf16[640,1024]{1,0:T(8,128)(2,1)} %get-tuple-element.133.rows_ref, bf16[640,1024]{1,0:T(8,128)(2,1)} %get-tuple-element.134.grads_ref, bf16[640,2048]{1,0:T(8,128)(2,1)} %get-tuple-element.174.hidden_ref, bf16[640,2048]{1,0:T(8,128)(2,1)} %get-tuple-element.135.dpre_ref), custom_call_target="tpu_custom_call" | custom-call | flops 5368709120 | bytes 25165824 | tf_op jit(solution)/shard_map/expert_grads/pallas_call | solution.py:800
  105.0 6.2 %collective-permute-done.6.refs_5_ = bf16[256,1024]{1,0:T(8,128)(2,1)S(1)} collective-permute-done((bf16[256,1024]{1,0:T(8,128)(2,1)S(1)}, bf16[256,1024]{1,0:T(8,128)(2,1)S(1)}, u32[]{:S(2)}, u32[]{:S(2)}) %collective-permute-start.6) | collective-permute-done | bytes 524320 | tf_op jit(solution)/shard_map/ppermute | solution.py:843
  114.4 1.1 collective-permute-done.9.other_ref
  115.5 3.4 %out_grad.1 = (bf16[512,1024]{1,0:T(8,128)(2,1)S(1)}, bf16[4,256,128]{2,1,0:T(8,128)(2,1)}, bf16[4,256,128]{2,1,0:T(8,128)(2,1)}, bf16[4,256,128]{2,1,0:T(8,128)(2,1)}, bf16[4,256,128]{2,1,0:T(8,128)(2,1)}) custom-call(s32[3]{0:T(128)S(1)} %pad_add_fusion.where_ref, bf16[256,1024]{1,0:T(8,128)(2,1)S(1)} %gather2.1.own_ref, ...), custom_call_target="tpu_custom_call" | custom-call | flops 536870912 | bytes 3670028 | tf_op jit(solution)/shard_map/out_grad/pallas_call | solution.py:740
  119.6 1.4 collective-permute-start.11
  121.0 1.5 collective-permute-start.12
  122.4 8.9 %attend_back.1 = (f32[256,1024]{1,0:T(8,128)S(1)}, bf16[256,1024]{1,0:T(8,128)(2,1)S(1)}, bf16[512,128]{1,0:T(8,128)(2,1)}, bf16[512,128]{1,0:T(8,128)(2,1)}, bf...) custom-call(s32[3]{0:T(128)S(1)} %pad_add_fusion.where_ref, ...), custom_call_target="tpu_custom_call" | custom-call | flops 7516192768 | bytes 10747936 | tf_op jit(solution)/shard_map/attend_back/pallas_call | solution.py:740
  131.4 2.6 %collective-permute-done.12.refs_14_ = bf16[4,256,128]{2,1,0:T(8,128)(2,1)S(1)} collective-permute-done((bf16[4,256,128]{2,1,0:T(8,128)(2,1)}, bf16[4,256,128]{2,1,0:T(8,128)(2,1)S(1)}, u32[]{:S(2)}, u32[]{:S(2)}) %collective-permute-start.12) | collective-permute-done | bytes 262176 | tf_op jit(solution)/shard_map/ppermute | solution.py:843
  134.9 1.5 collective-permute-start.16
  136.3 1.2 collective-permute-start.17
  137.5 1.4 scatter2.1
  139.0 1.6 collective-permute-done.15.refs_1_
  140.5 3.0 %collective-permute-done.16.refs_2_ = bf16[512,128]{1,0:T(8,128)(2,1)S(1)} collective-permute-done((bf16[512,128]{1,0:T(8,128)(2,1)}, bf16[512,128]{1,0:T(8,128)(2,1)S(1)}, u32[]{:S(2)}, u32[]{:S(2)}) %collective-permute-start.16) | collective-permute-done | bytes 131104 | tf_op jit(solution)/shard_map/ppermute | solution.py:843
  143.5 4.8 %all-to-all-start.3 = ((bf16[32,8,1280]{2,1,0:T(8,128)(2,1)}), bf16[32,8,1280]{2,1,0:T(8,128)(2,1)S(1)}, u32[]{:S(2)}, u32[]{:S(2)}) async-start(bf16[32,8,1280]{2,1,0:T(8,128)(2,1)} %bitcast.17), calls=%async_computation.3 | async-start | bytes 1310720 | tf_op jit(solution)/shard_map/all_to_all | solution.py:960
  148.4 4.0 %value_grad.1 = (bf16[2,512,128]{2,1,0:T(8,128)(2,1)}, bf16[2,512,128]{2,1,0:T(8,128)(2,1)S(1)}) custom-call(s32[3]{0:T(128)S(1)} %pad_add_fusion.where_ref, bf16[512,128]{1,0:T(8,128)(2,1)} %get-tuple-element.160.refs_0_, bf16[512,128]{1,0:T(8,128)(2,1)S(1)} %collective-permute-done.15.refs_1_, bf16[512,128]{1,0:T(8,128)(2,1)S(1)} %collective-permute-done.16.refs_2_, ...), custom_call_target="tpu_custom_call" | custom-call | flops 536870912 | bytes 6291468 | tf_op jit(solution)/shard_map/value_grad/pallas_call | solution.py:740
  152.4 1.5 collective-permute-start.23
  153.9 1.5 collective-permute-start.20
  155.4 1.5 collective-permute-start.21
  157.4 6.9 %expert_branch.1 = (bf16[320,1024]{1,0:T(8,128)(2,1)}, bf16[320,1024]{1,0:T(8,128)(2,1)}) custom-call(bf16[640,2048]{1,0:T(8,128)(2,1)} %get-tuple-element.174.hidden_ref, bf16[2048,1024]{1,0:T(8,128)(2,1)} %bitcast.44), custom_call_target="tpu_custom_call" | custom-call | flops 2684354560 | bytes 8388608 | tf_op jit(solution)/shard_map/expert_branch/pallas_call | solution.py:823
  164.3 2.8 %collective-permute-done.23.came_ref = bf16[2,512,128]{2,1,0:T(8,128)(2,1)S(1)} collective-permute-done((bf16[2,512,128]{2,1,0:T(8,128)(2,1)S(1)}, bf16[2,512,128]{2,1,0:T(8,128)(2,1)S(1)}, u32[]{:S(2)}, u32[]{:S(2)}) %collective-permute-start.23) | collective-permute-done | bytes 262176 | tf_op jit(solution)/shard_map/ppermute | solution.py:843
  167.1 1.7 add.17
  168.8 2.4 collective-permute-start.25
  171.6 4.4 %key_query_grad.1 = (bf16[2,512,128]{2,1,0:T(8,128)(2,1)}, bf16[2,512,128]{2,1,0:T(8,128)(2,1)S(1)}) custom-call(s32[3]{0:T(128)S(1)} %pad_add_fusion.where_ref, bf16[2,512,128]{2,1,0:T(8,128)(2,1)} %get-tuple-element.181.refs_0_, bf16[2,512,128]{2,1,0:T(8,128)(2,1)S(1)} %collective-permute-done.20.refs_1_, ...), custom_call_target="tpu_custom_call" | custom-call | flops 1073741824 | bytes 5767180 | tf_op jit(solution)/shard_map/key_query_grad/pallas_call | solution.py:740
  176.0 1.1 collective-permute-start.24
  177.3 0.9 last_add.1.own_ref
  178.2 1.7 collective-permute-start.27
  180.0 5.7 %collective-permute-done.24.came_ref = bf16[2,512,128]{2,1,0:T(8,128)(2,1)S(1)} collective-permute-done((bf16[2,512,128]{2,1,0:T(8,128)(2,1)S(1)}, bf16[2,512,128]{2,1,0:T(8,128)(2,1)S(1)}, u32[]{:S(2)}, u32[]{:S(2)}) %collective-permute-start.24) | collective-permute-done | bytes 262176 | tf_op jit(solution)/shard_map/ppermute | solution.py:843
  185.7 1.7 add.18
  187.4 1.2 collective-permute-start.31
  188.5 2.1 collective-permute-start.26
  190.7 3.9 %norm1_back.1 = (f32[320,1024]{1,0:T(8,128)}, f32[16,128]{1,0:T(8,128)S(1)}) custom-call(bf16[256,1280]{1,0:T(8,128)(2,1)S(1)} %bitcast.29, bf16[320,1024]{1,0:T(8,128)(2,1)} %x_ref.5, f32[320,1024]{1,0:T(8,128)} %get-tuple-element.179.dresid_ref, f32[1,1024]{1,0:T(1,128)} %bitcast.41), custom_call_target="tpu_custom_call" | custom-call | flops 503316480 | bytes 3944448 | tf_op jit(solution)/shard_map/norm1_back/pallas_call | solution.py:740
  195.9 1.0 last_add_sums.1.own_ref
  197.0 1.5 collective-permute-start.33
  198.5 2.7 %collective-permute-start.34 = (bf16[2048,128]{1,0:T(8,128)(2,1)S(1)}, bf16[2048,128]{1,0:T(8,128)(2,1)S(1)}, u32[]{:S(2)}, u32[]{:S(2)}) collective-permute-start(bf16[2048,128]{1,0:T(8,128)(2,1)S(1)} %stack.21.refs_0_), channel_id=1, source_target_pairs={{0,4},{2,6},{4,0},{6,2},{8,12},{10,14},{12,8},{14,10},{16,20},{18,... | collective-permute-start | bytes 1572872 | tf_op jit(solution)/shard_map/ppermute | solution.py:843
  201.2 2.2 collective-permute-start.30
  203.4 6.2 %collective-permute-done.30.came_ref = bf16[576,128]{1,0:T(8,128)(2,1)S(1)} collective-permute-done((bf16[576,128]{1,0:T(8,128)(2,1)S(1)}, bf16[576,128]{1,0:T(8,128)(2,1)S(1)}, u32[]{:S(2)}, u32[]{:S(2)}) %collective-permute-start.30) | collective-permute-done | bytes 147488 | tf_op jit(solution)/shard_map/ppermute | solution.py:843
  209.7 1.5 collective-permute-done.33.refs_1_
  211.2 1.2 collective-permute-done.34.refs_2_
  212.4 3.9 %collective-permute-done.32.came_ref = bf16[1088,128]{1,0:T(8,128)(2,1)S(1)} collective-permute-done((bf16[1088,128]{1,0:T(8,128)(2,1)S(1)}, bf16[1088,128]{1,0:T(8,128)(2,1)S(1)}, u32[]{:S(2)}, u32[]{:S(2)}) %collective-permute-start.32) | collective-permute-done | bytes 278560 | tf_op jit(solution)/shard_map/ppermute | solution.py:843
  216.7 1.6 collective-permute-start.36
  219.1 1.6 collective-permute-start.38
  220.7 1.1 add_convert_fusion
  221.8 2.8 %finish_out_value_near.1 = (f32[3,1024,512]{2,1,0:T(8,128)}, f32[512,1024]{1,0:T(8,128)}) custom-call(s32[3]{0:T(128)S(1)} %pad_add_fusion.where_ref, bf16[2048,128]{1,0:T(8,128)(2,1)S(1)} %stack.21.refs_0_, bf16[2048,128]{1,0:T(8,128)(2,1)S(1)} %collective-permute-done.33.refs_1_, bf16[2048,128]{1,0:T(8,128)(2,1)S(1)} %collective-permute-done.34.refs_2_), custom_call_target="tpu_custom_call" | custom-call | bytes 6291456 | tf_op jit(solution)/shard_map/finish_out_value_near/pallas_call | solution.py:898
  224.7 6.8 %collective-permute-done.37.refs_0_ = bf16[1024,128]{1,0:T(8,128)(2,1)S(1)} collective-permute-done((bf16[1024,128]{1,0:T(8,128)(2,1)S(1)}, bf16[1024,128]{1,0:T(8,128)(2,1)S(1)}, u32[]{:S(2)}, u32[]{:S(2)}) %collective-permute-start.37) | collective-permute-done | bytes 262176 | tf_op jit(solution)/shard_map/ppermute | solution.py:843
  231.5 2.7 %collective-permute-done.38.refs_1_ = bf16[1024,128]{1,0:T(8,128)(2,1)S(1)} collective-permute-done((bf16[1024,128]{1,0:T(8,128)(2,1)S(1)}, bf16[1024,128]{1,0:T(8,128)(2,1)S(1)}, u32[]{:S(2)}, u32[]{:S(2)}) %collective-permute-start.38) | collective-permute-done | bytes 262176 | tf_op jit(solution)/shard_map/ppermute | solution.py:843
  234.5 2.0 collective-permute-start.40
  236.5 1.6 finish_out_value_far.1
  238.0 3.0 %finish_near.1 = (f32[3,1024,512]{2,1,0:T(8,128)}, f32[32,128]{1,0:T(8,128)S(1)}) custom-call(s32[3]{0:T(128)S(1)} %pad_add_fusion.where_ref, bf16[2112,128]{1,0:T(8,128)(2,1)S(1)} %stack.23.refs_0_, bf16[2112,128]{1,0:T(8,128)(2,1)S(1)} %collective-permute-done.35.refs_1_, ...), custom_call_target="tpu_custom_call", output_to_operand_aliasing={{0}: (4, {})} | custom-call | bytes 6291456 | tf_op jit(solution)/shard_map/finish_near/pallas_call | solution.py:1168
  241.0 1.6 finish_far.1
  (100 shorter events, 12.5 us)
Async XLA Ops:
  0.6 10.7 %copy-start.3 = (s32[256]{0:T(256)S(1)}, s32[256]{0:T(256)}, u32[]{:S(2)}) copy-start(s32[256]{0:T(256)} %param.13) | copy-start | bytes 3076
  4.0 27.8 %copy-start.5 = (s32[1,5]{1,0:T(1,128)S(1)}, s32[1,5]{1,0:T(1,128)}, u32[]{:S(2)}) copy-start(s32[1,5]{1,0:T(1,128)} %lengths_ref.3) | copy-start | bytes 64
  4.0 25.2 %all-to-all-start = ((bf16[32,8,1280]{2,1,0:T(8,128)(2,1)}), bf16[32,8,1280]{2,1,0:T(8,128)(2,1)S(1)}, u32[]{:S(2)}, u32[]{:S(2)}) async-start(bf16[32,8,1280]{2,1,0:T(8,128)(2,1)} %bitcast.5), calls=%async_computation | async-start | bytes 1310720 | tf_op jit(solution)/shard_map/all_to_all | solution.py:960
  29.8 2.0 collective-permute-start
  40.0 2.0 collective-permute-start.1
  42.0 21.9 %copy-start = (bf16[320,1024]{1,0:T(8,128)(2,1)S(1)}, bf16[320,1024]{1,0:T(8,128)(2,1)}, u32[]{:S(2)}) copy-start(bf16[320,1024]{1,0:T(8,128)(2,1)} %x_ref.5) | copy-start | bytes 1966084
  42.0 21.9 %copy-start.1 = (bf16[320,1024]{1,0:T(8,128)(2,1)S(1)}, bf16[320,1024]{1,0:T(8,128)(2,1)}, u32[]{:S(2)}) copy-start(bf16[320,1024]{1,0:T(8,128)(2,1)} %grad_ref.3) | copy-start | bytes 1966084
  42.0 21.9 %copy-start.2 = (f32[1024]{0:T(1024)S(1)}, f32[1024]{0:T(1024)}, u32[]{:S(2)}) copy-start(f32[1024]{0:T(1024)} %param.17) | copy-start | bytes 12292
  42.0 21.9 %copy-start.4 = (f32[1024]{0:T(1024)S(1)}, f32[1024]{0:T(1024)}, u32[]{:S(2)}) copy-start(f32[1024]{0:T(1024)} %param.18) | copy-start | bytes 12292
  42.7 23.1 %copy-start.15 = (bf16[256,1024]{1,0:T(8,128)(2,1)S(1)}, bf16[256,1024]{1,0:T(8,128)(2,1)}, u32[]{:S(2)}) copy-start(bf16[256,1024]{1,0:T(8,128)(2,1)} %get-tuple-element.138) | copy-start | bytes 1572868
  65.1 2.9 %collective-permute-start.2 = (bf16[320,1024]{1,0:T(8,128)(2,1)S(1)}, bf16[320,1024]{1,0:T(8,128)(2,1)S(1)}, u32[]{:S(2)}, u32[]{:S(2)}) collective-permute-start(bf16[320,1024]{1,0:T(8,128)(2,1)S(1)} %get-tuple-element.124.h2_ref), channel_id=1, source_target_pairs={{0,1},{1,0},{2,3},{3,2},{4,5},{5,4},{6,7},{7,6},{8,9},{9,8},{10,11... | collective-permute-start | bytes 1966088 | tf_op jit(solution)/shard_map/ppermute | solution.py:843
  65.3 3.0 %collective-permute-start.3 = (bf16[320,1024]{1,0:T(8,128)(2,1)S(1)}, bf16[320,1024]{1,0:T(8,128)(2,1)S(1)}, u32[]{:S(2)}, u32[]{:S(2)}) collective-permute-start(bf16[320,1024]{1,0:T(8,128)(2,1)S(1)} %get-tuple-element.125.up_ref), channel_id=1, source_target_pairs={{0,1},{1,0},{2,3},{3,2},{4,5},{5,4},{6,7},{7,6},{8,9},{9,8},{10,11... | collective-permute-start | bytes 1966088 | tf_op jit(solution)/shard_map/ppermute | solution.py:843
  65.7 15.6 %collective-permute-start.4 = (bf16[256,1024]{1,0:T(8,128)(2,1)S(1)}, bf16[256,1024]{1,0:T(8,128)(2,1)S(1)}, u32[]{:S(2)}, u32[]{:S(2)}) collective-permute-start(bf16[256,1024]{1,0:T(8,128)(2,1)S(1)} %copy-done.15), channel_id=1, source_target_pairs={{0,6},{2,4},{4,2},{6,0},{8,14},{10,12},{12,10},{14,8},{16,22},{18,... | collective-permute-start | bytes 1572872 | tf_op jit(solution)/shard_map/ppermute | solution.py:843
  81.3 12.1 %copy-start.6 = (bf16[256,1024]{1,0:T(8,128)(2,1)}, bf16[256,1024]{1,0:T(8,128)(2,1)S(1)}, u32[]{:S(2)}) copy-start(bf16[256,1024]{1,0:T(8,128)(2,1)S(1)} %collective-permute-done.4.refs_7_) | copy-start | bytes 1572868
  81.3 2.2 collective-permute-start.5
  86.6 26.3 %all-to-all-start.2 = ((bf16[32,8,1280]{2,1,0:T(8,128)(2,1)}), bf16[32,8,1280]{2,1,0:T(8,128)(2,1)S(1)}, u32[]{:S(2)}, u32[]{:S(2)}) async-start(bf16[32,8,1280]{2,1,0:T(8,128)(2,1)} %bitcast.15), calls=%async_computation.2 | async-start | bytes 1310720 | tf_op jit(solution)/shard_map/all_to_all | solution.py:960
  90.4 20.9 %collective-permute-start.6 = (bf16[256,1024]{1,0:T(8,128)(2,1)S(1)}, bf16[256,1024]{1,0:T(8,128)(2,1)S(1)}, u32[]{:S(2)}, u32[]{:S(2)}) collective-permute-start(bf16[256,1024]{1,0:T(8,128)(2,1)S(1)} %copy-done.15), channel_id=1, source_target_pairs={{0,2},{2,0},{4,6},{6,4},{8,10},{10,8},{12,14},{14,12},{16,18},{18,... | collective-permute-start | bytes 1572872 | tf_op jit(solution)/shard_map/ppermute | solution.py:843
  92.0 19.5 %collective-permute-start.7 = (bf16[256,1024]{1,0:T(8,128)(2,1)S(1)}, bf16[256,1024]{1,0:T(8,128)(2,1)S(1)}, u32[]{:S(2)}, u32[]{:S(2)}) collective-permute-start(bf16[256,1024]{1,0:T(8,128)(2,1)S(1)} %copy-done.15), channel_id=1, source_target_pairs={{0,4},{2,6},{4,0},{6,2},{8,12},{10,14},{12,8},{14,10},{16,20},{18,... | collective-permute-start | bytes 1572872 | tf_op jit(solution)/shard_map/ppermute | solution.py:843
  93.4 19.4 %collective-permute-start.8 = (bf16[256,1024]{1,0:T(8,128)(2,1)S(1)}, bf16[256,1024]{1,0:T(8,128)(2,1)}, u32[]{:S(2)}, u32[]{:S(2)}) collective-permute-start(bf16[256,1024]{1,0:T(8,128)(2,1)S(1)} %collective-permute-done.4.refs_7_), channel_id=1, source_target_pairs={{0,1},{1,0},{2,3},{3,2},{4,5},{5,4},{6,7},{7,6},{8,9},{9,8},{10,11... | collective-permute-start | bytes 1572872 | tf_op jit(solution)/shard_map/ppermute | solution.py:843
  111.3 0.8 copy-start.7
  112.1 0.8 copy-start.9
  112.9 1.0 copy-start.8
  112.9 1.2 copy-start.10
  113.5 2.0 collective-permute-start.9
  113.9 17.4 %collective-permute-start.13 = (bf16[256,1024]{1,0:T(8,128)(2,1)S(1)}, bf16[256,1024]{1,0:T(8,128)(2,1)S(1)}, u32[]{:S(2)}, u32[]{:S(2)}) collective-permute-start(bf16[256,1024]{1,0:T(8,128)(2,1)S(1)} %copy-done.8), channel_id=1, source_target_pairs={{0,1},{1,0},{2,3},{3,2},{4,5},{5,4},{6,7},{7,6},{8,9},{9,8},{10,11... | collective-permute-start | bytes 1572872 | tf_op jit(solution)/shard_map/ppermute | solution.py:843
  114.1 17.3 %collective-permute-start.14 = (bf16[256,1024]{1,0:T(8,128)(2,1)S(1)}, bf16[256,1024]{1,0:T(8,128)(2,1)S(1)}, u32[]{:S(2)}, u32[]{:S(2)}) collective-permute-start(bf16[256,1024]{1,0:T(8,128)(2,1)S(1)} %copy-done.10), channel_id=1, source_target_pairs={{0,1},{1,0},{2,3},{3,2},{4,5},{5,4},{6,7},{7,6},{8,9},{9,8},{10,11... | collective-permute-start | bytes 1572872 | tf_op jit(solution)/shard_map/ppermute | solution.py:843
  118.9 12.5 %collective-permute-start.10 = (bf16[4,256,128]{2,1,0:T(8,128)(2,1)}, bf16[4,256,128]{2,1,0:T(8,128)(2,1)S(1)}, u32[]{:S(2)}, u32[]{:S(2)}) collective-permute-start(bf16[4,256,128]{2,1,0:T(8,128)(2,1)} %get-tuple-element.154), channel_id=1, source_target_pairs={{0,2},{2,0},{4,6},{6,4},{8,10},{10,8},{12,14},{14,12},{16,18},{18,... | collective-permute-start | bytes 786440 | tf_op jit(solution)/shard_map/ppermute | solution.py:843
  119.6 11.8 %collective-permute-start.11 = (bf16[4,256,128]{2,1,0:T(8,128)(2,1)}, bf16[4,256,128]{2,1,0:T(8,128)(2,1)S(1)}, u32[]{:S(2)}, u32[]{:S(2)}) collective-permute-start(bf16[4,256,128]{2,1,0:T(8,128)(2,1)} %get-tuple-element.155), channel_id=1, source_target_pairs={{0,4},{2,6},{4,0},{6,2},{8,12},{10,14},{12,8},{14,10},{16,20},{18,... | collective-permute-start | bytes 786440 | tf_op jit(solution)/shard_map/ppermute | solution.py:843
  121.0 13.0 %collective-permute-start.12 = (bf16[4,256,128]{2,1,0:T(8,128)(2,1)}, bf16[4,256,128]{2,1,0:T(8,128)(2,1)S(1)}, u32[]{:S(2)}, u32[]{:S(2)}) collective-permute-start(bf16[4,256,128]{2,1,0:T(8,128)(2,1)} %get-tuple-element.156), channel_id=1, source_target_pairs={{0,6},{2,4},{4,2},{6,0},{8,14},{10,12},{12,10},{14,8},{16,22},{18,... | collective-permute-start | bytes 786440 | tf_op jit(solution)/shard_map/ppermute | solution.py:843
  131.4 12.2 %copy-start.11 = (bf16[256,1024]{1,0:T(8,128)(2,1)}, bf16[256,1024]{1,0:T(8,128)(2,1)S(1)}, u32[]{:S(2)}) copy-start(bf16[256,1024]{1,0:T(8,128)(2,1)S(1)} %collective-permute-done.13.refs_8_) | copy-start | bytes 1572868
  131.4 12.2 %copy-start.12 = (bf16[256,1024]{1,0:T(8,128)(2,1)}, bf16[256,1024]{1,0:T(8,128)(2,1)S(1)}, u32[]{:S(2)}) copy-start(bf16[256,1024]{1,0:T(8,128)(2,1)S(1)} %collective-permute-done.14.refs_9_) | copy-start | bytes 1572868
  134.0 3.5 %collective-permute-start.19 = (bf16[256,1024]{1,0:T(8,128)(2,1)S(1)}, bf16[256,1024]{1,0:T(8,128)(2,1)S(1)}, u32[]{:S(2)}, u32[]{:S(2)}) collective-permute-start(bf16[256,1024]{1,0:T(8,128)(2,1)S(1)} %get-tuple-element.165), channel_id=1, source_target_pairs={{0,1},{1,0},{2,3},{3,2},{4,5},{5,4},{6,7},{7,6},{8,9},{9,8},{10,11... | collective-permute-start | bytes 1572872 | tf_op jit(solution)/shard_map/ppermute | solution.py:843
  134.0 6.5 %collective-permute-start.15 = (bf16[512,128]{1,0:T(8,128)(2,1)}, bf16[512,128]{1,0:T(8,128)(2,1)S(1)}, u32[]{:S(2)}, u32[]{:S(2)}) collective-permute-start(bf16[512,128]{1,0:T(8,128)(2,1)} %get-tuple-element.161), channel_id=1, source_target_pairs={{0,2},{2,0},{4,6},{6,4},{8,10},{10,8},{12,14},{14,12},{16,18},{18,... | collective-permute-start | bytes 393224 | tf_op jit(solution)/shard_map/ppermute | solution.py:843
  134.9 8.6 %collective-permute-start.16 = (bf16[512,128]{1,0:T(8,128)(2,1)}, bf16[512,128]{1,0:T(8,128)(2,1)S(1)}, u32[]{:S(2)}, u32[]{:S(2)}) collective-permute-start(bf16[512,128]{1,0:T(8,128)(2,1)} %get-tuple-element.162), channel_id=1, source_target_pairs={{0,4},{2,6},{4,0},{6,2},{8,12},{10,14},{12,8},{14,10},{16,20},{18,... | collective-permute-start | bytes 393224 | tf_op jit(solution)/shard_map/ppermute | solution.py:843
  136.3 7.2 %collective-permute-start.17 = (bf16[512,128]{1,0:T(8,128)(2,1)}, bf16[512,128]{1,0:T(8,128)(2,1)S(1)}, u32[]{:S(2)}, u32[]{:S(2)}) collective-permute-start(bf16[512,128]{1,0:T(8,128)(2,1)} %get-tuple-element.163), channel_id=1, source_target_pairs={{0,6},{2,4},{4,2},{6,0},{8,14},{10,12},{12,10},{14,8},{16,22},{18,... | collective-permute-start | bytes 393224 | tf_op jit(solution)/shard_map/ppermute | solution.py:843
  143.5 47.1 %all-to-all-start.3 = ((bf16[32,8,1280]{2,1,0:T(8,128)(2,1)}), bf16[32,8,1280]{2,1,0:T(8,128)(2,1)S(1)}, u32[]{:S(2)}, u32[]{:S(2)}) async-start(bf16[32,8,1280]{2,1,0:T(8,128)(2,1)} %bitcast.17), calls=%async_computation.3 | async-start | bytes 1310720 | tf_op jit(solution)/shard_map/all_to_all | solution.py:960
  148.4 5.5 %copy-start.18 = (bf16[2,512,128]{2,1,0:T(8,128)(2,1)S(1)}, bf16[2,512,128]{2,1,0:T(8,128)(2,1)}, u32[]{:S(2)}) copy-start(bf16[2,512,128]{2,1,0:T(8,128)(2,1)} %get-tuple-element.185) | copy-start | bytes 786436
  148.4 7.0 %copy-start.17 = (bf16[2,512,128]{2,1,0:T(8,128)(2,1)S(1)}, bf16[2,512,128]{2,1,0:T(8,128)(2,1)}, u32[]{:S(2)}) copy-start(bf16[2,512,128]{2,1,0:T(8,128)(2,1)} %get-tuple-element.186) | copy-start | bytes 786436
  148.4 8.4 %copy-start.16 = (bf16[2,512,128]{2,1,0:T(8,128)(2,1)S(1)}, bf16[2,512,128]{2,1,0:T(8,128)(2,1)}, u32[]{:S(2)}) copy-start(bf16[2,512,128]{2,1,0:T(8,128)(2,1)} %get-tuple-element.187) | copy-start | bytes 786436
  152.4 14.8 %collective-permute-start.23 = (bf16[2,512,128]{2,1,0:T(8,128)(2,1)S(1)}, bf16[2,512,128]{2,1,0:T(8,128)(2,1)S(1)}, u32[]{:S(2)}, u32[]{:S(2)}) collective-permute-start(bf16[2,512,128]{2,1,0:T(8,128)(2,1)S(1)} %get-tuple-element.173), channel_id=1, source_target_pairs={{0,8},{2,10},{4,12},{6,14},{8,0},{10,2},{12,4},{14,6},{16,24},{18,... | collective-permute-start | bytes 786440 | tf_op jit(solution)/shard_map/ppermute | solution.py:843
  153.9 17.3 %collective-permute-start.20 = (bf16[2,512,128]{2,1,0:T(8,128)(2,1)S(1)}, bf16[2,512,128]{2,1,0:T(8,128)(2,1)S(1)}, u32[]{:S(2)}, u32[]{:S(2)}) collective-permute-start(bf16[2,512,128]{2,1,0:T(8,128)(2,1)S(1)} %copy-done.18), channel_id=1, source_target_pairs={{0,2},{2,0},{4,6},{6,4},{8,10},{10,8},{12,14},{14,12},{16,18},{18,... | collective-permute-start | bytes 786440 | tf_op jit(solution)/shard_map/ppermute | solution.py:843
  155.4 16.3 %collective-permute-start.21 = (bf16[2,512,128]{2,1,0:T(8,128)(2,1)S(1)}, bf16[2,512,128]{2,1,0:T(8,128)(2,1)S(1)}, u32[]{:S(2)}, u32[]{:S(2)}) collective-permute-start(bf16[2,512,128]{2,1,0:T(8,128)(2,1)S(1)} %copy-done.17), channel_id=1, source_target_pairs={{0,4},{2,6},{4,0},{6,2},{8,12},{10,14},{12,8},{14,10},{16,20},{18,... | collective-permute-start | bytes 786440 | tf_op jit(solution)/shard_map/ppermute | solution.py:843
  156.8 14.8 %collective-permute-start.22 = (bf16[2,512,128]{2,1,0:T(8,128)(2,1)S(1)}, bf16[2,512,128]{2,1,0:T(8,128)(2,1)S(1)}, u32[]{:S(2)}, u32[]{:S(2)}) collective-permute-start(bf16[2,512,128]{2,1,0:T(8,128)(2,1)S(1)} %copy-done.16), channel_id=1, source_target_pairs={{0,6},{2,4},{4,2},{6,0},{8,14},{10,12},{12,10},{14,8},{16,22},{18,... | collective-permute-start | bytes 786440 | tf_op jit(solution)/shard_map/ppermute | solution.py:843
  168.8 8.5 %collective-permute-start.25 = (bf16[1,512,128]{2,1,0:T(8,128)(2,1)S(1)}, bf16[1,512,128]{2,1,0:T(8,128)(2,1)S(1)}, u32[]{:S(2)}, u32[]{:S(2)}) collective-permute-start(bf16[1,512,128]{2,1,0:T(8,128)(2,1)S(1)} %get-tuple-element.190), channel_id=1, source_target_pairs={{0,16},{2,18},{4,20},{6,22},{8,24},{10,26},{12,28},{14,30},{16,0},... | collective-permute-start | bytes 393224 | tf_op jit(solution)/shard_map/ppermute | solution.py:843
  176.0 9.7 %collective-permute-start.24 = (bf16[2,512,128]{2,1,0:T(8,128)(2,1)S(1)}, bf16[2,512,128]{2,1,0:T(8,128)(2,1)S(1)}, u32[]{:S(2)}, u32[]{:S(2)}) collective-permute-start(bf16[2,512,128]{2,1,0:T(8,128)(2,1)S(1)} %get-tuple-element.195), channel_id=1, source_target_pairs={{0,8},{2,10},{4,12},{6,14},{8,0},{10,2},{12,4},{14,6},{16,24},{18,... | collective-permute-start | bytes 786440 | tf_op jit(solution)/shard_map/ppermute | solution.py:843
  178.2 9.1 %collective-permute-start.27 = (bf16[512,128]{1,0:T(8,128)(2,1)S(1)}, bf16[512,128]{1,0:T(8,128)(2,1)S(1)}, u32[]{:S(2)}, u32[]{:S(2)}) collective-permute-start(bf16[512,128]{1,0:T(8,128)(2,1)S(1)} %last_add.1.own_ref), channel_id=1, source_target_pairs={{0,16},{2,18},{4,20},{6,22},{8,24},{10,26},{12,28},{14,30},{16,0},... | collective-permute-start | bytes 393224 | tf_op jit(solution)/shard_map/ppermute | solution.py:843
  187.4 9.5 %collective-permute-start.31 = (bf16[1024,128]{1,0:T(8,128)(2,1)S(1)}, bf16[1024,128]{1,0:T(8,128)(2,1)S(1)}, u32[]{:S(2)}, u32[]{:S(2)}) collective-permute-start(bf16[1024,128]{1,0:T(8,128)(2,1)S(1)} %stack.20.own_ref), channel_id=1, source_target_pairs={{0,8},{2,10},{4,12},{6,14},{8,0},{10,2},{12,4},{14,6},{16,24},{18,... | collective-permute-start | bytes 786440 | tf_op jit(solution)/shard_map/ppermute | solution.py:843
  188.5 6.6 %collective-permute-start.26 = (bf16[1,512,128]{2,1,0:T(8,128)(2,1)S(1)}, bf16[1,512,128]{2,1,0:T(8,128)(2,1)S(1)}, u32[]{:S(2)}, u32[]{:S(2)}) collective-permute-start(bf16[1,512,128]{2,1,0:T(8,128)(2,1)S(1)} %get-tuple-element.200), channel_id=1, source_target_pairs={{0,16},{2,18},{4,20},{6,22},{8,24},{10,26},{12,28},{14,30},{16,0},... | collective-permute-start | bytes 393224 | tf_op jit(solution)/shard_map/ppermute | solution.py:843
  190.7 4.4 %collective-permute-start.29 = (f32[16,128]{1,0:T(8,128)S(1)}, f32[16,128]{1,0:T(8,128)S(1)}, u32[]{:S(2)}, u32[]{:S(2)}) collective-permute-start(f32[16,128]{1,0:T(8,128)S(1)} %get-tuple-element.204.refs_2_), channel_id=1, source_target_pairs={{0,1},{1,0},{2,3},{3,2},{4,5},{5,4},{6,7},{7,6},{8,9},{9,8},{10,11... | collective-permute-start | bytes 24584 | tf_op jit(solution)/shard_map/ppermute | solution.py:843
  190.7 12.7 %copy-start.14 = (bf16[320,1024]{1,0:T(8,128)(2,1)S(1)}, bf16[320,1024]{1,0:T(8,128)(2,1)}, u32[]{:S(2)}) copy-start(bf16[320,1024]{1,0:T(8,128)(2,1)} %get-tuple-element.176) | copy-start | bytes 1966084
  194.6 1.3 collective-permute-start.28
  197.0 23.8 %copy-start.13 = (bf16[320,1024]{1,0:T(8,128)(2,1)S(1)}, bf16[320,1024]{1,0:T(8,128)(2,1)}, u32[]{:S(2)}) copy-start(bf16[320,1024]{1,0:T(8,128)(2,1)} %get-tuple-element.175) | copy-start | bytes 1966084
  197.0 14.2 %collective-permute-start.33 = (bf16[2048,128]{1,0:T(8,128)(2,1)S(1)}, bf16[2048,128]{1,0:T(8,128)(2,1)S(1)}, u32[]{:S(2)}, u32[]{:S(2)}) collective-permute-start(bf16[2048,128]{1,0:T(8,128)(2,1)S(1)} %stack.21.refs_0_), channel_id=1, source_target_pairs={{0,2},{2,0},{4,6},{6,4},{8,10},{10,8},{12,14},{14,12},{16,18},{18,... | collective-permute-start | bytes 1572872 | tf_op jit(solution)/shard_map/ppermute | solution.py:843
  198.5 13.9 %collective-permute-start.34 = (bf16[2048,128]{1,0:T(8,128)(2,1)S(1)}, bf16[2048,128]{1,0:T(8,128)(2,1)S(1)}, u32[]{:S(2)}, u32[]{:S(2)}) collective-permute-start(bf16[2048,128]{1,0:T(8,128)(2,1)S(1)} %stack.21.refs_0_), channel_id=1, source_target_pairs={{0,4},{2,6},{4,0},{6,2},{8,12},{10,14},{12,8},{14,10},{16,20},{18,... | collective-permute-start | bytes 1572872 | tf_op jit(solution)/shard_map/ppermute | solution.py:843
  201.2 8.4 %collective-permute-start.30 = (bf16[576,128]{1,0:T(8,128)(2,1)S(1)}, bf16[576,128]{1,0:T(8,128)(2,1)S(1)}, u32[]{:S(2)}, u32[]{:S(2)}) collective-permute-start(bf16[576,128]{1,0:T(8,128)(2,1)S(1)} %last_add_sums.1.own_ref), channel_id=1, source_target_pairs={{0,16},{2,18},{4,20},{6,22},{8,24},{10,26},{12,28},{14,30},{16,0},... | collective-permute-start | bytes 442376 | tf_op jit(solution)/shard_map/ppermute | solution.py:843
  203.4 17.3 %collective-permute-start.18 = (bf16[320,1024]{1,0:T(8,128)(2,1)S(1)}, bf16[320,1024]{1,0:T(8,128)(2,1)S(1)}, u32[]{:S(2)}, u32[]{:S(2)}) collective-permute-start(bf16[320,1024]{1,0:T(8,128)(2,1)S(1)} %copy-done.14), channel_id=1, source_target_pairs={{0,1},{1,0},{2,3},{3,2},{4,5},{5,4},{6,7},{7,6},{8,9},{9,8},{10,11... | collective-permute-start | bytes 1966088 | tf_op jit(solution)/shard_map/ppermute | solution.py:843
  209.6 6.6 %collective-permute-start.32 = (bf16[1088,128]{1,0:T(8,128)(2,1)S(1)}, bf16[1088,128]{1,0:T(8,128)(2,1)S(1)}, u32[]{:S(2)}, u32[]{:S(2)}) collective-permute-start(bf16[1088,128]{1,0:T(8,128)(2,1)S(1)} %stack.22.own_ref), channel_id=1, source_target_pairs={{0,8},{2,10},{4,12},{6,14},{8,0},{10,2},{12,4},{14,6},{16,24},{18,... | collective-permute-start | bytes 835592 | tf_op jit(solution)/shard_map/ppermute | solution.py:843
  216.3 17.9 %collective-permute-start.35 = (bf16[2112,128]{1,0:T(8,128)(2,1)S(1)}, bf16[2112,128]{1,0:T(8,128)(2,1)S(1)}, u32[]{:S(2)}, u32[]{:S(2)}) collective-permute-start(bf16[2112,128]{1,0:T(8,128)(2,1)S(1)} %stack.23.refs_0_), channel_id=1, source_target_pairs={{0,2},{2,0},{4,6},{6,4},{8,10},{10,8},{12,14},{14,12},{16,18},{18,... | collective-permute-start | bytes 1622024 | tf_op jit(solution)/shard_map/ppermute | solution.py:843
  216.7 17.4 %collective-permute-start.36 = (bf16[2112,128]{1,0:T(8,128)(2,1)S(1)}, bf16[2112,128]{1,0:T(8,128)(2,1)S(1)}, u32[]{:S(2)}, u32[]{:S(2)}) collective-permute-start(bf16[2112,128]{1,0:T(8,128)(2,1)S(1)} %stack.23.refs_0_), channel_id=1, source_target_pairs={{0,4},{2,6},{4,0},{6,2},{8,12},{10,14},{12,8},{14,10},{16,20},{18,... | collective-permute-start | bytes 1622024 | tf_op jit(solution)/shard_map/ppermute | solution.py:843
  218.4 13.0 %collective-permute-start.37 = (bf16[1024,128]{1,0:T(8,128)(2,1)S(1)}, bf16[1024,128]{1,0:T(8,128)(2,1)S(1)}, u32[]{:S(2)}, u32[]{:S(2)}) collective-permute-start(bf16[1024,128]{1,0:T(8,128)(2,1)S(1)} %slice.32), channel_id=1, source_target_pairs={{0,2},{2,0},{4,6},{6,4},{8,10},{10,8},{12,14},{14,12},{16,18},{18,... | collective-permute-start | bytes 786440 | tf_op jit(solution)/shard_map/ppermute | solution.py:843
  219.1 15.0 %collective-permute-start.38 = (bf16[1024,128]{1,0:T(8,128)(2,1)S(1)}, bf16[1024,128]{1,0:T(8,128)(2,1)S(1)}, u32[]{:S(2)}, u32[]{:S(2)}) collective-permute-start(bf16[1024,128]{1,0:T(8,128)(2,1)S(1)} %slice.33), channel_id=1, source_target_pairs={{0,4},{2,6},{4,0},{6,2},{8,12},{10,14},{12,8},{14,10},{16,20},{18,... | collective-permute-start | bytes 786440 | tf_op jit(solution)/shard_map/ppermute | solution.py:843
  234.2 6.9 %collective-permute-start.39 = (bf16[1056,128]{1,0:T(8,128)(2,1)S(1)}, bf16[1056,128]{1,0:T(8,128)(2,1)S(1)}, u32[]{:S(2)}, u32[]{:S(2)}) collective-permute-start(bf16[1056,128]{1,0:T(8,128)(2,1)S(1)} %slice.34), channel_id=1, source_target_pairs={{0,2},{2,0},{4,6},{6,4},{8,10},{10,8},{12,14},{14,12},{16,18},{18,... | collective-permute-start | bytes 811016 | tf_op jit(solution)/shard_map/ppermute | solution.py:843
  234.5 6.6 %collective-permute-start.40 = (bf16[1056,128]{1,0:T(8,128)(2,1)S(1)}, bf16[1056,128]{1,0:T(8,128)(2,1)S(1)}, u32[]{:S(2)}, u32[]{:S(2)}) collective-permute-start(bf16[1056,128]{1,0:T(8,128)(2,1)S(1)} %slice.35), channel_id=1, source_target_pairs={{0,4},{2,6},{4,0},{6,2},{8,12},{10,14},{12,8},{14,10},{16,20},{18,... | collective-permute-start | bytes 811016 | tf_op jit(solution)/shard_map/ppermute | solution.py:843

commit v3 on v2

--- a/solution.py
+++ b/solution.py
@@ -105,7 +105,10 @@
 
 
 def gather_kernel(packed_ref, dispatch_ref, out_ref, *, cap):
-    out_ref[...] = unpack(packed_ref, dispatch_ref[...], cap, out_ref.shape[1]).astype(BF16)
+    count = dispatch_ref.shape[1]
+    along = jnp.broadcast_to(dispatch_ref[...].astype(F32), (128, count))
+    slot_of = along.T[:, :1].astype(jnp.int32)
+    out_ref[...] = unpack(packed_ref, slot_of, cap, out_ref.shape[1]).astype(BF16)
 
 
 def two_heads(rows):
@@ -663,7 +666,7 @@
 
 
 def finish_far_kernel(where_ref, *refs, digits, sums):
-    halves, near_sums_ref, _, qkv_far, sums_ref, total_ref, sem = refs[:2], *refs[2:]
+    halves, near_sums_ref, _, qkv_far, *sums_refs, total_ref, sem = refs[:2], *refs[2:]
     width = total_ref.shape[1]
     rows = width // 4 ** (digits - 1)
 
@@ -676,7 +679,10 @@
     lanes = pl.ds(pl.multiple_of((where_ref[1] ^ 3) * 128, 128), 128)
     leaving = started(total_ref, qkv_far.at[pl.ds(0, 2), :, lanes], sem)
     half = halves[1].shape[0]
-    sums_ref[...] = near_sums_ref[...] + split_sum(halves[1:], half - sums, half)
+    total_sums = near_sums_ref[...] + split_sum(halves[1:], half - sums, half)
+    count = total_sums.shape[0] // len(sums_refs)
+    for at, sums_ref in enumerate(sums_refs):
+        sums_ref[...] = total_sums[at * count : (at + 1) * count]
     leaving.wait()
 
 
@@ -788,7 +794,7 @@
             flops=12 * count * width * units, bytes_accessed=16 * MIB, transcendentals=0
         ),
         compiler_params=pltpu.CompilerParams(vmem_limit_bytes=40 * MIB),
-    )(h2, h2_other, upstream, upstream_other, far(w_up), far(w_down))
+    )(h2, h2_other, upstream, upstream_other, w_up, w_down)
 
 
 def expert_grads(rows, grads, hidden, dpre):
@@ -953,7 +959,7 @@
     moving = 2 * devices * 8 * max(slots, seq_rows) * width * 3
     gain1, bias1 = ln1_gain.reshape(1, width), ln1_bias.reshape(1, width)
     gain2, bias2 = ln2_gain.reshape(1, width), ln2_bias.reshape(1, width)
-    down, along = dispatch.reshape(seq_rows, 1), dispatch.reshape(1, seq_rows)
+    along = dispatch.reshape(1, seq_rows)
 
     def exchange(value):
         value = value.reshape(devices, 8, cap * 128)
@@ -970,7 +976,7 @@
     arrived = exchange(h1)
     (own,) = call(
         functools.partial(gather_kernel, cap=cap), "gather1", [((seq_rows, width), BF16)],
-        [arrived, down], moving,
+        [arrived, along], moving,
     )
     other = cross(own)
     own_copy, inputs, qkv, context, logsum, attn_kept, attn_sent = call(
@@ -1040,7 +1046,7 @@
     plane_other = [cross(by_x), cross(by_y), far_other]
     (own,) = call(
         functools.partial(gather_kernel, cap=cap), "gather2", [((seq_rows, width), BF16)],
-        [arrived, down], moving,
+        [arrived, along], moving,
     )
     other = cross(own)
     piece = 4 * width // n_exp
@@ -1180,18 +1186,18 @@
         compiler_params=pltpu.CompilerParams(vmem_limit_bytes=20 * MIB),
     )(where, *key_query[:3], grad_qkv)
     halves = after_all(key_query[3:], sums)
-    grad_qkv, sums = pl.pallas_call(
+    grad_qkv, *sums = pl.pallas_call(
         functools.partial(finish_far_kernel, digits=digits, sums=extra),
         name="finish_far",
-        out_shape=[whole_qkv, sums_shape],
+        out_shape=[whole_qkv, *[jax.ShapeDtypeStruct((width // 128, 128), F32)] * 4],
         in_specs=[SMEM] + [VMEM] * 3 + [in_place],
-        out_specs=[in_place, VMEM],
+        out_specs=[in_place, *[VMEM] * 4],
         scratch_shapes=[pltpu.VMEM((2, width, 128), F32), pltpu.SemaphoreType.DMA],
         input_output_aliases={4: 0},
         cost_estimate=pl.CostEstimate(flops=0, bytes_accessed=2 * MIB, transcendentals=0),
         compiler_params=pltpu.CompilerParams(vmem_limit_bytes=16 * MIB),
     )(where, *halves, sums, grad_qkv)
-    sums = sums.reshape(4, width)
+    sums = [total.reshape(width) for total in sums]
     return (
         result,
         input_grad,

time: 244 us -> 244 us (level)
  blocking collectives: 21.2 us -> 46.3 us
  waiting for transfers between devices: 70.4 us -> 53.5 us
  starting transfers between devices: 57 us -> 50.4 us
    all_to_all x1 -> x2, blocking collectives: 21.2 us -> 46.3 us  [exchange(): lax.all_to_all(value, ('exp', 'head'), split_axis=0, concat_axis=0, tiled...]
    all_to_all x3 -> x2, waiting for transfers between devices: 17.8 us -> 0.01 us  [exchange(): lax.all_to_all(value, ('exp', 'head'), split_axis=0, concat_axis=0, tiled...]
    all_to_all x3 -> x2, starting transfers between devices: 15.9 us -> 8.57 us  [exchange(): lax.all_to_all(value, ('exp', 'head'), split_axis=0, concat_axis=0, tiled...]
  transfers between devices with their start and end apart: 44 -> 43, of which waited for: 22 -> 24; matrix products, arithmetic and copies ran while one was open for 1% -> 1% of each run, Pallas kernels for 29% -> 28%
where the time goes in v3:
time: 244 us; the launch traced here: 243 us
  Pallas kernels  88.7 us (36%)
  waiting for transfers between devices  53.5 us (22%)
  starting transfers between devices  50.4 us (21%)
  blocking collectives  46.3 us (19%)
    ppermute x41, waiting for transfers between devices, flip(): return lax.ppermute(value, axis, [(i, i ^ bit) for i in range(size)])  53.4 us
    pallas_call x21, Pallas kernels, call(): pl.pallas_call(kernel, name=name, out_shape=shapes, in_specs=[SMEM if at...  48.8 us
    all_to_all x2, blocking collectives, exchange(): lax.all_to_all(value, ('exp', 'head'), split_axis=0, concat_axis=0, tiled...  46.3 us
    ppermute x41, starting transfers between devices, flip(): return lax.ppermute(value, axis, [(i, i ^ bit) for i in range(size)])  41.9 us
    pallas_call x1, Pallas kernels, expert(): pl.pallas_call(expert_kernel, name='expert', grid=(units // tile,), out_s...  11.9 us
    pallas_call x1, Pallas kernels, expert_grads(): pl.pallas_call(expert_grad_kernel, name='expert_grads', grid=(units // ti...  11.6 us
    all_to_all x2, starting transfers between devices, exchange(): lax.all_to_all(value, ('exp', 'head'), split_axis=0, concat_axis=0, tiled...  8.57 us
    pallas_call x1, Pallas kernels, expert_branch(): pl.pallas_call(branch_kernel, name='expert_branch', grid=(units // tile,)...  6.91 us
  transfers between devices with their start and end apart: 43, of which 24 were waited for; matrix products, arithmetic and copies ran while one was open for 1% of the time, Pallas kernels for 28%

profile of v3, /device:TPU:0, one launch (start us, length us, event | category | flops | bytes accessed | tf_op | source)
XLA Modules:
  0.0 243.1 jit_solution(15349008050849132917)
XLA Ops:
  0.7 2.5 %norm1.1 = bf16[256,1280]{1,0:T(8,128)(2,1)S(1)} custom-call(bf16[320,1024]{1,0:T(8,128)(2,1)} %x_ref.5, f32[1,1024]{1,0:T(1,128)} %bitcast.40, f32[1,1024]{1,0:T(1,128)} %bitcast.42), custom_call_target="tpu_custom_call" | custom-call | flops 503316480 | bytes 1318912 | tf_op jit(solution)/shard_map/norm1/pallas_call | solution.py:746
  3.2 25.0 %all_to_all.20 = bf16[32,8,1280]{2,1,0:T(8,128)(2,1)S(1)} all-to-all(bf16[32,8,1280]{2,1,0:T(8,128)(2,1)S(1)} %bitcast.29), channel_id=1, replica_groups=mesh['exp'=16,'head'=2] {'exp','head'}, dimensions={0} | all-to-all | bytes 1310720 | tf_op jit(solution)/shard_map/all_to_all | solution.py:966
  29.2 1.8 collective-permute-done.other_ref
  30.9 8.5 %attend.1 = (bf16[256,1024]{1,0:T(8,128)(2,1)}, bf16[512,1024]{1,0:T(8,128)(2,1)}, bf16[3,512,512]{2,1,0:T(8,128)(2,1)}, bf16[512,512]{1,0:T(8,128)(2,1)}, f32[1...) custom-call(s32[3]{0:T(128)S(1)} %pad_add_fusion.where_ref, s32[1,5]{1,0:T(1,128)S(1)} %copy-done.7, ...), custom_call_target="tpu_custom_call" | custom-call | flops 4294967296 | bytes 10747936 | tf_op jit(solution)/shard_map/attend/pallas_call | solution.py:746
  39.6 1.8 collective-permute-done.1.came_ref
  42.1 21.2 %all_to_all.21 = bf16[32,8,1280]{2,1,0:T(8,128)(2,1)S(1)} all-to-all(bf16[32,8,1280]{2,1,0:T(8,128)(2,1)S(1)} %bitcast.26), channel_id=1, replica_groups=mesh['exp'=16,'head'=2] {'exp','head'}, dimensions={0} | all-to-all | bytes 1310720 | tf_op jit(solution)/shard_map/all_to_all | solution.py:966
  63.3 1.2 norm2.1
  65.1 2.3 collective-permute-start.4
  67.6 11.9 %expert.1 = (bf16[640,2048]{1,0:T(8,128)(2,1)}, bf16[640,2048]{1,0:T(8,128)(2,1)}, f32[320,1024]{1,0:T(8,128)S(1)}, bf16[320,1024]{1,0:T(8,128)(2,1)S(1)}, bf16[...) custom-call(bf16[320,1024]{1,0:T(8,128)(2,1)S(1)} %get-tuple-element.127.h2_ref, ...), custom_call_target="tpu_custom_call" | custom-call | flops 8053063680 | bytes 16777216 | tf_op jit(solution)/shard_map/expert/pallas_call | solution.py:776
  80.1 2.1 collective-permute-done.5.came_ref
  82.2 3.1 %norm2_back.1 = (f32[320,1024]{1,0:T(8,128)}, bf16[256,1280]{1,0:T(8,128)(2,1)}, f32[16,128]{1,0:T(8,128)S(1)}) custom-call(f32[320,1024]{1,0:T(8,128)S(1)} %get-tuple-element.131.kept_ref, bf16[320,1024]{1,0:T(8,128)(2,1)S(1)} %collective-permute-done.5.came_ref, f32[320,1024]{1,0:T(8,128)S(1)} %get-tuple-element.124.resid_ref, ...), custom_call_target="tpu_custom_call" | custom-call | flops 503316480 | bytes 5910528 | tf_op jit(solution)/shard_map/norm2_back/pallas_call | solution.py:746
  85.4 3.7 %all-to-all-start.2 = ((bf16[32,8,1280]{2,1,0:T(8,128)(2,1)}), bf16[32,8,1280]{2,1,0:T(8,128)(2,1)S(1)}, u32[]{:S(2)}, u32[]{:S(2)}) async-start(bf16[32,8,1280]{2,1,0:T(8,128)(2,1)} %bitcast.14), calls=%async_computation.2 | async-start | bytes 1310720 | tf_op jit(solution)/shard_map/all_to_all | solution.py:966
  89.1 1.6 collective-permute-start.6
  90.7 1.5 collective-permute-start.7
  92.2 11.6 %expert_grads.1 = (f32[1024,2048]{1,0:T(8,128)}, f32[2048,1024]{1,0:T(8,128)}) custom-call(bf16[640,1024]{1,0:T(8,128)(2,1)} %get-tuple-element.136.rows_ref, bf16[640,1024]{1,0:T(8,128)(2,1)} %get-tuple-element.137.grads_ref, bf16[640,2048]{1,0:T(8,128)(2,1)} %get-tuple-element.177.hidden_ref, bf16[640,2048]{1,0:T(8,128)(2,1)} %get-tuple-element.138.dpre_ref), custom_call_target="tpu_custom_call" | custom-call | flops 5368709120 | bytes 25165824 | tf_op jit(solution)/shard_map/expert_grads/pallas_call | solution.py:806
  103.8 6.2 %collective-permute-done.6.refs_5_ = bf16[256,1024]{1,0:T(8,128)(2,1)S(1)} collective-permute-done((bf16[256,1024]{1,0:T(8,128)(2,1)S(1)}, bf16[256,1024]{1,0:T(8,128)(2,1)S(1)}, u32[]{:S(2)}, u32[]{:S(2)}) %collective-permute-start.6) | collective-permute-done | bytes 524320 | tf_op jit(solution)/shard_map/ppermute | solution.py:849
  113.2 1.2 collective-permute-done.9.other_ref
  114.4 3.4 %out_grad.1 = (bf16[512,1024]{1,0:T(8,128)(2,1)S(1)}, bf16[4,256,128]{2,1,0:T(8,128)(2,1)}, bf16[4,256,128]{2,1,0:T(8,128)(2,1)}, bf16[4,256,128]{2,1,0:T(8,128)(2,1)}, bf16[4,256,128]{2,1,0:T(8,128)(2,1)}) custom-call(s32[3]{0:T(128)S(1)} %pad_add_fusion.where_ref, bf16[256,1024]{1,0:T(8,128)(2,1)S(1)} %gather2.1.own_ref, ...), custom_call_target="tpu_custom_call" | custom-call | flops 536870912 | bytes 3670028 | tf_op jit(solution)/shard_map/out_grad/pallas_call | solution.py:746
  118.5 1.4 collective-permute-start.11
  119.8 1.5 collective-permute-start.12
  121.3 8.9 %attend_back.1 = (f32[256,1024]{1,0:T(8,128)S(1)}, bf16[256,1024]{1,0:T(8,128)(2,1)S(1)}, bf16[512,128]{1,0:T(8,128)(2,1)}, bf16[512,128]{1,0:T(8,128)(2,1)}, bf...) custom-call(s32[3]{0:T(128)S(1)} %pad_add_fusion.where_ref, ...), custom_call_target="tpu_custom_call" | custom-call | flops 7516192768 | bytes 10747936 | tf_op jit(solution)/shard_map/attend_back/pallas_call | solution.py:746
  130.3 1.1 collective-permute-done.11.refs_13_
  131.4 1.5 collective-permute-done.12.refs_14_
  133.7 1.5 collective-permute-start.16
  135.2 1.2 collective-permute-start.17
  136.4 1.4 scatter2.1
  137.8 1.6 collective-permute-done.15.refs_1_
  139.4 3.0 %collective-permute-done.16.refs_2_ = bf16[512,128]{1,0:T(8,128)(2,1)S(1)} collective-permute-done((bf16[512,128]{1,0:T(8,128)(2,1)}, bf16[512,128]{1,0:T(8,128)(2,1)S(1)}, u32[]{:S(2)}, u32[]{:S(2)}) %collective-permute-start.16) | collective-permute-done | bytes 131104 | tf_op jit(solution)/shard_map/ppermute | solution.py:849
  142.4 4.8 %all-to-all-start.3 = ((bf16[32,8,1280]{2,1,0:T(8,128)(2,1)}), bf16[32,8,1280]{2,1,0:T(8,128)(2,1)S(1)}, u32[]{:S(2)}, u32[]{:S(2)}) async-start(bf16[32,8,1280]{2,1,0:T(8,128)(2,1)} %bitcast.16), calls=%async_computation.3 | async-start | bytes 1310720 | tf_op jit(solution)/shard_map/all_to_all | solution.py:966
  147.3 4.0 %value_grad.1 = (bf16[2,512,128]{2,1,0:T(8,128)(2,1)}, bf16[2,512,128]{2,1,0:T(8,128)(2,1)S(1)}) custom-call(s32[3]{0:T(128)S(1)} %pad_add_fusion.where_ref, bf16[512,128]{1,0:T(8,128)(2,1)} %get-tuple-element.163.refs_0_, bf16[512,128]{1,0:T(8,128)(2,1)S(1)} %collective-permute-done.15.refs_1_, bf16[512,128]{1,0:T(8,128)(2,1)S(1)} %collective-permute-done.16.refs_2_, ...), custom_call_target="tpu_custom_call" | custom-call | flops 536870912 | bytes 6291468 | tf_op jit(solution)/shard_map/value_grad/pallas_call | solution.py:746
  151.3 1.5 collective-permute-start.23
  152.8 1.5 collective-permute-start.20
  154.3 1.5 collective-permute-start.21
  156.3 6.9 %expert_branch.1 = (bf16[320,1024]{1,0:T(8,128)(2,1)}, bf16[320,1024]{1,0:T(8,128)(2,1)}) custom-call(bf16[640,2048]{1,0:T(8,128)(2,1)} %get-tuple-element.177.hidden_ref, bf16[2048,1024]{1,0:T(8,128)(2,1)} %bitcast.38), custom_call_target="tpu_custom_call" | custom-call | flops 2684354560 | bytes 8388608 | tf_op jit(solution)/shard_map/expert_branch/pallas_call | solution.py:829
  163.2 2.8 %collective-permute-done.23.came_ref = bf16[2,512,128]{2,1,0:T(8,128)(2,1)S(1)} collective-permute-done((bf16[2,512,128]{2,1,0:T(8,128)(2,1)S(1)}, bf16[2,512,128]{2,1,0:T(8,128)(2,1)S(1)}, u32[]{:S(2)}, u32[]{:S(2)}) %collective-permute-start.23) | collective-permute-done | bytes 262176 | tf_op jit(solution)/shard_map/ppermute | solution.py:849
  166.0 1.7 add.17
  167.7 2.4 collective-permute-start.25
  170.5 4.4 %key_query_grad.1 = (bf16[2,512,128]{2,1,0:T(8,128)(2,1)}, bf16[2,512,128]{2,1,0:T(8,128)(2,1)S(1)}) custom-call(s32[3]{0:T(128)S(1)} %pad_add_fusion.where_ref, bf16[2,512,128]{2,1,0:T(8,128)(2,1)} %get-tuple-element.184.refs_0_, bf16[2,512,128]{2,1,0:T(8,128)(2,1)S(1)} %collective-permute-done.20.refs_1_, ...), custom_call_target="tpu_custom_call" | custom-call | flops 1073741824 | bytes 5767180 | tf_op jit(solution)/shard_map/key_query_grad/pallas_call | solution.py:746
  174.9 1.1 collective-permute-start.24
  177.1 1.7 collective-permute-start.27
  178.8 5.7 %collective-permute-done.24.came_ref = bf16[2,512,128]{2,1,0:T(8,128)(2,1)S(1)} collective-permute-done((bf16[2,512,128]{2,1,0:T(8,128)(2,1)S(1)}, bf16[2,512,128]{2,1,0:T(8,128)(2,1)S(1)}, u32[]{:S(2)}, u32[]{:S(2)}) %collective-permute-start.24) | collective-permute-done | bytes 262176 | tf_op jit(solution)/shard_map/ppermute | solution.py:849
  184.5 1.7 add.18
  186.2 1.2 collective-permute-start.31
  187.4 2.1 collective-permute-start.26
  189.5 3.9 %norm1_back.1 = (f32[320,1024]{1,0:T(8,128)}, f32[16,128]{1,0:T(8,128)S(1)}) custom-call(bf16[256,1280]{1,0:T(8,128)(2,1)S(1)} %bitcast.24, bf16[320,1024]{1,0:T(8,128)(2,1)} %x_ref.5, f32[320,1024]{1,0:T(8,128)} %get-tuple-element.182.dresid_ref, f32[1,1024]{1,0:T(1,128)} %bitcast.41), custom_call_target="tpu_custom_call" | custom-call | flops 503316480 | bytes 3944448 | tf_op jit(solution)/shard_map/norm1_back/pallas_call | solution.py:746
  194.8 0.9 last_add_sums.1.own_ref
  195.8 1.5 collective-permute-start.33
  197.3 2.8 %collective-permute-start.34 = (bf16[2048,128]{1,0:T(8,128)(2,1)S(1)}, bf16[2048,128]{1,0:T(8,128)(2,1)S(1)}, u32[]{:S(2)}, u32[]{:S(2)}) collective-permute-start(bf16[2048,128]{1,0:T(8,128)(2,1)S(1)} %stack.21.refs_0_), channel_id=1, source_target_pairs={{0,4},{2,6},{4,0},{6,2},{8,12},{10,14},{12,8},{14,10},{16,20},{18,... | collective-permute-start | bytes 1572872 | tf_op jit(solution)/shard_map/ppermute | solution.py:849
  200.1 2.2 collective-permute-start.30
  202.3 6.2 %collective-permute-done.30.came_ref = bf16[576,128]{1,0:T(8,128)(2,1)S(1)} collective-permute-done((bf16[576,128]{1,0:T(8,128)(2,1)S(1)}, bf16[576,128]{1,0:T(8,128)(2,1)S(1)}, u32[]{:S(2)}, u32[]{:S(2)}) %collective-permute-start.30) | collective-permute-done | bytes 147488 | tf_op jit(solution)/shard_map/ppermute | solution.py:849
  208.6 1.5 collective-permute-done.33.refs_1_
  210.0 1.2 collective-permute-done.34.refs_2_
  211.2 3.9 %collective-permute-done.32.came_ref = bf16[1088,128]{1,0:T(8,128)(2,1)S(1)} collective-permute-done((bf16[1088,128]{1,0:T(8,128)(2,1)S(1)}, bf16[1088,128]{1,0:T(8,128)(2,1)S(1)}, u32[]{:S(2)}, u32[]{:S(2)}) %collective-permute-start.32) | collective-permute-done | bytes 278560 | tf_op jit(solution)/shard_map/ppermute | solution.py:849
  215.7 1.4 collective-permute-start.36
  217.3 1.4 collective-permute-start.37
  219.6 1.1 add_convert_fusion
  220.7 2.8 %finish_out_value_near.1 = (f32[3,1024,512]{2,1,0:T(8,128)}, f32[512,1024]{1,0:T(8,128)}) custom-call(s32[3]{0:T(128)S(1)} %pad_add_fusion.where_ref, bf16[2048,128]{1,0:T(8,128)(2,1)S(1)} %stack.21.refs_0_, bf16[2048,128]{1,0:T(8,128)(2,1)S(1)} %collective-permute-done.33.refs_1_, bf16[2048,128]{1,0:T(8,128)(2,1)S(1)} %collective-permute-done.34.refs_2_), custom_call_target="tpu_custom_call" | custom-call | bytes 6291456 | tf_op jit(solution)/shard_map/finish_out_value_near/pallas_call | solution.py:904
  223.5 6.8 %collective-permute-done.37.refs_0_ = bf16[1024,128]{1,0:T(8,128)(2,1)S(1)} collective-permute-done((bf16[1024,128]{1,0:T(8,128)(2,1)S(1)}, bf16[1024,128]{1,0:T(8,128)(2,1)S(1)}, u32[]{:S(2)}, u32[]{:S(2)}) %collective-permute-start.37) | collective-permute-done | bytes 262176 | tf_op jit(solution)/shard_map/ppermute | solution.py:849
  230.3 2.5 %collective-permute-done.38.refs_1_ = bf16[1024,128]{1,0:T(8,128)(2,1)S(1)} collective-permute-done((bf16[1024,128]{1,0:T(8,128)(2,1)S(1)}, bf16[1024,128]{1,0:T(8,128)(2,1)S(1)}, u32[]{:S(2)}, u32[]{:S(2)}) %collective-permute-start.38) | collective-permute-done | bytes 262176 | tf_op jit(solution)/shard_map/ppermute | solution.py:849
  232.9 1.3 collective-permute-start.39
  234.2 1.8 collective-permute-start.40
  236.0 1.6 finish_out_value_far.1
  237.6 3.0 %finish_near.1 = (f32[3,1024,512]{2,1,0:T(8,128)}, f32[32,128]{1,0:T(8,128)S(1)}) custom-call(s32[3]{0:T(128)S(1)} %pad_add_fusion.where_ref, bf16[2112,128]{1,0:T(8,128)(2,1)S(1)} %stack.23.refs_0_, bf16[2112,128]{1,0:T(8,128)(2,1)S(1)} %collective-permute-done.35.refs_1_, ...), custom_call_target="tpu_custom_call", output_to_operand_aliasing={{0}: (4, {})} | custom-call | bytes 6291456 | tf_op jit(solution)/shard_map/finish_near/pallas_call | solution.py:1174
  240.7 2.2 finish_far.1
  (101 shorter events, 13.5 us)
Async XLA Ops:
  0.6 27.5 %copy-start.4 = (s32[256]{0:T(256)S(1)}, s32[256]{0:T(256)}, u32[]{:S(2)}) copy-start(s32[256]{0:T(256)} %param.13) | copy-start | bytes 3076
  3.2 27.8 %copy-start.7 = (s32[1,5]{1,0:T(1,128)S(1)}, s32[1,5]{1,0:T(1,128)}, u32[]{:S(2)}) copy-start(s32[1,5]{1,0:T(1,128)} %lengths_ref.3) | copy-start | bytes 64
  29.0 2.0 collective-permute-start
  30.9 36.7 %copy-start.6 = (bf16[1,2048,1024]{2,1,0:T(8,128)(2,1)S(1)}, bf16[1,2048,1024]{2,1,0:T(8,128)(2,1)}, u32[]{:S(2)}) copy-start(bf16[1,2048,1024]{2,1,0:T(8,128)(2,1)} %param.22) | copy-start | bytes 12582916
  39.4 2.0 collective-permute-start.1
  41.4 21.9 %copy-start = (bf16[320,1024]{1,0:T(8,128)(2,1)S(1)}, bf16[320,1024]{1,0:T(8,128)(2,1)}, u32[]{:S(2)}) copy-start(bf16[320,1024]{1,0:T(8,128)(2,1)} %x_ref.5) | copy-start | bytes 1966084
  41.4 21.9 %copy-start.1 = (bf16[320,1024]{1,0:T(8,128)(2,1)S(1)}, bf16[320,1024]{1,0:T(8,128)(2,1)}, u32[]{:S(2)}) copy-start(bf16[320,1024]{1,0:T(8,128)(2,1)} %grad_ref.3) | copy-start | bytes 1966084
  41.4 21.9 %copy-start.2 = (f32[1024]{0:T(1024)S(1)}, f32[1024]{0:T(1024)}, u32[]{:S(2)}) copy-start(f32[1024]{0:T(1024)} %param.17) | copy-start | bytes 12292
  41.4 21.9 %copy-start.3 = (f32[1024]{0:T(1024)S(1)}, f32[1024]{0:T(1024)}, u32[]{:S(2)}) copy-start(f32[1024]{0:T(1024)} %param.18) | copy-start | bytes 12292
  41.4 26.2 %copy-start.5 = (bf16[1,1024,2048]{2,1,0:T(8,128)(2,1)S(1)}, bf16[1,1024,2048]{2,1,0:T(8,128)(2,1)}, u32[]{:S(2)}) copy-start(bf16[1,1024,2048]{2,1,0:T(8,128)(2,1)} %param.21) | copy-start | bytes 12582916
  64.5 2.9 %collective-permute-start.2 = (bf16[320,1024]{1,0:T(8,128)(2,1)S(1)}, bf16[320,1024]{1,0:T(8,128)(2,1)S(1)}, u32[]{:S(2)}, u32[]{:S(2)}) collective-permute-start(bf16[320,1024]{1,0:T(8,128)(2,1)S(1)} %get-tuple-element.127.h2_ref), channel_id=1, source_target_pairs={{0,1},{1,0},{2,3},{3,2},{4,5},{5,4},{6,7},{7,6},{8,9},{9,8},{10,11... | collective-permute-start | bytes 1966088 | tf_op jit(solution)/shard_map/ppermute | solution.py:849
  64.7 3.0 %collective-permute-start.3 = (bf16[320,1024]{1,0:T(8,128)(2,1)S(1)}, bf16[320,1024]{1,0:T(8,128)(2,1)S(1)}, u32[]{:S(2)}, u32[]{:S(2)}) collective-permute-start(bf16[320,1024]{1,0:T(8,128)(2,1)S(1)} %get-tuple-element.128.up_ref), channel_id=1, source_target_pairs={{0,1},{1,0},{2,3},{3,2},{4,5},{5,4},{6,7},{7,6},{8,9},{9,8},{10,11... | collective-permute-start | bytes 1966088 | tf_op jit(solution)/shard_map/ppermute | solution.py:849
  65.1 15.0 %collective-permute-start.4 = (bf16[256,1024]{1,0:T(8,128)(2,1)}, bf16[256,1024]{1,0:T(8,128)(2,1)S(1)}, u32[]{:S(2)}, u32[]{:S(2)}) collective-permute-start(bf16[256,1024]{1,0:T(8,128)(2,1)} %get-tuple-element.141), channel_id=1, source_target_pairs={{0,6},{2,4},{4,2},{6,0},{8,14},{10,12},{12,10},{14,8},{16,22},{18,... | collective-permute-start | bytes 1572872 | tf_op jit(solution)/shard_map/ppermute | solution.py:849
  80.1 12.1 %copy-start.8 = (bf16[256,1024]{1,0:T(8,128)(2,1)}, bf16[256,1024]{1,0:T(8,128)(2,1)S(1)}, u32[]{:S(2)}) copy-start(bf16[256,1024]{1,0:T(8,128)(2,1)S(1)} %collective-permute-done.4.refs_7_) | copy-start | bytes 1572868
  80.1 2.1 collective-permute-start.5
  82.2 6.9 %copy-start.17 = (bf16[256,1024]{1,0:T(8,128)(2,1)S(1)}, bf16[256,1024]{1,0:T(8,128)(2,1)}, u32[]{:S(2)}) copy-start(bf16[256,1024]{1,0:T(8,128)(2,1)} %get-tuple-element.141) | copy-start | bytes 1572868
  85.4 26.3 %all-to-all-start.2 = ((bf16[32,8,1280]{2,1,0:T(8,128)(2,1)}), bf16[32,8,1280]{2,1,0:T(8,128)(2,1)S(1)}, u32[]{:S(2)}, u32[]{:S(2)}) async-start(bf16[32,8,1280]{2,1,0:T(8,128)(2,1)} %bitcast.14), calls=%async_computation.2 | async-start | bytes 1310720 | tf_op jit(solution)/shard_map/all_to_all | solution.py:966
  89.1 20.9 %collective-permute-start.6 = (bf16[256,1024]{1,0:T(8,128)(2,1)S(1)}, bf16[256,1024]{1,0:T(8,128)(2,1)S(1)}, u32[]{:S(2)}, u32[]{:S(2)}) collective-permute-start(bf16[256,1024]{1,0:T(8,128)(2,1)S(1)} %copy-done.17), channel_id=1, source_target_pairs={{0,2},{2,0},{4,6},{6,4},{8,10},{10,8},{12,14},{14,12},{16,18},{18,... | collective-permute-start | bytes 1572872 | tf_op jit(solution)/shard_map/ppermute | solution.py:849
  90.7 19.5 %collective-permute-start.7 = (bf16[256,1024]{1,0:T(8,128)(2,1)S(1)}, bf16[256,1024]{1,0:T(8,128)(2,1)S(1)}, u32[]{:S(2)}, u32[]{:S(2)}) collective-permute-start(bf16[256,1024]{1,0:T(8,128)(2,1)S(1)} %copy-done.17), channel_id=1, source_target_pairs={{0,4},{2,6},{4,0},{6,2},{8,12},{10,14},{12,8},{14,10},{16,20},{18,... | collective-permute-start | bytes 1572872 | tf_op jit(solution)/shard_map/ppermute | solution.py:849
  92.2 19.4 %collective-permute-start.8 = (bf16[256,1024]{1,0:T(8,128)(2,1)S(1)}, bf16[256,1024]{1,0:T(8,128)(2,1)}, u32[]{:S(2)}, u32[]{:S(2)}) collective-permute-start(bf16[256,1024]{1,0:T(8,128)(2,1)S(1)} %collective-permute-done.4.refs_7_), channel_id=1, source_target_pairs={{0,1},{1,0},{2,3},{3,2},{4,5},{5,4},{6,7},{7,6},{8,9},{9,8},{10,11... | collective-permute-start | bytes 1572872 | tf_op jit(solution)/shard_map/ppermute | solution.py:849
  110.0 0.8 copy-start.9
  110.8 0.8 copy-start.11
  111.6 1.0 copy-start.10
  111.6 1.4 copy-start.12
  112.4 2.0 collective-permute-start.9
  112.7 17.6 %collective-permute-start.13 = (bf16[256,1024]{1,0:T(8,128)(2,1)S(1)}, bf16[256,1024]{1,0:T(8,128)(2,1)S(1)}, u32[]{:S(2)}, u32[]{:S(2)}) collective-permute-start(bf16[256,1024]{1,0:T(8,128)(2,1)S(1)} %copy-done.10), channel_id=1, source_target_pairs={{0,1},{1,0},{2,3},{3,2},{4,5},{5,4},{6,7},{7,6},{8,9},{9,8},{10,11... | collective-permute-start | bytes 1572872 | tf_op jit(solution)/shard_map/ppermute | solution.py:849
  113.0 17.2 %collective-permute-start.14 = (bf16[256,1024]{1,0:T(8,128)(2,1)S(1)}, bf16[256,1024]{1,0:T(8,128)(2,1)S(1)}, u32[]{:S(2)}, u32[]{:S(2)}) collective-permute-start(bf16[256,1024]{1,0:T(8,128)(2,1)S(1)} %copy-done.12), channel_id=1, source_target_pairs={{0,1},{1,0},{2,3},{3,2},{4,5},{5,4},{6,7},{7,6},{8,9},{9,8},{10,11... | collective-permute-start | bytes 1572872 | tf_op jit(solution)/shard_map/ppermute | solution.py:849
  117.7 12.5 %collective-permute-start.10 = (bf16[4,256,128]{2,1,0:T(8,128)(2,1)}, bf16[4,256,128]{2,1,0:T(8,128)(2,1)S(1)}, u32[]{:S(2)}, u32[]{:S(2)}) collective-permute-start(bf16[4,256,128]{2,1,0:T(8,128)(2,1)} %get-tuple-element.157), channel_id=1, source_target_pairs={{0,2},{2,0},{4,6},{6,4},{8,10},{10,8},{12,14},{14,12},{16,18},{18,... | collective-permute-start | bytes 786440 | tf_op jit(solution)/shard_map/ppermute | solution.py:849
  118.5 12.9 %collective-permute-start.11 = (bf16[4,256,128]{2,1,0:T(8,128)(2,1)}, bf16[4,256,128]{2,1,0:T(8,128)(2,1)S(1)}, u32[]{:S(2)}, u32[]{:S(2)}) collective-permute-start(bf16[4,256,128]{2,1,0:T(8,128)(2,1)} %get-tuple-element.158), channel_id=1, source_target_pairs={{0,4},{2,6},{4,0},{6,2},{8,12},{10,14},{12,8},{14,10},{16,20},{18,... | collective-permute-start | bytes 786440 | tf_op jit(solution)/shard_map/ppermute | solution.py:849
  119.8 13.0 %collective-permute-start.12 = (bf16[4,256,128]{2,1,0:T(8,128)(2,1)}, bf16[4,256,128]{2,1,0:T(8,128)(2,1)S(1)}, u32[]{:S(2)}, u32[]{:S(2)}) collective-permute-start(bf16[4,256,128]{2,1,0:T(8,128)(2,1)} %get-tuple-element.159), channel_id=1, source_target_pairs={{0,6},{2,4},{4,2},{6,0},{8,14},{10,12},{12,10},{14,8},{16,22},{18,... | collective-permute-start | bytes 786440 | tf_op jit(solution)/shard_map/ppermute | solution.py:849
  130.2 12.2 %copy-start.13 = (bf16[256,1024]{1,0:T(8,128)(2,1)}, bf16[256,1024]{1,0:T(8,128)(2,1)S(1)}, u32[]{:S(2)}) copy-start(bf16[256,1024]{1,0:T(8,128)(2,1)S(1)} %collective-permute-done.13.refs_8_) | copy-start | bytes 1572868
  130.2 12.2 %copy-start.14 = (bf16[256,1024]{1,0:T(8,128)(2,1)}, bf16[256,1024]{1,0:T(8,128)(2,1)S(1)}, u32[]{:S(2)}) copy-start(bf16[256,1024]{1,0:T(8,128)(2,1)S(1)} %collective-permute-done.14.refs_9_) | copy-start | bytes 1572868
  132.9 3.5 %collective-permute-start.19 = (bf16[256,1024]{1,0:T(8,128)(2,1)S(1)}, bf16[256,1024]{1,0:T(8,128)(2,1)S(1)}, u32[]{:S(2)}, u32[]{:S(2)}) collective-permute-start(bf16[256,1024]{1,0:T(8,128)(2,1)S(1)} %get-tuple-element.168), channel_id=1, source_target_pairs={{0,1},{1,0},{2,3},{3,2},{4,5},{5,4},{6,7},{7,6},{8,9},{9,8},{10,11... | collective-permute-start | bytes 1572872 | tf_op jit(solution)/shard_map/ppermute | solution.py:849
  132.9 6.5 %collective-permute-start.15 = (bf16[512,128]{1,0:T(8,128)(2,1)}, bf16[512,128]{1,0:T(8,128)(2,1)S(1)}, u32[]{:S(2)}, u32[]{:S(2)}) collective-permute-start(bf16[512,128]{1,0:T(8,128)(2,1)} %get-tuple-element.164), channel_id=1, source_target_pairs={{0,2},{2,0},{4,6},{6,4},{8,10},{10,8},{12,14},{14,12},{16,18},{18,... | collective-permute-start | bytes 393224 | tf_op jit(solution)/shard_map/ppermute | solution.py:849
  133.7 8.6 %collective-permute-start.16 = (bf16[512,128]{1,0:T(8,128)(2,1)}, bf16[512,128]{1,0:T(8,128)(2,1)S(1)}, u32[]{:S(2)}, u32[]{:S(2)}) collective-permute-start(bf16[512,128]{1,0:T(8,128)(2,1)} %get-tuple-element.165), channel_id=1, source_target_pairs={{0,4},{2,6},{4,0},{6,2},{8,12},{10,14},{12,8},{14,10},{16,20},{18,... | collective-permute-start | bytes 393224 | tf_op jit(solution)/shard_map/ppermute | solution.py:849
  135.2 7.2 %collective-permute-start.17 = (bf16[512,128]{1,0:T(8,128)(2,1)}, bf16[512,128]{1,0:T(8,128)(2,1)S(1)}, u32[]{:S(2)}, u32[]{:S(2)}) collective-permute-start(bf16[512,128]{1,0:T(8,128)(2,1)} %get-tuple-element.166), channel_id=1, source_target_pairs={{0,6},{2,4},{4,2},{6,0},{8,14},{10,12},{12,10},{14,8},{16,22},{18,... | collective-permute-start | bytes 393224 | tf_op jit(solution)/shard_map/ppermute | solution.py:849
  142.4 47.1 %all-to-all-start.3 = ((bf16[32,8,1280]{2,1,0:T(8,128)(2,1)}), bf16[32,8,1280]{2,1,0:T(8,128)(2,1)S(1)}, u32[]{:S(2)}, u32[]{:S(2)}) async-start(bf16[32,8,1280]{2,1,0:T(8,128)(2,1)} %bitcast.16), calls=%async_computation.3 | async-start | bytes 1310720 | tf_op jit(solution)/shard_map/all_to_all | solution.py:966
  147.2 5.5 %copy-start.20 = (bf16[2,512,128]{2,1,0:T(8,128)(2,1)S(1)}, bf16[2,512,128]{2,1,0:T(8,128)(2,1)}, u32[]{:S(2)}) copy-start(bf16[2,512,128]{2,1,0:T(8,128)(2,1)} %get-tuple-element.188) | copy-start | bytes 786436
  147.2 7.0 %copy-start.19 = (bf16[2,512,128]{2,1,0:T(8,128)(2,1)S(1)}, bf16[2,512,128]{2,1,0:T(8,128)(2,1)}, u32[]{:S(2)}) copy-start(bf16[2,512,128]{2,1,0:T(8,128)(2,1)} %get-tuple-element.189) | copy-start | bytes 786436
  147.3 8.5 %copy-start.18 = (bf16[2,512,128]{2,1,0:T(8,128)(2,1)S(1)}, bf16[2,512,128]{2,1,0:T(8,128)(2,1)}, u32[]{:S(2)}) copy-start(bf16[2,512,128]{2,1,0:T(8,128)(2,1)} %get-tuple-element.190) | copy-start | bytes 786436
  151.3 14.7 %collective-permute-start.23 = (bf16[2,512,128]{2,1,0:T(8,128)(2,1)S(1)}, bf16[2,512,128]{2,1,0:T(8,128)(2,1)S(1)}, u32[]{:S(2)}, u32[]{:S(2)}) collective-permute-start(bf16[2,512,128]{2,1,0:T(8,128)(2,1)S(1)} %get-tuple-element.176), channel_id=1, source_target_pairs={{0,8},{2,10},{4,12},{6,14},{8,0},{10,2},{12,4},{14,6},{16,24},{18,... | collective-permute-start | bytes 786440 | tf_op jit(solution)/shard_map/ppermute | solution.py:849
  152.8 17.3 %collective-permute-start.20 = (bf16[2,512,128]{2,1,0:T(8,128)(2,1)S(1)}, bf16[2,512,128]{2,1,0:T(8,128)(2,1)S(1)}, u32[]{:S(2)}, u32[]{:S(2)}) collective-permute-start(bf16[2,512,128]{2,1,0:T(8,128)(2,1)S(1)} %copy-done.20), channel_id=1, source_target_pairs={{0,2},{2,0},{4,6},{6,4},{8,10},{10,8},{12,14},{14,12},{16,18},{18,... | collective-permute-start | bytes 786440 | tf_op jit(solution)/shard_map/ppermute | solution.py:849
  154.3 16.2 %collective-permute-start.21 = (bf16[2,512,128]{2,1,0:T(8,128)(2,1)S(1)}, bf16[2,512,128]{2,1,0:T(8,128)(2,1)S(1)}, u32[]{:S(2)}, u32[]{:S(2)}) collective-permute-start(bf16[2,512,128]{2,1,0:T(8,128)(2,1)S(1)} %copy-done.19), channel_id=1, source_target_pairs={{0,4},{2,6},{4,0},{6,2},{8,12},{10,14},{12,8},{14,10},{16,20},{18,... | collective-permute-start | bytes 786440 | tf_op jit(solution)/shard_map/ppermute | solution.py:849
  155.7 14.8 %collective-permute-start.22 = (bf16[2,512,128]{2,1,0:T(8,128)(2,1)S(1)}, bf16[2,512,128]{2,1,0:T(8,128)(2,1)S(1)}, u32[]{:S(2)}, u32[]{:S(2)}) collective-permute-start(bf16[2,512,128]{2,1,0:T(8,128)(2,1)S(1)} %copy-done.18), channel_id=1, source_target_pairs={{0,6},{2,4},{4,2},{6,0},{8,14},{10,12},{12,10},{14,8},{16,22},{18,... | collective-permute-start | bytes 786440 | tf_op jit(solution)/shard_map/ppermute | solution.py:849
  167.7 8.5 %collective-permute-start.25 = (bf16[1,512,128]{2,1,0:T(8,128)(2,1)S(1)}, bf16[1,512,128]{2,1,0:T(8,128)(2,1)S(1)}, u32[]{:S(2)}, u32[]{:S(2)}) collective-permute-start(bf16[1,512,128]{2,1,0:T(8,128)(2,1)S(1)} %get-tuple-element.193), channel_id=1, source_target_pairs={{0,16},{2,18},{4,20},{6,22},{8,24},{10,26},{12,28},{14,30},{16,0},... | collective-permute-start | bytes 393224 | tf_op jit(solution)/shard_map/ppermute | solution.py:849
  174.9 9.6 %collective-permute-start.24 = (bf16[2,512,128]{2,1,0:T(8,128)(2,1)S(1)}, bf16[2,512,128]{2,1,0:T(8,128)(2,1)S(1)}, u32[]{:S(2)}, u32[]{:S(2)}) collective-permute-start(bf16[2,512,128]{2,1,0:T(8,128)(2,1)S(1)} %get-tuple-element.198), channel_id=1, source_target_pairs={{0,8},{2,10},{4,12},{6,14},{8,0},{10,2},{12,4},{14,6},{16,24},{18,... | collective-permute-start | bytes 786440 | tf_op jit(solution)/shard_map/ppermute | solution.py:849
  177.1 9.0 %collective-permute-start.27 = (bf16[512,128]{1,0:T(8,128)(2,1)S(1)}, bf16[512,128]{1,0:T(8,128)(2,1)S(1)}, u32[]{:S(2)}, u32[]{:S(2)}) collective-permute-start(bf16[512,128]{1,0:T(8,128)(2,1)S(1)} %last_add.1.own_ref), channel_id=1, source_target_pairs={{0,16},{2,18},{4,20},{6,22},{8,24},{10,26},{12,28},{14,30},{16,0},... | collective-permute-start | bytes 393224 | tf_op jit(solution)/shard_map/ppermute | solution.py:849
  186.2 9.5 %collective-permute-start.31 = (bf16[1024,128]{1,0:T(8,128)(2,1)S(1)}, bf16[1024,128]{1,0:T(8,128)(2,1)S(1)}, u32[]{:S(2)}, u32[]{:S(2)}) collective-permute-start(bf16[1024,128]{1,0:T(8,128)(2,1)S(1)} %stack.20.own_ref), channel_id=1, source_target_pairs={{0,8},{2,10},{4,12},{6,14},{8,0},{10,2},{12,4},{14,6},{16,24},{18,... | collective-permute-start | bytes 786440 | tf_op jit(solution)/shard_map/ppermute | solution.py:849
  187.4 6.5 %collective-permute-start.26 = (bf16[1,512,128]{2,1,0:T(8,128)(2,1)S(1)}, bf16[1,512,128]{2,1,0:T(8,128)(2,1)S(1)}, u32[]{:S(2)}, u32[]{:S(2)}) collective-permute-start(bf16[1,512,128]{2,1,0:T(8,128)(2,1)S(1)} %get-tuple-element.203), channel_id=1, source_target_pairs={{0,16},{2,18},{4,20},{6,22},{8,24},{10,26},{12,28},{14,30},{16,0},... | collective-permute-start | bytes 393224 | tf_op jit(solution)/shard_map/ppermute | solution.py:849
  189.5 4.4 %collective-permute-start.29 = (f32[16,128]{1,0:T(8,128)S(1)}, f32[16,128]{1,0:T(8,128)S(1)}, u32[]{:S(2)}, u32[]{:S(2)}) collective-permute-start(f32[16,128]{1,0:T(8,128)S(1)} %get-tuple-element.207.refs_2_), channel_id=1, source_target_pairs={{0,1},{1,0},{2,3},{3,2},{4,5},{5,4},{6,7},{7,6},{8,9},{9,8},{10,11... | collective-permute-start | bytes 24584 | tf_op jit(solution)/shard_map/ppermute | solution.py:849
  189.5 12.7 %copy-start.16 = (bf16[320,1024]{1,0:T(8,128)(2,1)S(1)}, bf16[320,1024]{1,0:T(8,128)(2,1)}, u32[]{:S(2)}) copy-start(bf16[320,1024]{1,0:T(8,128)(2,1)} %get-tuple-element.179) | copy-start | bytes 1966084
  193.4 1.3 collective-permute-start.28
  195.8 23.8 %copy-start.15 = (bf16[320,1024]{1,0:T(8,128)(2,1)S(1)}, bf16[320,1024]{1,0:T(8,128)(2,1)}, u32[]{:S(2)}) copy-start(bf16[320,1024]{1,0:T(8,128)(2,1)} %get-tuple-element.178) | copy-start | bytes 1966084
  195.8 14.2 %collective-permute-start.33 = (bf16[2048,128]{1,0:T(8,128)(2,1)S(1)}, bf16[2048,128]{1,0:T(8,128)(2,1)S(1)}, u32[]{:S(2)}, u32[]{:S(2)}) collective-permute-start(bf16[2048,128]{1,0:T(8,128)(2,1)S(1)} %stack.21.refs_0_), channel_id=1, source_target_pairs={{0,2},{2,0},{4,6},{6,4},{8,10},{10,8},{12,14},{14,12},{16,18},{18,... | collective-permute-start | bytes 1572872 | tf_op jit(solution)/shard_map/ppermute | solution.py:849
  197.3 13.9 %collective-permute-start.34 = (bf16[2048,128]{1,0:T(8,128)(2,1)S(1)}, bf16[2048,128]{1,0:T(8,128)(2,1)S(1)}, u32[]{:S(2)}, u32[]{:S(2)}) collective-permute-start(bf16[2048,128]{1,0:T(8,128)(2,1)S(1)} %stack.21.refs_0_), channel_id=1, source_target_pairs={{0,4},{2,6},{4,0},{6,2},{8,12},{10,14},{12,8},{14,10},{16,20},{18,... | collective-permute-start | bytes 1572872 | tf_op jit(solution)/shard_map/ppermute | solution.py:849
  200.1 8.3 %collective-permute-start.30 = (bf16[576,128]{1,0:T(8,128)(2,1)S(1)}, bf16[576,128]{1,0:T(8,128)(2,1)S(1)}, u32[]{:S(2)}, u32[]{:S(2)}) collective-permute-start(bf16[576,128]{1,0:T(8,128)(2,1)S(1)} %last_add_sums.1.own_ref), channel_id=1, source_target_pairs={{0,16},{2,18},{4,20},{6,22},{8,24},{10,26},{12,28},{14,30},{16,0},... | collective-permute-start | bytes 442376 | tf_op jit(solution)/shard_map/ppermute | solution.py:849
  202.3 17.3 %collective-permute-start.18 = (bf16[320,1024]{1,0:T(8,128)(2,1)S(1)}, bf16[320,1024]{1,0:T(8,128)(2,1)S(1)}, u32[]{:S(2)}, u32[]{:S(2)}) collective-permute-start(bf16[320,1024]{1,0:T(8,128)(2,1)S(1)} %copy-done.16), channel_id=1, source_target_pairs={{0,1},{1,0},{2,3},{3,2},{4,5},{5,4},{6,7},{7,6},{8,9},{9,8},{10,11... | collective-permute-start | bytes 1966088 | tf_op jit(solution)/shard_map/ppermute | solution.py:849
  208.5 6.6 %collective-permute-start.32 = (bf16[1088,128]{1,0:T(8,128)(2,1)S(1)}, bf16[1088,128]{1,0:T(8,128)(2,1)S(1)}, u32[]{:S(2)}, u32[]{:S(2)}) collective-permute-start(bf16[1088,128]{1,0:T(8,128)(2,1)S(1)} %stack.22.own_ref), channel_id=1, source_target_pairs={{0,8},{2,10},{4,12},{6,14},{8,0},{10,2},{12,4},{14,6},{16,24},{18,... | collective-permute-start | bytes 835592 | tf_op jit(solution)/shard_map/ppermute | solution.py:849
  215.1 17.7 %collective-permute-start.35 = (bf16[2112,128]{1,0:T(8,128)(2,1)S(1)}, bf16[2112,128]{1,0:T(8,128)(2,1)S(1)}, u32[]{:S(2)}, u32[]{:S(2)}) collective-permute-start(bf16[2112,128]{1,0:T(8,128)(2,1)S(1)} %stack.23.refs_0_), channel_id=1, source_target_pairs={{0,2},{2,0},{4,6},{6,4},{8,10},{10,8},{12,14},{14,12},{16,18},{18,... | collective-permute-start | bytes 1622024 | tf_op jit(solution)/shard_map/ppermute | solution.py:849
  215.7 17.2 %collective-permute-start.36 = (bf16[2112,128]{1,0:T(8,128)(2,1)S(1)}, bf16[2112,128]{1,0:T(8,128)(2,1)S(1)}, u32[]{:S(2)}, u32[]{:S(2)}) collective-permute-start(bf16[2112,128]{1,0:T(8,128)(2,1)S(1)} %stack.23.refs_0_), channel_id=1, source_target_pairs={{0,4},{2,6},{4,0},{6,2},{8,12},{10,14},{12,8},{14,10},{16,20},{18,... | collective-permute-start | bytes 1622024 | tf_op jit(solution)/shard_map/ppermute | solution.py:849
  217.3 13.1 %collective-permute-start.37 = (bf16[1024,128]{1,0:T(8,128)(2,1)S(1)}, bf16[1024,128]{1,0:T(8,128)(2,1)S(1)}, u32[]{:S(2)}, u32[]{:S(2)}) collective-permute-start(bf16[1024,128]{1,0:T(8,128)(2,1)S(1)} %slice.16), channel_id=1, source_target_pairs={{0,2},{2,0},{4,6},{6,4},{8,10},{10,8},{12,14},{14,12},{16,18},{18,... | collective-permute-start | bytes 786440 | tf_op jit(solution)/shard_map/ppermute | solution.py:849
  218.7 14.2 %collective-permute-start.38 = (bf16[1024,128]{1,0:T(8,128)(2,1)S(1)}, bf16[1024,128]{1,0:T(8,128)(2,1)S(1)}, u32[]{:S(2)}, u32[]{:S(2)}) collective-permute-start(bf16[1024,128]{1,0:T(8,128)(2,1)S(1)} %slice.17), channel_id=1, source_target_pairs={{0,4},{2,6},{4,0},{6,2},{8,12},{10,14},{12,8},{14,10},{16,20},{18,... | collective-permute-start | bytes 786440 | tf_op jit(solution)/shard_map/ppermute | solution.py:849
  232.9 7.7 %collective-permute-start.39 = (bf16[1056,128]{1,0:T(8,128)(2,1)S(1)}, bf16[1056,128]{1,0:T(8,128)(2,1)S(1)}, u32[]{:S(2)}, u32[]{:S(2)}) collective-permute-start(bf16[1056,128]{1,0:T(8,128)(2,1)S(1)} %slice.18), channel_id=1, source_target_pairs={{0,2},{2,0},{4,6},{6,4},{8,10},{10,8},{12,14},{14,12},{16,18},{18,... | collective-permute-start | bytes 811016 | tf_op jit(solution)/shard_map/ppermute | solution.py:849
  234.2 6.5 %collective-permute-start.40 = (bf16[1056,128]{1,0:T(8,128)(2,1)S(1)}, bf16[1056,128]{1,0:T(8,128)(2,1)S(1)}, u32[]{:S(2)}, u32[]{:S(2)}) collective-permute-start(bf16[1056,128]{1,0:T(8,128)(2,1)S(1)} %slice.19), channel_id=1, source_target_pairs={{0,4},{2,6},{4,0},{6,2},{8,12},{10,14},{12,8},{14,10},{16,20},{18,... | collective-permute-start | bytes 811016 | tf_op jit(solution)/shard_map/ppermute | solution.py:849

commit v4 on v3

--- a/solution.py
+++ b/solution.py
@@ -872,16 +872,14 @@
             return call(
                 functools.partial(add_kernel, bit=bit + 1), "add",
                 [((owners // 2, rows, columns), BF16)] * 2, [where, halves[0], came], 0, scalars=1,
-                away=(1,), out_away=(0,),
             )
         if sums is None:
             return call(
                 last_add_kernel, "last_add", [((rows, columns), BF16)], [halves[0], came], 0,
-                away=(0,),
             )
         return call(
             last_add_sums_kernel, "last_add_sums", [((rows + extra, columns), BF16)],
-            [halves[0], came, *sums], 0, away=(0,),
+            [halves[0], came, *sums], 0,
         )
 
     def stack(own, came, sums):
@@ -1118,7 +1116,6 @@
     out_value = call(
         value_grad_kernel, "value_grad", split, [where, *value_parts, *tokens, *out_parts],
         product, scalars=1, scratch=[pltpu.VMEM((width, 128), F32)], away=(1, *range(5, 13)),
-        out_away=(0,),
     )
     branch_kept, branch_sent = expert_branch(after(hidden, out_value[1]), w_down[0])
     branch_came = cross(branch_sent)
@@ -1130,7 +1127,7 @@
         return call(
             key_query_grad_kernel, "key_query_grad", split,
             [where, key_query_parts[0], *came, *tokens], 2 * product, scalars=1,
-            scratch=[pltpu.VMEM((width, 128), F32)], away=(1, *range(5, 12)), out_away=(0,),
+            scratch=[pltpu.VMEM((width, 128), F32)], away=(1, *range(5, 12)),
         )
 
     sums = [sums1, cross(sums1), sums2, cross(sums2)]

time: 244 us -> 241 us (0.988)
  waiting for transfers between devices: 53.5 us -> 58.9 us
  Pallas kernels: 88.7 us -> 83.5 us
  starting transfers between devices: 50.4 us -> 47.8 us
    ppermute x41, waiting for transfers between devices: 53.4 us -> 58.9 us  [flip(): return lax.ppermute(value, axis, [(i, i ^ bit) for i in range(size)])]
    pallas_call x21, Pallas kernels: 48.8 us -> 43.6 us  [call(): pl.pallas_call(kernel, name=name, out_shape=shapes, in_specs=[SMEM if at...]
    ppermute x41, starting transfers between devices: 41.9 us -> 39.2 us  [flip(): return lax.ppermute(value, axis, [(i, i ^ bit) for i in range(size)])]
  transfers between devices with their start and end apart: 43 -> 43, of which waited for: 24 -> 25; matrix products, arithmetic and copies ran while one was open for 1% -> 1% of each run, Pallas kernels for 28% -> 27%
where the time goes in v4:
time: 241 us
  Pallas kernels  83.5 us (35%)
  waiting for transfers between devices  58.9 us (24%)
  starting transfers between devices  47.8 us (20%)
  blocking collectives  46.3 us (19%)
    ppermute x41, waiting for transfers between devices, flip(): return lax.ppermute(value, axis, [(i, i ^ bit) for i in range(size)])  58.9 us
    all_to_all x2, blocking collectives, exchange(): lax.all_to_all(value, ('exp', 'head'), split_axis=0, concat_axis=0, tiled...  46.3 us
    pallas_call x21, Pallas kernels, call(): pl.pallas_call(kernel, name=name, out_shape=shapes, in_specs=[SMEM if at...  43.6 us
    ppermute x41, starting transfers between devices, flip(): return lax.ppermute(value, axis, [(i, i ^ bit) for i in range(size)])  39.2 us
    pallas_call x1, Pallas kernels, expert(): pl.pallas_call(expert_kernel, name='expert', grid=(units // tile,), out_s...  11.9 us
    pallas_call x1, Pallas kernels, expert_grads(): pl.pallas_call(expert_grad_kernel, name='expert_grads', grid=(units // ti...  11.6 us
    all_to_all x2, starting transfers between devices, exchange(): lax.all_to_all(value, ('exp', 'head'), split_axis=0, concat_axis=0, tiled...  8.57 us
    pallas_call x1, Pallas kernels, expert_branch(): pl.pallas_call(branch_kernel, name='expert_branch', grid=(units // tile,)...  6.91 us
  transfers between devices with their start and end apart: 43, of which 25 were waited for; matrix products, arithmetic and copies ran while one was open for 1% of the time, Pallas kernels for 27%

profile of v4, /device:TPU:0, one launch (start us, length us, event | category | flops | bytes accessed | tf_op | source)
XLA Modules:
  0.0 240.8 jit_solution(16657316869277497669)
XLA Ops:
  0.7 2.5 %norm1.1 = bf16[256,1280]{1,0:T(8,128)(2,1)S(1)} custom-call(bf16[320,1024]{1,0:T(8,128)(2,1)} %x_ref.5, f32[1,1024]{1,0:T(1,128)} %bitcast.40, f32[1,1024]{1,0:T(1,128)} %bitcast.42), custom_call_target="tpu_custom_call" | custom-call | flops 503316480 | bytes 1318912 | tf_op jit(solution)/shard_map/norm1/pallas_call | solution.py:746
  3.2 25.0 %all_to_all.20 = bf16[32,8,1280]{2,1,0:T(8,128)(2,1)S(1)} all-to-all(bf16[32,8,1280]{2,1,0:T(8,128)(2,1)S(1)} %bitcast.29), channel_id=1, replica_groups=mesh['exp'=16,'head'=2] {'exp','head'}, dimensions={0} | all-to-all | bytes 1310720 | tf_op jit(solution)/shard_map/all_to_all | solution.py:964
  29.2 1.8 collective-permute-done.other_ref
  30.9 8.5 %attend.1 = (bf16[256,1024]{1,0:T(8,128)(2,1)}, bf16[512,1024]{1,0:T(8,128)(2,1)}, bf16[3,512,512]{2,1,0:T(8,128)(2,1)}, bf16[512,512]{1,0:T(8,128)(2,1)}, f32[1...) custom-call(s32[3]{0:T(128)S(1)} %pad_add_fusion.where_ref, s32[1,5]{1,0:T(1,128)S(1)} %copy-done.7, ...), custom_call_target="tpu_custom_call" | custom-call | flops 4294967296 | bytes 10747936 | tf_op jit(solution)/shard_map/attend/pallas_call | solution.py:746
  39.6 1.8 collective-permute-done.1.came_ref
  42.1 21.2 %all_to_all.21 = bf16[32,8,1280]{2,1,0:T(8,128)(2,1)S(1)} all-to-all(bf16[32,8,1280]{2,1,0:T(8,128)(2,1)S(1)} %bitcast.26), channel_id=1, replica_groups=mesh['exp'=16,'head'=2] {'exp','head'}, dimensions={0} | all-to-all | bytes 1310720 | tf_op jit(solution)/shard_map/all_to_all | solution.py:964
  63.3 1.2 norm2.1
  65.1 2.3 collective-permute-start.4
  67.6 11.9 %expert.1 = (bf16[640,2048]{1,0:T(8,128)(2,1)}, bf16[640,2048]{1,0:T(8,128)(2,1)}, f32[320,1024]{1,0:T(8,128)S(1)}, bf16[320,1024]{1,0:T(8,128)(2,1)S(1)}, bf16[...) custom-call(bf16[320,1024]{1,0:T(8,128)(2,1)S(1)} %get-tuple-element.127.h2_ref, ...), custom_call_target="tpu_custom_call" | custom-call | flops 8053063680 | bytes 16777216 | tf_op jit(solution)/shard_map/expert/pallas_call | solution.py:776
  80.1 2.1 collective-permute-done.5.came_ref
  82.2 3.1 %norm2_back.1 = (f32[320,1024]{1,0:T(8,128)}, bf16[256,1280]{1,0:T(8,128)(2,1)}, f32[16,128]{1,0:T(8,128)S(1)}) custom-call(f32[320,1024]{1,0:T(8,128)S(1)} %get-tuple-element.131.kept_ref, bf16[320,1024]{1,0:T(8,128)(2,1)S(1)} %collective-permute-done.5.came_ref, f32[320,1024]{1,0:T(8,128)S(1)} %get-tuple-element.124.resid_ref, ...), custom_call_target="tpu_custom_call" | custom-call | flops 503316480 | bytes 5910528 | tf_op jit(solution)/shard_map/norm2_back/pallas_call | solution.py:746
  85.4 3.7 %all-to-all-start.2 = ((bf16[32,8,1280]{2,1,0:T(8,128)(2,1)}), bf16[32,8,1280]{2,1,0:T(8,128)(2,1)S(1)}, u32[]{:S(2)}, u32[]{:S(2)}) async-start(bf16[32,8,1280]{2,1,0:T(8,128)(2,1)} %bitcast.14), calls=%async_computation.2 | async-start | bytes 1310720 | tf_op jit(solution)/shard_map/all_to_all | solution.py:964
  89.1 1.6 collective-permute-start.6
  90.7 1.5 collective-permute-start.7
  92.2 11.6 %expert_grads.1 = (f32[1024,2048]{1,0:T(8,128)}, f32[2048,1024]{1,0:T(8,128)}) custom-call(bf16[640,1024]{1,0:T(8,128)(2,1)} %get-tuple-element.136.rows_ref, bf16[640,1024]{1,0:T(8,128)(2,1)} %get-tuple-element.137.grads_ref, bf16[640,2048]{1,0:T(8,128)(2,1)} %get-tuple-element.177.hidden_ref, bf16[640,2048]{1,0:T(8,128)(2,1)} %get-tuple-element.138.dpre_ref), custom_call_target="tpu_custom_call" | custom-call | flops 5368709120 | bytes 25165824 | tf_op jit(solution)/shard_map/expert_grads/pallas_call | solution.py:806
  103.8 6.2 %collective-permute-done.6.refs_5_ = bf16[256,1024]{1,0:T(8,128)(2,1)S(1)} collective-permute-done((bf16[256,1024]{1,0:T(8,128)(2,1)S(1)}, bf16[256,1024]{1,0:T(8,128)(2,1)S(1)}, u32[]{:S(2)}, u32[]{:S(2)}) %collective-permute-start.6) | collective-permute-done | bytes 524320 | tf_op jit(solution)/shard_map/ppermute | solution.py:849
  110.8 0.8 copy-done.11
  113.2 1.2 collective-permute-done.9.other_ref
  114.4 3.4 %out_grad.1 = (bf16[512,1024]{1,0:T(8,128)(2,1)S(1)}, bf16[4,256,128]{2,1,0:T(8,128)(2,1)}, bf16[4,256,128]{2,1,0:T(8,128)(2,1)}, bf16[4,256,128]{2,1,0:T(8,128)(2,1)}, bf16[4,256,128]{2,1,0:T(8,128)(2,1)}) custom-call(s32[3]{0:T(128)S(1)} %pad_add_fusion.where_ref, bf16[256,1024]{1,0:T(8,128)(2,1)S(1)} %gather2.1.own_ref, ...), custom_call_target="tpu_custom_call" | custom-call | flops 536870912 | bytes 3670028 | tf_op jit(solution)/shard_map/out_grad/pallas_call | solution.py:746
  118.5 1.4 collective-permute-start.11
  119.8 1.5 collective-permute-start.12
  121.3 8.9 %attend_back.1 = (f32[256,1024]{1,0:T(8,128)S(1)}, bf16[256,1024]{1,0:T(8,128)(2,1)S(1)}, bf16[512,128]{1,0:T(8,128)(2,1)}, bf16[512,128]{1,0:T(8,128)(2,1)}, bf...) custom-call(s32[3]{0:T(128)S(1)} %pad_add_fusion.where_ref, ...), custom_call_target="tpu_custom_call" | custom-call | flops 7516192768 | bytes 10747936 | tf_op jit(solution)/shard_map/attend_back/pallas_call | solution.py:746
  130.3 1.1 collective-permute-done.11.refs_13_
  131.4 1.5 collective-permute-done.12.refs_14_
  132.9 0.9 collective-permute-start.15
  133.7 1.5 collective-permute-start.16
  135.2 1.2 collective-permute-start.17
  136.4 1.4 scatter2.1
  137.8 1.6 collective-permute-done.15.refs_1_
  139.4 3.0 %collective-permute-done.16.refs_2_ = bf16[512,128]{1,0:T(8,128)(2,1)S(1)} collective-permute-done((bf16[512,128]{1,0:T(8,128)(2,1)}, bf16[512,128]{1,0:T(8,128)(2,1)S(1)}, u32[]{:S(2)}, u32[]{:S(2)}) %collective-permute-start.16) | collective-permute-done | bytes 131104 | tf_op jit(solution)/shard_map/ppermute | solution.py:849
  142.4 4.8 %all-to-all-start.3 = ((bf16[32,8,1280]{2,1,0:T(8,128)(2,1)}), bf16[32,8,1280]{2,1,0:T(8,128)(2,1)S(1)}, u32[]{:S(2)}, u32[]{:S(2)}) async-start(bf16[32,8,1280]{2,1,0:T(8,128)(2,1)} %bitcast.16), calls=%async_computation.3 | async-start | bytes 1310720 | tf_op jit(solution)/shard_map/all_to_all | solution.py:964
  147.3 3.3 %value_grad.1 = (bf16[2,512,128]{2,1,0:T(8,128)(2,1)S(1)}, bf16[2,512,128]{2,1,0:T(8,128)(2,1)S(1)}) custom-call(s32[3]{0:T(128)S(1)} %pad_add_fusion.where_ref, bf16[512,128]{1,0:T(8,128)(2,1)} %get-tuple-element.163.refs_0_, bf16[512,128]{1,0:T(8,128)(2,1)S(1)} %collective-permute-done.15.refs_1_, bf16[512,128]{1,0:T(8,128)(2,1)S(1)} %collective-permute-done.16.refs_2_, ...), custom_call_target="tpu_custom_call" | custom-call | flops 536870912 | bytes 6291468 | tf_op jit(solution)/shard_map/value_grad/pallas_call | solution.py:746
  150.6 1.6 collective-permute-start.23
  152.2 1.5 collective-permute-start.20
  153.7 1.5 collective-permute-start.21
  155.7 6.9 %expert_branch.1 = (bf16[320,1024]{1,0:T(8,128)(2,1)}, bf16[320,1024]{1,0:T(8,128)(2,1)}) custom-call(bf16[640,2048]{1,0:T(8,128)(2,1)} %get-tuple-element.177.hidden_ref, bf16[2048,1024]{1,0:T(8,128)(2,1)} %bitcast.38), custom_call_target="tpu_custom_call" | custom-call | flops 2684354560 | bytes 8388608 | tf_op jit(solution)/shard_map/expert_branch/pallas_call | solution.py:829
  162.6 3.4 %collective-permute-done.23.came_ref = bf16[2,512,128]{2,1,0:T(8,128)(2,1)S(1)} collective-permute-done((bf16[2,512,128]{2,1,0:T(8,128)(2,1)S(1)}, bf16[2,512,128]{2,1,0:T(8,128)(2,1)S(1)}, u32[]{:S(2)}, u32[]{:S(2)}) %collective-permute-start.23) | collective-permute-done | bytes 262176 | tf_op jit(solution)/shard_map/ppermute | solution.py:849
  166.6 2.5 %collective-permute-start.25 = (bf16[1,512,128]{2,1,0:T(8,128)(2,1)S(1)}, bf16[1,512,128]{2,1,0:T(8,128)(2,1)S(1)}, u32[]{:S(2)}, u32[]{:S(2)}) collective-permute-start(bf16[1,512,128]{2,1,0:T(8,128)(2,1)S(1)} %get-tuple-element.193), channel_id=1, source_target_pairs={{0,16},{2,18},{4,20},{6,22},{8,24},{10,26},{12,28},{14,30},{16,0},... | collective-permute-start | bytes 393224 | tf_op jit(solution)/shard_map/ppermute | solution.py:849
  169.1 0.9 collective-permute-done.21.refs_2_
  170.0 3.7 %key_query_grad.1 = (bf16[2,512,128]{2,1,0:T(8,128)(2,1)S(1)}, bf16[2,512,128]{2,1,0:T(8,128)(2,1)S(1)}) custom-call(s32[3]{0:T(128)S(1)} %pad_add_fusion.where_ref, bf16[2,512,128]{2,1,0:T(8,128)(2,1)} %get-tuple-element.184.refs_0_, bf16[2,512,128]{2,1,0:T(8,128)(2,1)S(1)} %collective-permute-done.20.refs_1_, ...), custom_call_target="tpu_custom_call" | custom-call | flops 1073741824 | bytes 5767180 | tf_op jit(solution)/shard_map/key_query_grad/pallas_call | solution.py:746
  173.7 1.5 collective-permute-start.24
  175.3 1.8 collective-permute-start.27
  177.1 7.2 %collective-permute-done.24.came_ref = bf16[2,512,128]{2,1,0:T(8,128)(2,1)S(1)} collective-permute-done((bf16[2,512,128]{2,1,0:T(8,128)(2,1)S(1)}, bf16[2,512,128]{2,1,0:T(8,128)(2,1)S(1)}, u32[]{:S(2)}, u32[]{:S(2)}) %collective-permute-start.24) | collective-permute-done | bytes 262176 | tf_op jit(solution)/shard_map/ppermute | solution.py:849
  184.9 1.1 collective-permute-start.31
  186.0 2.3 collective-permute-start.26
  188.3 3.9 %norm1_back.1 = (f32[320,1024]{1,0:T(8,128)}, f32[16,128]{1,0:T(8,128)S(1)}) custom-call(bf16[256,1280]{1,0:T(8,128)(2,1)S(1)} %bitcast.24, bf16[320,1024]{1,0:T(8,128)(2,1)} %x_ref.5, f32[320,1024]{1,0:T(8,128)} %get-tuple-element.182.dresid_ref, f32[1,1024]{1,0:T(1,128)} %bitcast.41), custom_call_target="tpu_custom_call" | custom-call | flops 503316480 | bytes 3944448 | tf_op jit(solution)/shard_map/norm1_back/pallas_call | solution.py:746
  192.8 0.8 collective-permute-done.28.refs_1_
  194.2 0.9 collective-permute-start.33
  195.2 1.7 collective-permute-start.34
  196.9 2.0 collective-permute-start.30
  198.9 7.2 %collective-permute-done.30.came_ref = bf16[576,128]{1,0:T(8,128)(2,1)S(1)} collective-permute-done((bf16[576,128]{1,0:T(8,128)(2,1)S(1)}, bf16[576,128]{1,0:T(8,128)(2,1)S(1)}, u32[]{:S(2)}, u32[]{:S(2)}) %collective-permute-start.30) | collective-permute-done | bytes 147488 | tf_op jit(solution)/shard_map/ppermute | solution.py:849
  206.2 1.7 collective-permute-done.33.refs_1_
  208.5 4.2 %collective-permute-done.32.came_ref = bf16[1088,128]{1,0:T(8,128)(2,1)S(1)} collective-permute-done((bf16[1088,128]{1,0:T(8,128)(2,1)S(1)}, bf16[1088,128]{1,0:T(8,128)(2,1)S(1)}, u32[]{:S(2)}, u32[]{:S(2)}) %collective-permute-start.32) | collective-permute-done | bytes 278560 | tf_op jit(solution)/shard_map/ppermute | solution.py:849
  213.3 0.9 collective-permute-start.36
  214.3 1.0 collective-permute-start.37
  215.4 1.8 collective-permute-start.38
  217.2 1.1 add_convert_fusion
  218.3 2.8 %finish_out_value_near.1 = (f32[3,1024,512]{2,1,0:T(8,128)}, f32[512,1024]{1,0:T(8,128)}) custom-call(s32[3]{0:T(128)S(1)} %pad_add_fusion.where_ref, bf16[2048,128]{1,0:T(8,128)(2,1)S(1)} %stack.21.refs_0_, bf16[2048,128]{1,0:T(8,128)(2,1)S(1)} %collective-permute-done.33.refs_1_, bf16[2048,128]{1,0:T(8,128)(2,1)S(1)} %collective-permute-done.34.refs_2_), custom_call_target="tpu_custom_call" | custom-call | bytes 6291456 | tf_op jit(solution)/shard_map/finish_out_value_near/pallas_call | solution.py:902
  221.1 8.9 %collective-permute-done.37.refs_0_ = bf16[1024,128]{1,0:T(8,128)(2,1)S(1)} collective-permute-done((bf16[1024,128]{1,0:T(8,128)(2,1)S(1)}, bf16[1024,128]{1,0:T(8,128)(2,1)S(1)}, u32[]{:S(2)}, u32[]{:S(2)}) %collective-permute-start.37) | collective-permute-done | bytes 262176 | tf_op jit(solution)/shard_map/ppermute | solution.py:849
  230.8 1.1 collective-permute-start.39
  232.3 1.6 finish_out_value_far.1
  233.9 3.0 %finish_near.1 = (f32[3,1024,512]{2,1,0:T(8,128)}, f32[32,128]{1,0:T(8,128)S(1)}) custom-call(s32[3]{0:T(128)S(1)} %pad_add_fusion.where_ref, bf16[2112,128]{1,0:T(8,128)(2,1)S(1)} %stack.23.refs_0_, bf16[2112,128]{1,0:T(8,128)(2,1)S(1)} %collective-permute-done.35.refs_1_, ...), custom_call_target="tpu_custom_call", output_to_operand_aliasing={{0}: (4, {})} | custom-call | bytes 6291456 | tf_op jit(solution)/shard_map/finish_near/pallas_call | solution.py:1171
  237.3 1.1 collective-permute-done.40.refs_1_
  238.4 2.2 finish_far.1
  (101 shorter events, 12.4 us)
Async XLA Ops:
  0.6 27.5 %copy-start.4 = (s32[256]{0:T(256)S(1)}, s32[256]{0:T(256)}, u32[]{:S(2)}) copy-start(s32[256]{0:T(256)} %param.13) | copy-start | bytes 3076
  3.2 27.8 %copy-start.7 = (s32[1,5]{1,0:T(1,128)S(1)}, s32[1,5]{1,0:T(1,128)}, u32[]{:S(2)}) copy-start(s32[1,5]{1,0:T(1,128)} %lengths_ref.3) | copy-start | bytes 64
  29.0 2.0 collective-permute-start
  30.9 36.7 %copy-start.6 = (bf16[1,2048,1024]{2,1,0:T(8,128)(2,1)S(1)}, bf16[1,2048,1024]{2,1,0:T(8,128)(2,1)}, u32[]{:S(2)}) copy-start(bf16[1,2048,1024]{2,1,0:T(8,128)(2,1)} %param.22) | copy-start | bytes 12582916
  39.4 2.0 collective-permute-start.1
  41.4 21.9 %copy-start = (bf16[320,1024]{1,0:T(8,128)(2,1)S(1)}, bf16[320,1024]{1,0:T(8,128)(2,1)}, u32[]{:S(2)}) copy-start(bf16[320,1024]{1,0:T(8,128)(2,1)} %x_ref.5) | copy-start | bytes 1966084
  41.4 21.9 %copy-start.1 = (bf16[320,1024]{1,0:T(8,128)(2,1)S(1)}, bf16[320,1024]{1,0:T(8,128)(2,1)}, u32[]{:S(2)}) copy-start(bf16[320,1024]{1,0:T(8,128)(2,1)} %grad_ref.3) | copy-start | bytes 1966084
  41.4 21.9 %copy-start.2 = (f32[1024]{0:T(1024)S(1)}, f32[1024]{0:T(1024)}, u32[]{:S(2)}) copy-start(f32[1024]{0:T(1024)} %param.17) | copy-start | bytes 12292
  41.4 21.9 %copy-start.3 = (f32[1024]{0:T(1024)S(1)}, f32[1024]{0:T(1024)}, u32[]{:S(2)}) copy-start(f32[1024]{0:T(1024)} %param.18) | copy-start | bytes 12292
  41.4 26.2 %copy-start.5 = (bf16[1,1024,2048]{2,1,0:T(8,128)(2,1)S(1)}, bf16[1,1024,2048]{2,1,0:T(8,128)(2,1)}, u32[]{:S(2)}) copy-start(bf16[1,1024,2048]{2,1,0:T(8,128)(2,1)} %param.21) | copy-start | bytes 12582916
  64.5 2.9 %collective-permute-start.2 = (bf16[320,1024]{1,0:T(8,128)(2,1)S(1)}, bf16[320,1024]{1,0:T(8,128)(2,1)S(1)}, u32[]{:S(2)}, u32[]{:S(2)}) collective-permute-start(bf16[320,1024]{1,0:T(8,128)(2,1)S(1)} %get-tuple-element.127.h2_ref), channel_id=1, source_target_pairs={{0,1},{1,0},{2,3},{3,2},{4,5},{5,4},{6,7},{7,6},{8,9},{9,8},{10,11... | collective-permute-start | bytes 1966088 | tf_op jit(solution)/shard_map/ppermute | solution.py:849
  64.7 3.0 %collective-permute-start.3 = (bf16[320,1024]{1,0:T(8,128)(2,1)S(1)}, bf16[320,1024]{1,0:T(8,128)(2,1)S(1)}, u32[]{:S(2)}, u32[]{:S(2)}) collective-permute-start(bf16[320,1024]{1,0:T(8,128)(2,1)S(1)} %get-tuple-element.128.up_ref), channel_id=1, source_target_pairs={{0,1},{1,0},{2,3},{3,2},{4,5},{5,4},{6,7},{7,6},{8,9},{9,8},{10,11... | collective-permute-start | bytes 1966088 | tf_op jit(solution)/shard_map/ppermute | solution.py:849
  65.1 15.0 %collective-permute-start.4 = (bf16[256,1024]{1,0:T(8,128)(2,1)}, bf16[256,1024]{1,0:T(8,128)(2,1)S(1)}, u32[]{:S(2)}, u32[]{:S(2)}) collective-permute-start(bf16[256,1024]{1,0:T(8,128)(2,1)} %get-tuple-element.141), channel_id=1, source_target_pairs={{0,6},{2,4},{4,2},{6,0},{8,14},{10,12},{12,10},{14,8},{16,22},{18,... | collective-permute-start | bytes 1572872 | tf_op jit(solution)/shard_map/ppermute | solution.py:849
  80.1 12.1 %copy-start.8 = (bf16[256,1024]{1,0:T(8,128)(2,1)}, bf16[256,1024]{1,0:T(8,128)(2,1)S(1)}, u32[]{:S(2)}) copy-start(bf16[256,1024]{1,0:T(8,128)(2,1)S(1)} %collective-permute-done.4.refs_7_) | copy-start | bytes 1572868
  80.1 2.1 collective-permute-start.5
  82.2 6.9 %copy-start.17 = (bf16[256,1024]{1,0:T(8,128)(2,1)S(1)}, bf16[256,1024]{1,0:T(8,128)(2,1)}, u32[]{:S(2)}) copy-start(bf16[256,1024]{1,0:T(8,128)(2,1)} %get-tuple-element.141) | copy-start | bytes 1572868
  85.4 26.3 %all-to-all-start.2 = ((bf16[32,8,1280]{2,1,0:T(8,128)(2,1)}), bf16[32,8,1280]{2,1,0:T(8,128)(2,1)S(1)}, u32[]{:S(2)}, u32[]{:S(2)}) async-start(bf16[32,8,1280]{2,1,0:T(8,128)(2,1)} %bitcast.14), calls=%async_computation.2 | async-start | bytes 1310720 | tf_op jit(solution)/shard_map/all_to_all | solution.py:964
  89.1 20.9 %collective-permute-start.6 = (bf16[256,1024]{1,0:T(8,128)(2,1)S(1)}, bf16[256,1024]{1,0:T(8,128)(2,1)S(1)}, u32[]{:S(2)}, u32[]{:S(2)}) collective-permute-start(bf16[256,1024]{1,0:T(8,128)(2,1)S(1)} %copy-done.17), channel_id=1, source_target_pairs={{0,2},{2,0},{4,6},{6,4},{8,10},{10,8},{12,14},{14,12},{16,18},{18,... | collective-permute-start | bytes 1572872 | tf_op jit(solution)/shard_map/ppermute | solution.py:849
  90.7 19.5 %collective-permute-start.7 = (bf16[256,1024]{1,0:T(8,128)(2,1)S(1)}, bf16[256,1024]{1,0:T(8,128)(2,1)S(1)}, u32[]{:S(2)}, u32[]{:S(2)}) collective-permute-start(bf16[256,1024]{1,0:T(8,128)(2,1)S(1)} %copy-done.17), channel_id=1, source_target_pairs={{0,4},{2,6},{4,0},{6,2},{8,12},{10,14},{12,8},{14,10},{16,20},{18,... | collective-permute-start | bytes 1572872 | tf_op jit(solution)/shard_map/ppermute | solution.py:849
  92.2 19.4 %collective-permute-start.8 = (bf16[256,1024]{1,0:T(8,128)(2,1)S(1)}, bf16[256,1024]{1,0:T(8,128)(2,1)}, u32[]{:S(2)}, u32[]{:S(2)}) collective-permute-start(bf16[256,1024]{1,0:T(8,128)(2,1)S(1)} %collective-permute-done.4.refs_7_), channel_id=1, source_target_pairs={{0,1},{1,0},{2,3},{3,2},{4,5},{5,4},{6,7},{7,6},{8,9},{9,8},{10,11... | collective-permute-start | bytes 1572872 | tf_op jit(solution)/shard_map/ppermute | solution.py:849
  110.0 0.8 copy-start.9
  110.8 0.8 copy-start.11
  111.6 1.0 copy-start.10
  111.6 1.4 copy-start.12
  112.4 2.0 collective-permute-start.9
  112.7 17.6 %collective-permute-start.13 = (bf16[256,1024]{1,0:T(8,128)(2,1)S(1)}, bf16[256,1024]{1,0:T(8,128)(2,1)S(1)}, u32[]{:S(2)}, u32[]{:S(2)}) collective-permute-start(bf16[256,1024]{1,0:T(8,128)(2,1)S(1)} %copy-done.10), channel_id=1, source_target_pairs={{0,1},{1,0},{2,3},{3,2},{4,5},{5,4},{6,7},{7,6},{8,9},{9,8},{10,11... | collective-permute-start | bytes 1572872 | tf_op jit(solution)/shard_map/ppermute | solution.py:849
  113.0 17.2 %collective-permute-start.14 = (bf16[256,1024]{1,0:T(8,128)(2,1)S(1)}, bf16[256,1024]{1,0:T(8,128)(2,1)S(1)}, u32[]{:S(2)}, u32[]{:S(2)}) collective-permute-start(bf16[256,1024]{1,0:T(8,128)(2,1)S(1)} %copy-done.12), channel_id=1, source_target_pairs={{0,1},{1,0},{2,3},{3,2},{4,5},{5,4},{6,7},{7,6},{8,9},{9,8},{10,11... | collective-permute-start | bytes 1572872 | tf_op jit(solution)/shard_map/ppermute | solution.py:849
  117.7 12.5 %collective-permute-start.10 = (bf16[4,256,128]{2,1,0:T(8,128)(2,1)}, bf16[4,256,128]{2,1,0:T(8,128)(2,1)S(1)}, u32[]{:S(2)}, u32[]{:S(2)}) collective-permute-start(bf16[4,256,128]{2,1,0:T(8,128)(2,1)} %get-tuple-element.157), channel_id=1, source_target_pairs={{0,2},{2,0},{4,6},{6,4},{8,10},{10,8},{12,14},{14,12},{16,18},{18,... | collective-permute-start | bytes 786440 | tf_op jit(solution)/shard_map/ppermute | solution.py:849
  118.5 12.9 %collective-permute-start.11 = (bf16[4,256,128]{2,1,0:T(8,128)(2,1)}, bf16[4,256,128]{2,1,0:T(8,128)(2,1)S(1)}, u32[]{:S(2)}, u32[]{:S(2)}) collective-permute-start(bf16[4,256,128]{2,1,0:T(8,128)(2,1)} %get-tuple-element.158), channel_id=1, source_target_pairs={{0,4},{2,6},{4,0},{6,2},{8,12},{10,14},{12,8},{14,10},{16,20},{18,... | collective-permute-start | bytes 786440 | tf_op jit(solution)/shard_map/ppermute | solution.py:849
  119.8 13.0 %collective-permute-start.12 = (bf16[4,256,128]{2,1,0:T(8,128)(2,1)}, bf16[4,256,128]{2,1,0:T(8,128)(2,1)S(1)}, u32[]{:S(2)}, u32[]{:S(2)}) collective-permute-start(bf16[4,256,128]{2,1,0:T(8,128)(2,1)} %get-tuple-element.159), channel_id=1, source_target_pairs={{0,6},{2,4},{4,2},{6,0},{8,14},{10,12},{12,10},{14,8},{16,22},{18,... | collective-permute-start | bytes 786440 | tf_op jit(solution)/shard_map/ppermute | solution.py:849
  130.2 12.2 %copy-start.13 = (bf16[256,1024]{1,0:T(8,128)(2,1)}, bf16[256,1024]{1,0:T(8,128)(2,1)S(1)}, u32[]{:S(2)}) copy-start(bf16[256,1024]{1,0:T(8,128)(2,1)S(1)} %collective-permute-done.13.refs_8_) | copy-start | bytes 1572868
  130.2 12.2 %copy-start.14 = (bf16[256,1024]{1,0:T(8,128)(2,1)}, bf16[256,1024]{1,0:T(8,128)(2,1)S(1)}, u32[]{:S(2)}) copy-start(bf16[256,1024]{1,0:T(8,128)(2,1)S(1)} %collective-permute-done.14.refs_9_) | copy-start | bytes 1572868
  132.9 3.5 %collective-permute-start.19 = (bf16[256,1024]{1,0:T(8,128)(2,1)S(1)}, bf16[256,1024]{1,0:T(8,128)(2,1)S(1)}, u32[]{:S(2)}, u32[]{:S(2)}) collective-permute-start(bf16[256,1024]{1,0:T(8,128)(2,1)S(1)} %get-tuple-element.168), channel_id=1, source_target_pairs={{0,1},{1,0},{2,3},{3,2},{4,5},{5,4},{6,7},{7,6},{8,9},{9,8},{10,11... | collective-permute-start | bytes 1572872 | tf_op jit(solution)/shard_map/ppermute | solution.py:849
  132.9 6.5 %collective-permute-start.15 = (bf16[512,128]{1,0:T(8,128)(2,1)}, bf16[512,128]{1,0:T(8,128)(2,1)S(1)}, u32[]{:S(2)}, u32[]{:S(2)}) collective-permute-start(bf16[512,128]{1,0:T(8,128)(2,1)} %get-tuple-element.164), channel_id=1, source_target_pairs={{0,2},{2,0},{4,6},{6,4},{8,10},{10,8},{12,14},{14,12},{16,18},{18,... | collective-permute-start | bytes 393224 | tf_op jit(solution)/shard_map/ppermute | solution.py:849
  133.7 8.6 %collective-permute-start.16 = (bf16[512,128]{1,0:T(8,128)(2,1)}, bf16[512,128]{1,0:T(8,128)(2,1)S(1)}, u32[]{:S(2)}, u32[]{:S(2)}) collective-permute-start(bf16[512,128]{1,0:T(8,128)(2,1)} %get-tuple-element.165), channel_id=1, source_target_pairs={{0,4},{2,6},{4,0},{6,2},{8,12},{10,14},{12,8},{14,10},{16,20},{18,... | collective-permute-start | bytes 393224 | tf_op jit(solution)/shard_map/ppermute | solution.py:849
  135.2 7.2 %collective-permute-start.17 = (bf16[512,128]{1,0:T(8,128)(2,1)}, bf16[512,128]{1,0:T(8,128)(2,1)S(1)}, u32[]{:S(2)}, u32[]{:S(2)}) collective-permute-start(bf16[512,128]{1,0:T(8,128)(2,1)} %get-tuple-element.166), channel_id=1, source_target_pairs={{0,6},{2,4},{4,2},{6,0},{8,14},{10,12},{12,10},{14,8},{16,22},{18,... | collective-permute-start | bytes 393224 | tf_op jit(solution)/shard_map/ppermute | solution.py:849
  142.4 45.9 %all-to-all-start.3 = ((bf16[32,8,1280]{2,1,0:T(8,128)(2,1)}), bf16[32,8,1280]{2,1,0:T(8,128)(2,1)S(1)}, u32[]{:S(2)}, u32[]{:S(2)}) async-start(bf16[32,8,1280]{2,1,0:T(8,128)(2,1)} %bitcast.16), calls=%async_computation.3 | async-start | bytes 1310720 | tf_op jit(solution)/shard_map/all_to_all | solution.py:964
  147.2 5.0 %copy-start.20 = (bf16[2,512,128]{2,1,0:T(8,128)(2,1)S(1)}, bf16[2,512,128]{2,1,0:T(8,128)(2,1)}, u32[]{:S(2)}) copy-start(bf16[2,512,128]{2,1,0:T(8,128)(2,1)} %get-tuple-element.188) | copy-start | bytes 786436
  147.2 6.4 %copy-start.19 = (bf16[2,512,128]{2,1,0:T(8,128)(2,1)S(1)}, bf16[2,512,128]{2,1,0:T(8,128)(2,1)}, u32[]{:S(2)}) copy-start(bf16[2,512,128]{2,1,0:T(8,128)(2,1)} %get-tuple-element.189) | copy-start | bytes 786436
  147.3 7.9 %copy-start.18 = (bf16[2,512,128]{2,1,0:T(8,128)(2,1)S(1)}, bf16[2,512,128]{2,1,0:T(8,128)(2,1)}, u32[]{:S(2)}) copy-start(bf16[2,512,128]{2,1,0:T(8,128)(2,1)} %get-tuple-element.190) | copy-start | bytes 786436
  150.6 15.4 %collective-permute-start.23 = (bf16[2,512,128]{2,1,0:T(8,128)(2,1)S(1)}, bf16[2,512,128]{2,1,0:T(8,128)(2,1)S(1)}, u32[]{:S(2)}, u32[]{:S(2)}) collective-permute-start(bf16[2,512,128]{2,1,0:T(8,128)(2,1)S(1)} %get-tuple-element.176), channel_id=1, source_target_pairs={{0,8},{2,10},{4,12},{6,14},{8,0},{10,2},{12,4},{14,6},{16,24},{18,... | collective-permute-start | bytes 786440 | tf_op jit(solution)/shard_map/ppermute | solution.py:849
  152.2 16.9 %collective-permute-start.20 = (bf16[2,512,128]{2,1,0:T(8,128)(2,1)S(1)}, bf16[2,512,128]{2,1,0:T(8,128)(2,1)S(1)}, u32[]{:S(2)}, u32[]{:S(2)}) collective-permute-start(bf16[2,512,128]{2,1,0:T(8,128)(2,1)S(1)} %copy-done.20), channel_id=1, source_target_pairs={{0,2},{2,0},{4,6},{6,4},{8,10},{10,8},{12,14},{14,12},{16,18},{18,... | collective-permute-start | bytes 786440 | tf_op jit(solution)/shard_map/ppermute | solution.py:849
  153.7 16.3 %collective-permute-start.21 = (bf16[2,512,128]{2,1,0:T(8,128)(2,1)S(1)}, bf16[2,512,128]{2,1,0:T(8,128)(2,1)S(1)}, u32[]{:S(2)}, u32[]{:S(2)}) collective-permute-start(bf16[2,512,128]{2,1,0:T(8,128)(2,1)S(1)} %copy-done.19), channel_id=1, source_target_pairs={{0,4},{2,6},{4,0},{6,2},{8,12},{10,14},{12,8},{14,10},{16,20},{18,... | collective-permute-start | bytes 786440 | tf_op jit(solution)/shard_map/ppermute | solution.py:849
  155.2 14.8 %collective-permute-start.22 = (bf16[2,512,128]{2,1,0:T(8,128)(2,1)S(1)}, bf16[2,512,128]{2,1,0:T(8,128)(2,1)S(1)}, u32[]{:S(2)}, u32[]{:S(2)}) collective-permute-start(bf16[2,512,128]{2,1,0:T(8,128)(2,1)S(1)} %copy-done.18), channel_id=1, source_target_pairs={{0,6},{2,4},{4,2},{6,0},{8,14},{10,12},{12,10},{14,8},{16,22},{18,... | collective-permute-start | bytes 786440 | tf_op jit(solution)/shard_map/ppermute | solution.py:849
  166.6 8.6 %collective-permute-start.25 = (bf16[1,512,128]{2,1,0:T(8,128)(2,1)S(1)}, bf16[1,512,128]{2,1,0:T(8,128)(2,1)S(1)}, u32[]{:S(2)}, u32[]{:S(2)}) collective-permute-start(bf16[1,512,128]{2,1,0:T(8,128)(2,1)S(1)} %get-tuple-element.193), channel_id=1, source_target_pairs={{0,16},{2,18},{4,20},{6,22},{8,24},{10,26},{12,28},{14,30},{16,0},... | collective-permute-start | bytes 393224 | tf_op jit(solution)/shard_map/ppermute | solution.py:849
  173.7 10.6 %collective-permute-start.24 = (bf16[2,512,128]{2,1,0:T(8,128)(2,1)S(1)}, bf16[2,512,128]{2,1,0:T(8,128)(2,1)S(1)}, u32[]{:S(2)}, u32[]{:S(2)}) collective-permute-start(bf16[2,512,128]{2,1,0:T(8,128)(2,1)S(1)} %get-tuple-element.198), channel_id=1, source_target_pairs={{0,8},{2,10},{4,12},{6,14},{8,0},{10,2},{12,4},{14,6},{16,24},{18,... | collective-permute-start | bytes 786440 | tf_op jit(solution)/shard_map/ppermute | solution.py:849
  175.3 9.6 %collective-permute-start.27 = (bf16[512,128]{1,0:T(8,128)(2,1)S(1)}, bf16[512,128]{1,0:T(8,128)(2,1)S(1)}, u32[]{:S(2)}, u32[]{:S(2)}) collective-permute-start(bf16[512,128]{1,0:T(8,128)(2,1)S(1)} %last_add.1.own_ref), channel_id=1, source_target_pairs={{0,16},{2,18},{4,20},{6,22},{8,24},{10,26},{12,28},{14,30},{16,0},... | collective-permute-start | bytes 393224 | tf_op jit(solution)/shard_map/ppermute | solution.py:849
  184.9 9.3 %collective-permute-start.31 = (bf16[1024,128]{1,0:T(8,128)(2,1)S(1)}, bf16[1024,128]{1,0:T(8,128)(2,1)S(1)}, u32[]{:S(2)}, u32[]{:S(2)}) collective-permute-start(bf16[1024,128]{1,0:T(8,128)(2,1)S(1)} %stack.20.own_ref), channel_id=1, source_target_pairs={{0,8},{2,10},{4,12},{6,14},{8,0},{10,2},{12,4},{14,6},{16,24},{18,... | collective-permute-start | bytes 786440 | tf_op jit(solution)/shard_map/ppermute | solution.py:849
  186.0 6.7 %collective-permute-start.26 = (bf16[1,512,128]{2,1,0:T(8,128)(2,1)S(1)}, bf16[1,512,128]{2,1,0:T(8,128)(2,1)S(1)}, u32[]{:S(2)}, u32[]{:S(2)}) collective-permute-start(bf16[1,512,128]{2,1,0:T(8,128)(2,1)S(1)} %get-tuple-element.203), channel_id=1, source_target_pairs={{0,16},{2,18},{4,20},{6,22},{8,24},{10,26},{12,28},{14,30},{16,0},... | collective-permute-start | bytes 393224 | tf_op jit(solution)/shard_map/ppermute | solution.py:849
  188.3 4.4 %collective-permute-start.29 = (f32[16,128]{1,0:T(8,128)S(1)}, f32[16,128]{1,0:T(8,128)S(1)}, u32[]{:S(2)}, u32[]{:S(2)}) collective-permute-start(f32[16,128]{1,0:T(8,128)S(1)} %get-tuple-element.207.refs_2_), channel_id=1, source_target_pairs={{0,1},{1,0},{2,3},{3,2},{4,5},{5,4},{6,7},{7,6},{8,9},{9,8},{10,11... | collective-permute-start | bytes 24584 | tf_op jit(solution)/shard_map/ppermute | solution.py:849
  188.3 10.6 %copy-start.16 = (bf16[320,1024]{1,0:T(8,128)(2,1)S(1)}, bf16[320,1024]{1,0:T(8,128)(2,1)}, u32[]{:S(2)}) copy-start(bf16[320,1024]{1,0:T(8,128)(2,1)} %get-tuple-element.179) | copy-start | bytes 1966084
  192.3 1.3 collective-permute-start.28
  194.2 22.9 %copy-start.15 = (bf16[320,1024]{1,0:T(8,128)(2,1)S(1)}, bf16[320,1024]{1,0:T(8,128)(2,1)}, u32[]{:S(2)}) copy-start(bf16[320,1024]{1,0:T(8,128)(2,1)} %get-tuple-element.178) | copy-start | bytes 1966084
  194.2 13.7 %collective-permute-start.33 = (bf16[2048,128]{1,0:T(8,128)(2,1)S(1)}, bf16[2048,128]{1,0:T(8,128)(2,1)S(1)}, u32[]{:S(2)}, u32[]{:S(2)}) collective-permute-start(bf16[2048,128]{1,0:T(8,128)(2,1)S(1)} %stack.21.refs_0_), channel_id=1, source_target_pairs={{0,2},{2,0},{4,6},{6,4},{8,10},{10,8},{12,14},{14,12},{16,18},{18,... | collective-permute-start | bytes 1572872 | tf_op jit(solution)/shard_map/ppermute | solution.py:849
  195.2 13.3 %collective-permute-start.34 = (bf16[2048,128]{1,0:T(8,128)(2,1)S(1)}, bf16[2048,128]{1,0:T(8,128)(2,1)S(1)}, u32[]{:S(2)}, u32[]{:S(2)}) collective-permute-start(bf16[2048,128]{1,0:T(8,128)(2,1)S(1)} %stack.21.refs_0_), channel_id=1, source_target_pairs={{0,4},{2,6},{4,0},{6,2},{8,12},{10,14},{12,8},{14,10},{16,20},{18,... | collective-permute-start | bytes 1572872 | tf_op jit(solution)/shard_map/ppermute | solution.py:849
  196.9 9.2 %collective-permute-start.30 = (bf16[576,128]{1,0:T(8,128)(2,1)S(1)}, bf16[576,128]{1,0:T(8,128)(2,1)S(1)}, u32[]{:S(2)}, u32[]{:S(2)}) collective-permute-start(bf16[576,128]{1,0:T(8,128)(2,1)S(1)} %last_add_sums.1.own_ref), channel_id=1, source_target_pairs={{0,16},{2,18},{4,20},{6,22},{8,24},{10,26},{12,28},{14,30},{16,0},... | collective-permute-start | bytes 442376 | tf_op jit(solution)/shard_map/ppermute | solution.py:849
  198.9 18.3 %collective-permute-start.18 = (bf16[320,1024]{1,0:T(8,128)(2,1)S(1)}, bf16[320,1024]{1,0:T(8,128)(2,1)S(1)}, u32[]{:S(2)}, u32[]{:S(2)}) collective-permute-start(bf16[320,1024]{1,0:T(8,128)(2,1)S(1)} %copy-done.16), channel_id=1, source_target_pairs={{0,1},{1,0},{2,3},{3,2},{4,5},{5,4},{6,7},{7,6},{8,9},{9,8},{10,11... | collective-permute-start | bytes 1966088 | tf_op jit(solution)/shard_map/ppermute | solution.py:849
  206.1 6.6 %collective-permute-start.32 = (bf16[1088,128]{1,0:T(8,128)(2,1)S(1)}, bf16[1088,128]{1,0:T(8,128)(2,1)S(1)}, u32[]{:S(2)}, u32[]{:S(2)}) collective-permute-start(bf16[1088,128]{1,0:T(8,128)(2,1)S(1)} %stack.22.own_ref), channel_id=1, source_target_pairs={{0,8},{2,10},{4,12},{6,14},{8,0},{10,2},{12,4},{14,6},{16,24},{18,... | collective-permute-start | bytes 835592 | tf_op jit(solution)/shard_map/ppermute | solution.py:849
  212.8 18.0 %collective-permute-start.35 = (bf16[2112,128]{1,0:T(8,128)(2,1)S(1)}, bf16[2112,128]{1,0:T(8,128)(2,1)S(1)}, u32[]{:S(2)}, u32[]{:S(2)}) collective-permute-start(bf16[2112,128]{1,0:T(8,128)(2,1)S(1)} %stack.23.refs_0_), channel_id=1, source_target_pairs={{0,2},{2,0},{4,6},{6,4},{8,10},{10,8},{12,14},{14,12},{16,18},{18,... | collective-permute-start | bytes 1622024 | tf_op jit(solution)/shard_map/ppermute | solution.py:849
  213.3 17.4 %collective-permute-start.36 = (bf16[2112,128]{1,0:T(8,128)(2,1)S(1)}, bf16[2112,128]{1,0:T(8,128)(2,1)S(1)}, u32[]{:S(2)}, u32[]{:S(2)}) collective-permute-start(bf16[2112,128]{1,0:T(8,128)(2,1)S(1)} %stack.23.refs_0_), channel_id=1, source_target_pairs={{0,4},{2,6},{4,0},{6,2},{8,12},{10,14},{12,8},{14,10},{16,20},{18,... | collective-permute-start | bytes 1622024 | tf_op jit(solution)/shard_map/ppermute | solution.py:849
  214.3 15.8 %collective-permute-start.37 = (bf16[1024,128]{1,0:T(8,128)(2,1)S(1)}, bf16[1024,128]{1,0:T(8,128)(2,1)S(1)}, u32[]{:S(2)}, u32[]{:S(2)}) collective-permute-start(bf16[1024,128]{1,0:T(8,128)(2,1)S(1)} %slice.16), channel_id=1, source_target_pairs={{0,2},{2,0},{4,6},{6,4},{8,10},{10,8},{12,14},{14,12},{16,18},{18,... | collective-permute-start | bytes 786440 | tf_op jit(solution)/shard_map/ppermute | solution.py:849
  215.4 15.4 %collective-permute-start.38 = (bf16[1024,128]{1,0:T(8,128)(2,1)S(1)}, bf16[1024,128]{1,0:T(8,128)(2,1)S(1)}, u32[]{:S(2)}, u32[]{:S(2)}) collective-permute-start(bf16[1024,128]{1,0:T(8,128)(2,1)S(1)} %slice.17), channel_id=1, source_target_pairs={{0,4},{2,6},{4,0},{6,2},{8,12},{10,14},{12,8},{14,10},{16,20},{18,... | collective-permute-start | bytes 786440 | tf_op jit(solution)/shard_map/ppermute | solution.py:849
  230.8 6.5 %collective-permute-start.39 = (bf16[1056,128]{1,0:T(8,128)(2,1)S(1)}, bf16[1056,128]{1,0:T(8,128)(2,1)S(1)}, u32[]{:S(2)}, u32[]{:S(2)}) collective-permute-start(bf16[1056,128]{1,0:T(8,128)(2,1)S(1)} %slice.18), channel_id=1, source_target_pairs={{0,2},{2,0},{4,6},{6,4},{8,10},{10,8},{12,14},{14,12},{16,18},{18,... | collective-permute-start | bytes 811016 | tf_op jit(solution)/shard_map/ppermute | solution.py:849
  231.8 6.5 %collective-permute-start.40 = (bf16[1056,128]{1,0:T(8,128)(2,1)S(1)}, bf16[1056,128]{1,0:T(8,128)(2,1)S(1)}, u32[]{:S(2)}, u32[]{:S(2)}) collective-permute-start(bf16[1056,128]{1,0:T(8,128)(2,1)S(1)} %slice.19), channel_id=1, source_target_pairs={{0,4},{2,6},{4,0},{6,2},{8,12},{10,14},{12,8},{14,10},{16,20},{18,... | collective-permute-start | bytes 811016 | tf_op jit(solution)/shard_map/ppermute | solution.py:849

commit v5 on v4

--- a/solution.py
+++ b/solution.py
@@ -331,7 +331,7 @@
 
 def out_grad_kernel(where_ref, own_ref, other_ref, context_far, dattn_ref, *rest):
     piece_fars, (context_ref, grad_ref, piece_ref, sems) = rest[:4], rest[4:]
-    arriving = started(context_far, context_ref, sems.at[4])
+    arriving = started(context_far, context_ref, sems.at[1])
     half = own_ref.shape[0]
     here = where_ref[0]
     dattn_ref[pl.ds(pl.multiple_of(here * half, half), half), :] = own_ref[...]
@@ -340,20 +340,18 @@
     grad_ref[...] = dot_tn(context_ref[...], dattn_ref[...])
     width = grad_ref.shape[1]
     quarter = grad_ref.shape[0] // 4
-    owners = piece_ref.shape[1]
+    owners = piece_ref.shape[0]
     rows = quarter // owners
-    leaving = []
-    for step in (1, 2, 3, 0):
+    for step in range(4):
         first = (where_ref[1] ^ step) * quarter
         for owner in range(owners):
             start = pl.multiple_of(first + owner * rows, rows)
             block = grad_ref[pl.ds(start, rows), :]
-            piece_ref[step, owner] = jnp.concatenate(
+            target_ref = piece_fars[step] if step else piece_ref
+            target_ref[owner] = jnp.concatenate(
                 [block[:, at : at + 128] for at in range(0, width, 128)], axis=0
             ).astype(BF16)
-        leaving.append(started(piece_ref.at[step], piece_fars[step], sems.at[step]))
-    for copy in leaving:
-        copy.wait()
+    started(piece_ref, piece_fars[0], sems.at[0]).wait()
 
 
 def attend_back_kernel(
@@ -652,15 +650,15 @@
 def finish_near_kernel(where_ref, *refs, digits, sums):
     qkv_ref, sums_ref = refs[4:]
     width = qkv_ref.shape[1]
-    rows = width // 4 ** (digits - 1)
-
-    def use(column, owner, load):
-        lanes = pl.ds(pl.multiple_of(column * 128, 128), 128)
-        down = pl.ds(pl.multiple_of(owner * rows, rows), rows)
-        qkv_ref[1, down, lanes] = load(0, rows).astype(F32)
-        qkv_ref[0, down, lanes] = load(rows, 2 * rows).astype(F32)
-
-    each_piece(where_ref, refs[:3], digits, rows, use, range(3))
+    owners = 4 ** (digits - 1)
+    rows = width // owners
+    for step in range(3):
+        lanes = pl.ds(pl.multiple_of((where_ref[1] ^ step) * 128, 128), 128)
+        for at in range(owners):
+            owner = place_rows(where_ref, digits, at)
+            down = pl.ds(pl.multiple_of(owner * rows, rows), rows)
+            start = pl.multiple_of((2 * at + 1 - pl.program_id(0)) * rows, rows)
+            qkv_ref[0, down, lanes] = refs[step][pl.ds(start, rows), :].astype(F32)
     total = refs[0].shape[0]
     sums_ref[...] = split_sum(refs[:3], total - sums, total)
 
@@ -1058,11 +1056,11 @@
         scratch=[
             pltpu.VMEM((span, columns), BF16),
             pltpu.VMEM((columns, width), F32),
-            pltpu.VMEM((4, n_exp // 4, piece, 128), BF16),
-            pltpu.SemaphoreType.DMA((5,)),
+            pltpu.VMEM((n_exp // 4, piece, 128), BF16),
+            pltpu.SemaphoreType.DMA((2,)),
         ],
         raw=(3,),
-        out_raw=range(1, 5),
+        out_raw=(1,),
     )
     out_parts = [out_pieces[0], *to_others(out_pieces, 0)]
     du_kept, du_sent, *parts = call(
@@ -1171,11 +1169,11 @@
     grad_qkv, sums = pl.pallas_call(
         functools.partial(finish_near_kernel, digits=digits, sums=extra),
         name="finish_near",
-        grid=(1,),
+        grid=(2,),
         out_shape=[whole_qkv, sums_shape],
         in_specs=[SMEM] + [VMEM] * 3 + [in_place],
         out_specs=[
-            pl.BlockSpec((2, width, columns), lambda i: (0, 0, 0)),
+            pl.BlockSpec((1, width, columns), lambda i: (i, 0, 0)),
             pl.BlockSpec((extra // 2, 128), lambda i: (0, 0)),
         ],
         input_output_aliases={4: 0},

time: 241 us -> 241 us (level)
  transfers between devices with their start and end apart: 43 -> 43, of which waited for: 25 -> 25; matrix products, arithmetic and copies ran while one was open for 1% -> 1% of each run, Pallas kernels for 27% -> 26%
where the time goes in v5:
time: 241 us; the launch traced here: 240 us
  Pallas kernels  83.2 us (35%)
  waiting for transfers between devices  58.8 us (24%)
  starting transfers between devices  47.9 us (20%)
  blocking collectives  46.3 us (19%)
    ppermute x41, waiting for transfers between devices, flip(): return lax.ppermute(value, axis, [(i, i ^ bit) for i in range(size)])  58.8 us
    all_to_all x2, blocking collectives, exchange(): lax.all_to_all(value, ('exp', 'head'), split_axis=0, concat_axis=0, tiled...  46.3 us
    pallas_call x21, Pallas kernels, call(): pl.pallas_call(kernel, name=name, out_shape=shapes, in_specs=[SMEM if at...  43.4 us
    ppermute x41, starting transfers between devices, flip(): return lax.ppermute(value, axis, [(i, i ^ bit) for i in range(size)])  39.3 us
    pallas_call x1, Pallas kernels, expert(): pl.pallas_call(expert_kernel, name='expert', grid=(units // tile,), out_s...  11.9 us
    pallas_call x1, Pallas kernels, expert_grads(): pl.pallas_call(expert_grad_kernel, name='expert_grads', grid=(units // ti...  11.6 us
    all_to_all x2, starting transfers between devices, exchange(): lax.all_to_all(value, ('exp', 'head'), split_axis=0, concat_axis=0, tiled...  8.57 us
    pallas_call x1, Pallas kernels, expert_branch(): pl.pallas_call(branch_kernel, name='expert_branch', grid=(units // tile,)...  6.91 us
  transfers between devices with their start and end apart: 43, of which 25 were waited for; matrix products, arithmetic and copies ran while one was open for 1% of the time, Pallas kernels for 26%

profile of v5, /device:TPU:0, one launch (start us, length us, event | category | flops | bytes accessed | tf_op | source)
XLA Modules:
  0.0 240.4 jit_solution(7488692752524497371)
XLA Ops:
  0.7 2.5 %norm1.1 = bf16[256,1280]{1,0:T(8,128)(2,1)S(1)} custom-call(bf16[320,1024]{1,0:T(8,128)(2,1)} %x_ref.5, f32[1,1024]{1,0:T(1,128)} %bitcast.40, f32[1,1024]{1,0:T(1,128)} %bitcast.42), custom_call_target="tpu_custom_call" | custom-call | flops 503316480 | bytes 1318912 | tf_op jit(solution)/shard_map/norm1/pallas_call | solution.py:744
  3.2 25.0 %all_to_all.20 = bf16[32,8,1280]{2,1,0:T(8,128)(2,1)S(1)} all-to-all(bf16[32,8,1280]{2,1,0:T(8,128)(2,1)S(1)} %bitcast.29), channel_id=1, replica_groups=mesh['exp'=16,'head'=2] {'exp','head'}, dimensions={0} | all-to-all | bytes 1310720 | tf_op jit(solution)/shard_map/all_to_all | solution.py:962
  29.2 1.8 collective-permute-done.other_ref
  30.9 8.5 %attend.1 = (bf16[256,1024]{1,0:T(8,128)(2,1)}, bf16[512,1024]{1,0:T(8,128)(2,1)}, bf16[3,512,512]{2,1,0:T(8,128)(2,1)}, bf16[512,512]{1,0:T(8,128)(2,1)}, f32[1...) custom-call(s32[3]{0:T(128)S(1)} %pad_add_fusion.where_ref, s32[1,5]{1,0:T(1,128)S(1)} %copy-done.7, ...), custom_call_target="tpu_custom_call" | custom-call | flops 4294967296 | bytes 10747936 | tf_op jit(solution)/shard_map/attend/pallas_call | solution.py:744
  39.6 1.8 collective-permute-done.1.came_ref
  42.1 21.2 %all_to_all.21 = bf16[32,8,1280]{2,1,0:T(8,128)(2,1)S(1)} all-to-all(bf16[32,8,1280]{2,1,0:T(8,128)(2,1)S(1)} %bitcast.26), channel_id=1, replica_groups=mesh['exp'=16,'head'=2] {'exp','head'}, dimensions={0} | all-to-all | bytes 1310720 | tf_op jit(solution)/shard_map/all_to_all | solution.py:962
  63.3 1.2 norm2.1
  65.1 2.3 collective-permute-start.4
  67.6 11.9 %expert.1 = (bf16[640,2048]{1,0:T(8,128)(2,1)}, bf16[640,2048]{1,0:T(8,128)(2,1)}, f32[320,1024]{1,0:T(8,128)S(1)}, bf16[320,1024]{1,0:T(8,128)(2,1)S(1)}, bf16[...) custom-call(bf16[320,1024]{1,0:T(8,128)(2,1)S(1)} %get-tuple-element.127.h2_ref, ...), custom_call_target="tpu_custom_call" | custom-call | flops 8053063680 | bytes 16777216 | tf_op jit(solution)/shard_map/expert/pallas_call | solution.py:774
  80.1 2.1 collective-permute-done.5.came_ref
  82.2 3.1 %norm2_back.1 = (f32[320,1024]{1,0:T(8,128)}, bf16[256,1280]{1,0:T(8,128)(2,1)}, f32[16,128]{1,0:T(8,128)S(1)}) custom-call(f32[320,1024]{1,0:T(8,128)S(1)} %get-tuple-element.131.kept_ref, bf16[320,1024]{1,0:T(8,128)(2,1)S(1)} %collective-permute-done.5.came_ref, f32[320,1024]{1,0:T(8,128)S(1)} %get-tuple-element.124.resid_ref, ...), custom_call_target="tpu_custom_call" | custom-call | flops 503316480 | bytes 5910528 | tf_op jit(solution)/shard_map/norm2_back/pallas_call | solution.py:744
  85.4 3.7 %all-to-all-start.2 = ((bf16[32,8,1280]{2,1,0:T(8,128)(2,1)}), bf16[32,8,1280]{2,1,0:T(8,128)(2,1)S(1)}, u32[]{:S(2)}, u32[]{:S(2)}) async-start(bf16[32,8,1280]{2,1,0:T(8,128)(2,1)} %bitcast.14), calls=%async_computation.2 | async-start | bytes 1310720 | tf_op jit(solution)/shard_map/all_to_all | solution.py:962
  89.1 1.6 collective-permute-start.6
  90.7 1.5 collective-permute-start.7
  92.2 11.6 %expert_grads.1 = (f32[1024,2048]{1,0:T(8,128)}, f32[2048,1024]{1,0:T(8,128)}) custom-call(bf16[640,1024]{1,0:T(8,128)(2,1)} %get-tuple-element.136.rows_ref, bf16[640,1024]{1,0:T(8,128)(2,1)} %get-tuple-element.137.grads_ref, bf16[640,2048]{1,0:T(8,128)(2,1)} %get-tuple-element.177.hidden_ref, bf16[640,2048]{1,0:T(8,128)(2,1)} %get-tuple-element.138.dpre_ref), custom_call_target="tpu_custom_call" | custom-call | flops 5368709120 | bytes 25165824 | tf_op jit(solution)/shard_map/expert_grads/pallas_call | solution.py:804
  103.8 6.2 %collective-permute-done.6.refs_5_ = bf16[256,1024]{1,0:T(8,128)(2,1)S(1)} collective-permute-done((bf16[256,1024]{1,0:T(8,128)(2,1)S(1)}, bf16[256,1024]{1,0:T(8,128)(2,1)S(1)}, u32[]{:S(2)}, u32[]{:S(2)}) %collective-permute-start.6) | collective-permute-done | bytes 524320 | tf_op jit(solution)/shard_map/ppermute | solution.py:847
  110.8 0.8 copy-done.11
  113.2 1.2 collective-permute-done.9.other_ref
  114.4 3.1 %out_grad.1 = (bf16[512,1024]{1,0:T(8,128)(2,1)S(1)}, bf16[4,256,128]{2,1,0:T(8,128)(2,1)}, bf16[4,256,128]{2,1,0:T(8,128)(2,1)S(1)}, bf16[4,256,128]{2,1,0:T(8,128)(2,1)S(1)}, bf16[4,256,128]{2,1,0:T(8,128)(2,1)S(1)}) custom-call(s32[3]{0:T(128)S(1)} %pad_add_fusion.where_ref, bf16[256,1024]{1,0:T(8,128)(2,1)S(1)} %gather2.1.own_ref, ...), custom_call_target="tpu_custom_call" | custom-call | flops 536870912 | bytes 3670028 | tf_op jit(solution)/shard_map/out_grad/pallas_call | solution.py:744
  118.3 1.4 collective-permute-start.11
  119.6 1.5 collective-permute-start.12
  121.1 8.9 %attend_back.1 = (f32[256,1024]{1,0:T(8,128)S(1)}, bf16[256,1024]{1,0:T(8,128)(2,1)S(1)}, bf16[512,128]{1,0:T(8,128)(2,1)}, bf16[512,128]{1,0:T(8,128)(2,1)}, bf...) custom-call(s32[3]{0:T(128)S(1)} %pad_add_fusion.where_ref, ...), custom_call_target="tpu_custom_call" | custom-call | flops 7516192768 | bytes 10747936 | tf_op jit(solution)/shard_map/attend_back/pallas_call | solution.py:744
  130.1 0.8 collective-permute-done.11.refs_13_
  130.9 1.6 collective-permute-done.12.refs_14_
  132.5 0.9 collective-permute-start.15
  133.3 1.5 collective-permute-start.16
  134.8 1.2 collective-permute-start.17
  136.0 1.4 scatter2.1
  137.4 1.6 collective-permute-done.15.refs_1_
  139.0 3.0 %collective-permute-done.16.refs_2_ = bf16[512,128]{1,0:T(8,128)(2,1)S(1)} collective-permute-done((bf16[512,128]{1,0:T(8,128)(2,1)}, bf16[512,128]{1,0:T(8,128)(2,1)S(1)}, u32[]{:S(2)}, u32[]{:S(2)}) %collective-permute-start.16) | collective-permute-done | bytes 131104 | tf_op jit(solution)/shard_map/ppermute | solution.py:847
  142.0 4.8 %all-to-all-start.3 = ((bf16[32,8,1280]{2,1,0:T(8,128)(2,1)}), bf16[32,8,1280]{2,1,0:T(8,128)(2,1)S(1)}, u32[]{:S(2)}, u32[]{:S(2)}) async-start(bf16[32,8,1280]{2,1,0:T(8,128)(2,1)} %bitcast.16), calls=%async_computation.3 | async-start | bytes 1310720 | tf_op jit(solution)/shard_map/all_to_all | solution.py:962
  146.8 3.3 %value_grad.1 = (bf16[2,512,128]{2,1,0:T(8,128)(2,1)S(1)}, bf16[2,512,128]{2,1,0:T(8,128)(2,1)S(1)}) custom-call(s32[3]{0:T(128)S(1)} %pad_add_fusion.where_ref, bf16[512,128]{1,0:T(8,128)(2,1)} %get-tuple-element.163.refs_0_, bf16[512,128]{1,0:T(8,128)(2,1)S(1)} %collective-permute-done.15.refs_1_, bf16[512,128]{1,0:T(8,128)(2,1)S(1)} %collective-permute-done.16.refs_2_, ...), custom_call_target="tpu_custom_call" | custom-call | flops 536870912 | bytes 6291468 | tf_op jit(solution)/shard_map/value_grad/pallas_call | solution.py:744
  150.2 1.6 collective-permute-start.23
  151.8 1.5 collective-permute-start.20
  153.3 1.5 collective-permute-start.21
  155.3 6.9 %expert_branch.1 = (bf16[320,1024]{1,0:T(8,128)(2,1)}, bf16[320,1024]{1,0:T(8,128)(2,1)}) custom-call(bf16[640,2048]{1,0:T(8,128)(2,1)} %get-tuple-element.177.hidden_ref, bf16[2048,1024]{1,0:T(8,128)(2,1)} %bitcast.38), custom_call_target="tpu_custom_call" | custom-call | flops 2684354560 | bytes 8388608 | tf_op jit(solution)/shard_map/expert_branch/pallas_call | solution.py:827
  162.2 3.4 %collective-permute-done.23.came_ref = bf16[2,512,128]{2,1,0:T(8,128)(2,1)S(1)} collective-permute-done((bf16[2,512,128]{2,1,0:T(8,128)(2,1)S(1)}, bf16[2,512,128]{2,1,0:T(8,128)(2,1)S(1)}, u32[]{:S(2)}, u32[]{:S(2)}) %collective-permute-start.23) | collective-permute-done | bytes 262176 | tf_op jit(solution)/shard_map/ppermute | solution.py:847
  166.2 2.5 %collective-permute-start.25 = (bf16[1,512,128]{2,1,0:T(8,128)(2,1)S(1)}, bf16[1,512,128]{2,1,0:T(8,128)(2,1)S(1)}, u32[]{:S(2)}, u32[]{:S(2)}) collective-permute-start(bf16[1,512,128]{2,1,0:T(8,128)(2,1)S(1)} %get-tuple-element.193), channel_id=1, source_target_pairs={{0,16},{2,18},{4,20},{6,22},{8,24},{10,26},{12,28},{14,30},{16,0},... | collective-permute-start | bytes 393224 | tf_op jit(solution)/shard_map/ppermute | solution.py:847
  168.7 0.9 collective-permute-done.21.refs_2_
  169.5 3.7 %key_query_grad.1 = (bf16[2,512,128]{2,1,0:T(8,128)(2,1)S(1)}, bf16[2,512,128]{2,1,0:T(8,128)(2,1)S(1)}) custom-call(s32[3]{0:T(128)S(1)} %pad_add_fusion.where_ref, bf16[2,512,128]{2,1,0:T(8,128)(2,1)} %get-tuple-element.184.refs_0_, bf16[2,512,128]{2,1,0:T(8,128)(2,1)S(1)} %collective-permute-done.20.refs_1_, ...), custom_call_target="tpu_custom_call" | custom-call | flops 1073741824 | bytes 5767180 | tf_op jit(solution)/shard_map/key_query_grad/pallas_call | solution.py:744
  173.3 1.5 collective-permute-start.24
  174.9 1.8 collective-permute-start.27
  176.7 7.2 %collective-permute-done.24.came_ref = bf16[2,512,128]{2,1,0:T(8,128)(2,1)S(1)} collective-permute-done((bf16[2,512,128]{2,1,0:T(8,128)(2,1)S(1)}, bf16[2,512,128]{2,1,0:T(8,128)(2,1)S(1)}, u32[]{:S(2)}, u32[]{:S(2)}) %collective-permute-start.24) | collective-permute-done | bytes 262176 | tf_op jit(solution)/shard_map/ppermute | solution.py:847
  184.5 1.1 collective-permute-start.31
  185.6 2.3 collective-permute-start.26
  187.9 3.9 %norm1_back.1 = (f32[320,1024]{1,0:T(8,128)}, f32[16,128]{1,0:T(8,128)S(1)}) custom-call(bf16[256,1280]{1,0:T(8,128)(2,1)S(1)} %bitcast.24, bf16[320,1024]{1,0:T(8,128)(2,1)} %x_ref.5, f32[320,1024]{1,0:T(8,128)} %get-tuple-element.182.dresid_ref, f32[1,1024]{1,0:T(1,128)} %bitcast.41), custom_call_target="tpu_custom_call" | custom-call | flops 503316480 | bytes 3944448 | tf_op jit(solution)/shard_map/norm1_back/pallas_call | solution.py:744
  192.3 0.8 collective-permute-done.28.refs_1_
  193.8 0.9 collective-permute-start.33
  194.7 1.7 collective-permute-start.34
  196.5 2.0 collective-permute-start.30
  198.5 7.2 %collective-permute-done.30.came_ref = bf16[576,128]{1,0:T(8,128)(2,1)S(1)} collective-permute-done((bf16[576,128]{1,0:T(8,128)(2,1)S(1)}, bf16[576,128]{1,0:T(8,128)(2,1)S(1)}, u32[]{:S(2)}, u32[]{:S(2)}) %collective-permute-start.30) | collective-permute-done | bytes 147488 | tf_op jit(solution)/shard_map/ppermute | solution.py:847
  205.8 1.7 collective-permute-done.33.refs_1_
  208.1 4.2 %collective-permute-done.32.came_ref = bf16[1088,128]{1,0:T(8,128)(2,1)S(1)} collective-permute-done((bf16[1088,128]{1,0:T(8,128)(2,1)S(1)}, bf16[1088,128]{1,0:T(8,128)(2,1)S(1)}, u32[]{:S(2)}, u32[]{:S(2)}) %collective-permute-start.32) | collective-permute-done | bytes 278560 | tf_op jit(solution)/shard_map/ppermute | solution.py:847
  212.9 0.9 collective-permute-start.36
  213.9 1.0 collective-permute-start.37
  215.0 1.8 collective-permute-start.38
  216.8 1.1 add_convert_fusion
  217.9 2.8 %finish_out_value_near.1 = (f32[3,1024,512]{2,1,0:T(8,128)}, f32[512,1024]{1,0:T(8,128)}) custom-call(s32[3]{0:T(128)S(1)} %pad_add_fusion.where_ref, bf16[2048,128]{1,0:T(8,128)(2,1)S(1)} %stack.21.refs_0_, bf16[2048,128]{1,0:T(8,128)(2,1)S(1)} %collective-permute-done.33.refs_1_, bf16[2048,128]{1,0:T(8,128)(2,1)S(1)} %collective-permute-done.34.refs_2_), custom_call_target="tpu_custom_call" | custom-call | bytes 6291456 | tf_op jit(solution)/shard_map/finish_out_value_near/pallas_call | solution.py:900
  220.7 8.9 %collective-permute-done.37.refs_0_ = bf16[1024,128]{1,0:T(8,128)(2,1)S(1)} collective-permute-done((bf16[1024,128]{1,0:T(8,128)(2,1)S(1)}, bf16[1024,128]{1,0:T(8,128)(2,1)S(1)}, u32[]{:S(2)}, u32[]{:S(2)}) %collective-permute-start.37) | collective-permute-done | bytes 262176 | tf_op jit(solution)/shard_map/ppermute | solution.py:847
  230.3 1.1 collective-permute-start.39
  231.9 1.6 finish_out_value_far.1
  233.5 2.8 %finish_near.1 = (f32[3,1024,512]{2,1,0:T(8,128)}, f32[32,128]{1,0:T(8,128)S(1)}) custom-call(s32[3]{0:T(128)S(1)} %pad_add_fusion.where_ref, bf16[2112,128]{1,0:T(8,128)(2,1)S(1)} %stack.23.refs_0_, bf16[2112,128]{1,0:T(8,128)(2,1)S(1)} %collective-permute-done.35.refs_1_, ...), custom_call_target="tpu_custom_call", output_to_operand_aliasing={{0}: (4, {})} | custom-call | bytes 6291456 | tf_op jit(solution)/shard_map/finish_near/pallas_call | solution.py:1169
  236.8 1.2 collective-permute-done.40.refs_1_
  238.0 2.2 finish_far.1
  (101 shorter events, 12.4 us)
Async XLA Ops:
  0.6 27.5 %copy-start.4 = (s32[256]{0:T(256)S(1)}, s32[256]{0:T(256)}, u32[]{:S(2)}) copy-start(s32[256]{0:T(256)} %param.13) | copy-start | bytes 3076
  3.2 27.8 %copy-start.7 = (s32[1,5]{1,0:T(1,128)S(1)}, s32[1,5]{1,0:T(1,128)}, u32[]{:S(2)}) copy-start(s32[1,5]{1,0:T(1,128)} %lengths_ref.3) | copy-start | bytes 64
  29.0 2.0 collective-permute-start
  30.9 36.7 %copy-start.6 = (bf16[1,2048,1024]{2,1,0:T(8,128)(2,1)S(1)}, bf16[1,2048,1024]{2,1,0:T(8,128)(2,1)}, u32[]{:S(2)}) copy-start(bf16[1,2048,1024]{2,1,0:T(8,128)(2,1)} %param.22) | copy-start | bytes 12582916
  39.4 2.0 collective-permute-start.1
  41.4 21.9 %copy-start = (bf16[320,1024]{1,0:T(8,128)(2,1)S(1)}, bf16[320,1024]{1,0:T(8,128)(2,1)}, u32[]{:S(2)}) copy-start(bf16[320,1024]{1,0:T(8,128)(2,1)} %x_ref.5) | copy-start | bytes 1966084
  41.4 21.9 %copy-start.1 = (bf16[320,1024]{1,0:T(8,128)(2,1)S(1)}, bf16[320,1024]{1,0:T(8,128)(2,1)}, u32[]{:S(2)}) copy-start(bf16[320,1024]{1,0:T(8,128)(2,1)} %grad_ref.3) | copy-start | bytes 1966084
  41.4 21.9 %copy-start.2 = (f32[1024]{0:T(1024)S(1)}, f32[1024]{0:T(1024)}, u32[]{:S(2)}) copy-start(f32[1024]{0:T(1024)} %param.17) | copy-start | bytes 12292
  41.4 21.9 %copy-start.3 = (f32[1024]{0:T(1024)S(1)}, f32[1024]{0:T(1024)}, u32[]{:S(2)}) copy-start(f32[1024]{0:T(1024)} %param.18) | copy-start | bytes 12292
  41.4 26.2 %copy-start.5 = (bf16[1,1024,2048]{2,1,0:T(8,128)(2,1)S(1)}, bf16[1,1024,2048]{2,1,0:T(8,128)(2,1)}, u32[]{:S(2)}) copy-start(bf16[1,1024,2048]{2,1,0:T(8,128)(2,1)} %param.21) | copy-start | bytes 12582916
  64.5 2.9 %collective-permute-start.2 = (bf16[320,1024]{1,0:T(8,128)(2,1)S(1)}, bf16[320,1024]{1,0:T(8,128)(2,1)S(1)}, u32[]{:S(2)}, u32[]{:S(2)}) collective-permute-start(bf16[320,1024]{1,0:T(8,128)(2,1)S(1)} %get-tuple-element.127.h2_ref), channel_id=1, source_target_pairs={{0,1},{1,0},{2,3},{3,2},{4,5},{5,4},{6,7},{7,6},{8,9},{9,8},{10,11... | collective-permute-start | bytes 1966088 | tf_op jit(solution)/shard_map/ppermute | solution.py:847
  64.7 3.0 %collective-permute-start.3 = (bf16[320,1024]{1,0:T(8,128)(2,1)S(1)}, bf16[320,1024]{1,0:T(8,128)(2,1)S(1)}, u32[]{:S(2)}, u32[]{:S(2)}) collective-permute-start(bf16[320,1024]{1,0:T(8,128)(2,1)S(1)} %get-tuple-element.128.up_ref), channel_id=1, source_target_pairs={{0,1},{1,0},{2,3},{3,2},{4,5},{5,4},{6,7},{7,6},{8,9},{9,8},{10,11... | collective-permute-start | bytes 1966088 | tf_op jit(solution)/shard_map/ppermute | solution.py:847
  65.1 15.0 %collective-permute-start.4 = (bf16[256,1024]{1,0:T(8,128)(2,1)}, bf16[256,1024]{1,0:T(8,128)(2,1)S(1)}, u32[]{:S(2)}, u32[]{:S(2)}) collective-permute-start(bf16[256,1024]{1,0:T(8,128)(2,1)} %get-tuple-element.141), channel_id=1, source_target_pairs={{0,6},{2,4},{4,2},{6,0},{8,14},{10,12},{12,10},{14,8},{16,22},{18,... | collective-permute-start | bytes 1572872 | tf_op jit(solution)/shard_map/ppermute | solution.py:847
  80.1 12.1 %copy-start.8 = (bf16[256,1024]{1,0:T(8,128)(2,1)}, bf16[256,1024]{1,0:T(8,128)(2,1)S(1)}, u32[]{:S(2)}) copy-start(bf16[256,1024]{1,0:T(8,128)(2,1)S(1)} %collective-permute-done.4.refs_7_) | copy-start | bytes 1572868
  80.1 2.1 collective-permute-start.5
  82.2 6.9 %copy-start.17 = (bf16[256,1024]{1,0:T(8,128)(2,1)S(1)}, bf16[256,1024]{1,0:T(8,128)(2,1)}, u32[]{:S(2)}) copy-start(bf16[256,1024]{1,0:T(8,128)(2,1)} %get-tuple-element.141) | copy-start | bytes 1572868
  85.4 26.3 %all-to-all-start.2 = ((bf16[32,8,1280]{2,1,0:T(8,128)(2,1)}), bf16[32,8,1280]{2,1,0:T(8,128)(2,1)S(1)}, u32[]{:S(2)}, u32[]{:S(2)}) async-start(bf16[32,8,1280]{2,1,0:T(8,128)(2,1)} %bitcast.14), calls=%async_computation.2 | async-start | bytes 1310720 | tf_op jit(solution)/shard_map/all_to_all | solution.py:962
  89.1 20.9 %collective-permute-start.6 = (bf16[256,1024]{1,0:T(8,128)(2,1)S(1)}, bf16[256,1024]{1,0:T(8,128)(2,1)S(1)}, u32[]{:S(2)}, u32[]{:S(2)}) collective-permute-start(bf16[256,1024]{1,0:T(8,128)(2,1)S(1)} %copy-done.17), channel_id=1, source_target_pairs={{0,2},{2,0},{4,6},{6,4},{8,10},{10,8},{12,14},{14,12},{16,18},{18,... | collective-permute-start | bytes 1572872 | tf_op jit(solution)/shard_map/ppermute | solution.py:847
  90.7 19.5 %collective-permute-start.7 = (bf16[256,1024]{1,0:T(8,128)(2,1)S(1)}, bf16[256,1024]{1,0:T(8,128)(2,1)S(1)}, u32[]{:S(2)}, u32[]{:S(2)}) collective-permute-start(bf16[256,1024]{1,0:T(8,128)(2,1)S(1)} %copy-done.17), channel_id=1, source_target_pairs={{0,4},{2,6},{4,0},{6,2},{8,12},{10,14},{12,8},{14,10},{16,20},{18,... | collective-permute-start | bytes 1572872 | tf_op jit(solution)/shard_map/ppermute | solution.py:847
  92.2 19.4 %collective-permute-start.8 = (bf16[256,1024]{1,0:T(8,128)(2,1)S(1)}, bf16[256,1024]{1,0:T(8,128)(2,1)}, u32[]{:S(2)}, u32[]{:S(2)}) collective-permute-start(bf16[256,1024]{1,0:T(8,128)(2,1)S(1)} %collective-permute-done.4.refs_7_), channel_id=1, source_target_pairs={{0,1},{1,0},{2,3},{3,2},{4,5},{5,4},{6,7},{7,6},{8,9},{9,8},{10,11... | collective-permute-start | bytes 1572872 | tf_op jit(solution)/shard_map/ppermute | solution.py:847
  110.0 0.8 copy-start.9
  110.8 0.8 copy-start.11
  111.6 1.0 copy-start.10
  111.6 1.4 copy-start.12
  112.4 2.0 collective-permute-start.9
  112.7 17.4 %collective-permute-start.13 = (bf16[256,1024]{1,0:T(8,128)(2,1)S(1)}, bf16[256,1024]{1,0:T(8,128)(2,1)S(1)}, u32[]{:S(2)}, u32[]{:S(2)}) collective-permute-start(bf16[256,1024]{1,0:T(8,128)(2,1)S(1)} %copy-done.10), channel_id=1, source_target_pairs={{0,1},{1,0},{2,3},{3,2},{4,5},{5,4},{6,7},{7,6},{8,9},{9,8},{10,11... | collective-permute-start | bytes 1572872 | tf_op jit(solution)/shard_map/ppermute | solution.py:847
  113.0 17.0 %collective-permute-start.14 = (bf16[256,1024]{1,0:T(8,128)(2,1)S(1)}, bf16[256,1024]{1,0:T(8,128)(2,1)S(1)}, u32[]{:S(2)}, u32[]{:S(2)}) collective-permute-start(bf16[256,1024]{1,0:T(8,128)(2,1)S(1)} %copy-done.12), channel_id=1, source_target_pairs={{0,1},{1,0},{2,3},{3,2},{4,5},{5,4},{6,7},{7,6},{8,9},{9,8},{10,11... | collective-permute-start | bytes 1572872 | tf_op jit(solution)/shard_map/ppermute | solution.py:847
  117.5 12.5 %collective-permute-start.10 = (bf16[4,256,128]{2,1,0:T(8,128)(2,1)S(1)}, bf16[4,256,128]{2,1,0:T(8,128)(2,1)S(1)}, u32[]{:S(2)}, u32[]{:S(2)}) collective-permute-start(bf16[4,256,128]{2,1,0:T(8,128)(2,1)S(1)} %get-tuple-element.157), channel_id=1, source_target_pairs={{0,2},{2,0},{4,6},{6,4},{8,10},{10,8},{12,14},{14,12},{16,18},{18,... | collective-permute-start | bytes 786440 | tf_op jit(solution)/shard_map/ppermute | solution.py:847
  118.3 12.6 %collective-permute-start.11 = (bf16[4,256,128]{2,1,0:T(8,128)(2,1)S(1)}, bf16[4,256,128]{2,1,0:T(8,128)(2,1)S(1)}, u32[]{:S(2)}, u32[]{:S(2)}) collective-permute-start(bf16[4,256,128]{2,1,0:T(8,128)(2,1)S(1)} %get-tuple-element.158), channel_id=1, source_target_pairs={{0,4},{2,6},{4,0},{6,2},{8,12},{10,14},{12,8},{14,10},{16,20},{18,... | collective-permute-start | bytes 786440 | tf_op jit(solution)/shard_map/ppermute | solution.py:847
  119.6 12.8 %collective-permute-start.12 = (bf16[4,256,128]{2,1,0:T(8,128)(2,1)S(1)}, bf16[4,256,128]{2,1,0:T(8,128)(2,1)S(1)}, u32[]{:S(2)}, u32[]{:S(2)}) collective-permute-start(bf16[4,256,128]{2,1,0:T(8,128)(2,1)S(1)} %get-tuple-element.159), channel_id=1, source_target_pairs={{0,6},{2,4},{4,2},{6,0},{8,14},{10,12},{12,10},{14,8},{16,22},{18,... | collective-permute-start | bytes 786440 | tf_op jit(solution)/shard_map/ppermute | solution.py:847
  130.0 12.0 %copy-start.13 = (bf16[256,1024]{1,0:T(8,128)(2,1)}, bf16[256,1024]{1,0:T(8,128)(2,1)S(1)}, u32[]{:S(2)}) copy-start(bf16[256,1024]{1,0:T(8,128)(2,1)S(1)} %collective-permute-done.13.refs_8_) | copy-start | bytes 1572868
  130.0 11.9 %copy-start.14 = (bf16[256,1024]{1,0:T(8,128)(2,1)}, bf16[256,1024]{1,0:T(8,128)(2,1)S(1)}, u32[]{:S(2)}) copy-start(bf16[256,1024]{1,0:T(8,128)(2,1)S(1)} %collective-permute-done.14.refs_9_) | copy-start | bytes 1572868
  132.5 3.5 %collective-permute-start.19 = (bf16[256,1024]{1,0:T(8,128)(2,1)S(1)}, bf16[256,1024]{1,0:T(8,128)(2,1)S(1)}, u32[]{:S(2)}, u32[]{:S(2)}) collective-permute-start(bf16[256,1024]{1,0:T(8,128)(2,1)S(1)} %get-tuple-element.168), channel_id=1, source_target_pairs={{0,1},{1,0},{2,3},{3,2},{4,5},{5,4},{6,7},{7,6},{8,9},{9,8},{10,11... | collective-permute-start | bytes 1572872 | tf_op jit(solution)/shard_map/ppermute | solution.py:847
  132.5 6.5 %collective-permute-start.15 = (bf16[512,128]{1,0:T(8,128)(2,1)}, bf16[512,128]{1,0:T(8,128)(2,1)S(1)}, u32[]{:S(2)}, u32[]{:S(2)}) collective-permute-start(bf16[512,128]{1,0:T(8,128)(2,1)} %get-tuple-element.164), channel_id=1, source_target_pairs={{0,2},{2,0},{4,6},{6,4},{8,10},{10,8},{12,14},{14,12},{16,18},{18,... | collective-permute-start | bytes 393224 | tf_op jit(solution)/shard_map/ppermute | solution.py:847
  133.3 8.6 %collective-permute-start.16 = (bf16[512,128]{1,0:T(8,128)(2,1)}, bf16[512,128]{1,0:T(8,128)(2,1)S(1)}, u32[]{:S(2)}, u32[]{:S(2)}) collective-permute-start(bf16[512,128]{1,0:T(8,128)(2,1)} %get-tuple-element.165), channel_id=1, source_target_pairs={{0,4},{2,6},{4,0},{6,2},{8,12},{10,14},{12,8},{14,10},{16,20},{18,... | collective-permute-start | bytes 393224 | tf_op jit(solution)/shard_map/ppermute | solution.py:847
  134.8 7.2 %collective-permute-start.17 = (bf16[512,128]{1,0:T(8,128)(2,1)}, bf16[512,128]{1,0:T(8,128)(2,1)S(1)}, u32[]{:S(2)}, u32[]{:S(2)}) collective-permute-start(bf16[512,128]{1,0:T(8,128)(2,1)} %get-tuple-element.166), channel_id=1, source_target_pairs={{0,6},{2,4},{4,2},{6,0},{8,14},{10,12},{12,10},{14,8},{16,22},{18,... | collective-permute-start | bytes 393224 | tf_op jit(solution)/shard_map/ppermute | solution.py:847
  142.0 45.9 %all-to-all-start.3 = ((bf16[32,8,1280]{2,1,0:T(8,128)(2,1)}), bf16[32,8,1280]{2,1,0:T(8,128)(2,1)S(1)}, u32[]{:S(2)}, u32[]{:S(2)}) async-start(bf16[32,8,1280]{2,1,0:T(8,128)(2,1)} %bitcast.16), calls=%async_computation.3 | async-start | bytes 1310720 | tf_op jit(solution)/shard_map/all_to_all | solution.py:962
  146.8 5.0 %copy-start.20 = (bf16[2,512,128]{2,1,0:T(8,128)(2,1)S(1)}, bf16[2,512,128]{2,1,0:T(8,128)(2,1)}, u32[]{:S(2)}) copy-start(bf16[2,512,128]{2,1,0:T(8,128)(2,1)} %get-tuple-element.188) | copy-start | bytes 786436
  146.8 6.4 %copy-start.19 = (bf16[2,512,128]{2,1,0:T(8,128)(2,1)S(1)}, bf16[2,512,128]{2,1,0:T(8,128)(2,1)}, u32[]{:S(2)}) copy-start(bf16[2,512,128]{2,1,0:T(8,128)(2,1)} %get-tuple-element.189) | copy-start | bytes 786436
  146.8 7.9 %copy-start.18 = (bf16[2,512,128]{2,1,0:T(8,128)(2,1)S(1)}, bf16[2,512,128]{2,1,0:T(8,128)(2,1)}, u32[]{:S(2)}) copy-start(bf16[2,512,128]{2,1,0:T(8,128)(2,1)} %get-tuple-element.190) | copy-start | bytes 786436
  150.2 15.4 %collective-permute-start.23 = (bf16[2,512,128]{2,1,0:T(8,128)(2,1)S(1)}, bf16[2,512,128]{2,1,0:T(8,128)(2,1)S(1)}, u32[]{:S(2)}, u32[]{:S(2)}) collective-permute-start(bf16[2,512,128]{2,1,0:T(8,128)(2,1)S(1)} %get-tuple-element.176), channel_id=1, source_target_pairs={{0,8},{2,10},{4,12},{6,14},{8,0},{10,2},{12,4},{14,6},{16,24},{18,... | collective-permute-start | bytes 786440 | tf_op jit(solution)/shard_map/ppermute | solution.py:847
  151.8 16.9 %collective-permute-start.20 = (bf16[2,512,128]{2,1,0:T(8,128)(2,1)S(1)}, bf16[2,512,128]{2,1,0:T(8,128)(2,1)S(1)}, u32[]{:S(2)}, u32[]{:S(2)}) collective-permute-start(bf16[2,512,128]{2,1,0:T(8,128)(2,1)S(1)} %copy-done.20), channel_id=1, source_target_pairs={{0,2},{2,0},{4,6},{6,4},{8,10},{10,8},{12,14},{14,12},{16,18},{18,... | collective-permute-start | bytes 786440 | tf_op jit(solution)/shard_map/ppermute | solution.py:847
  153.3 16.3 %collective-permute-start.21 = (bf16[2,512,128]{2,1,0:T(8,128)(2,1)S(1)}, bf16[2,512,128]{2,1,0:T(8,128)(2,1)S(1)}, u32[]{:S(2)}, u32[]{:S(2)}) collective-permute-start(bf16[2,512,128]{2,1,0:T(8,128)(2,1)S(1)} %copy-done.19), channel_id=1, source_target_pairs={{0,4},{2,6},{4,0},{6,2},{8,12},{10,14},{12,8},{14,10},{16,20},{18,... | collective-permute-start | bytes 786440 | tf_op jit(solution)/shard_map/ppermute | solution.py:847
  154.7 14.8 %collective-permute-start.22 = (bf16[2,512,128]{2,1,0:T(8,128)(2,1)S(1)}, bf16[2,512,128]{2,1,0:T(8,128)(2,1)S(1)}, u32[]{:S(2)}, u32[]{:S(2)}) collective-permute-start(bf16[2,512,128]{2,1,0:T(8,128)(2,1)S(1)} %copy-done.18), channel_id=1, source_target_pairs={{0,6},{2,4},{4,2},{6,0},{8,14},{10,12},{12,10},{14,8},{16,22},{18,... | collective-permute-start | bytes 786440 | tf_op jit(solution)/shard_map/ppermute | solution.py:847
  166.2 8.6 %collective-permute-start.25 = (bf16[1,512,128]{2,1,0:T(8,128)(2,1)S(1)}, bf16[1,512,128]{2,1,0:T(8,128)(2,1)S(1)}, u32[]{:S(2)}, u32[]{:S(2)}) collective-permute-start(bf16[1,512,128]{2,1,0:T(8,128)(2,1)S(1)} %get-tuple-element.193), channel_id=1, source_target_pairs={{0,16},{2,18},{4,20},{6,22},{8,24},{10,26},{12,28},{14,30},{16,0},... | collective-permute-start | bytes 393224 | tf_op jit(solution)/shard_map/ppermute | solution.py:847
  173.3 10.6 %collective-permute-start.24 = (bf16[2,512,128]{2,1,0:T(8,128)(2,1)S(1)}, bf16[2,512,128]{2,1,0:T(8,128)(2,1)S(1)}, u32[]{:S(2)}, u32[]{:S(2)}) collective-permute-start(bf16[2,512,128]{2,1,0:T(8,128)(2,1)S(1)} %get-tuple-element.198), channel_id=1, source_target_pairs={{0,8},{2,10},{4,12},{6,14},{8,0},{10,2},{12,4},{14,6},{16,24},{18,... | collective-permute-start | bytes 786440 | tf_op jit(solution)/shard_map/ppermute | solution.py:847
  174.9 9.6 %collective-permute-start.27 = (bf16[512,128]{1,0:T(8,128)(2,1)S(1)}, bf16[512,128]{1,0:T(8,128)(2,1)S(1)}, u32[]{:S(2)}, u32[]{:S(2)}) collective-permute-start(bf16[512,128]{1,0:T(8,128)(2,1)S(1)} %last_add.1.own_ref), channel_id=1, source_target_pairs={{0,16},{2,18},{4,20},{6,22},{8,24},{10,26},{12,28},{14,30},{16,0},... | collective-permute-start | bytes 393224 | tf_op jit(solution)/shard_map/ppermute | solution.py:847
  184.5 9.3 %collective-permute-start.31 = (bf16[1024,128]{1,0:T(8,128)(2,1)S(1)}, bf16[1024,128]{1,0:T(8,128)(2,1)S(1)}, u32[]{:S(2)}, u32[]{:S(2)}) collective-permute-start(bf16[1024,128]{1,0:T(8,128)(2,1)S(1)} %stack.20.own_ref), channel_id=1, source_target_pairs={{0,8},{2,10},{4,12},{6,14},{8,0},{10,2},{12,4},{14,6},{16,24},{18,... | collective-permute-start | bytes 786440 | tf_op jit(solution)/shard_map/ppermute | solution.py:847
  185.6 6.7 %collective-permute-start.26 = (bf16[1,512,128]{2,1,0:T(8,128)(2,1)S(1)}, bf16[1,512,128]{2,1,0:T(8,128)(2,1)S(1)}, u32[]{:S(2)}, u32[]{:S(2)}) collective-permute-start(bf16[1,512,128]{2,1,0:T(8,128)(2,1)S(1)} %get-tuple-element.203), channel_id=1, source_target_pairs={{0,16},{2,18},{4,20},{6,22},{8,24},{10,26},{12,28},{14,30},{16,0},... | collective-permute-start | bytes 393224 | tf_op jit(solution)/shard_map/ppermute | solution.py:847
  187.9 4.4 %collective-permute-start.29 = (f32[16,128]{1,0:T(8,128)S(1)}, f32[16,128]{1,0:T(8,128)S(1)}, u32[]{:S(2)}, u32[]{:S(2)}) collective-permute-start(f32[16,128]{1,0:T(8,128)S(1)} %get-tuple-element.207.refs_2_), channel_id=1, source_target_pairs={{0,1},{1,0},{2,3},{3,2},{4,5},{5,4},{6,7},{7,6},{8,9},{9,8},{10,11... | collective-permute-start | bytes 24584 | tf_op jit(solution)/shard_map/ppermute | solution.py:847
  187.9 10.6 %copy-start.16 = (bf16[320,1024]{1,0:T(8,128)(2,1)S(1)}, bf16[320,1024]{1,0:T(8,128)(2,1)}, u32[]{:S(2)}) copy-start(bf16[320,1024]{1,0:T(8,128)(2,1)} %get-tuple-element.179) | copy-start | bytes 1966084
  191.8 1.3 collective-permute-start.28
  193.8 23.0 %copy-start.15 = (bf16[320,1024]{1,0:T(8,128)(2,1)S(1)}, bf16[320,1024]{1,0:T(8,128)(2,1)}, u32[]{:S(2)}) copy-start(bf16[320,1024]{1,0:T(8,128)(2,1)} %get-tuple-element.178) | copy-start | bytes 1966084
  193.8 13.7 %collective-permute-start.33 = (bf16[2048,128]{1,0:T(8,128)(2,1)S(1)}, bf16[2048,128]{1,0:T(8,128)(2,1)S(1)}, u32[]{:S(2)}, u32[]{:S(2)}) collective-permute-start(bf16[2048,128]{1,0:T(8,128)(2,1)S(1)} %stack.21.refs_0_), channel_id=1, source_target_pairs={{0,2},{2,0},{4,6},{6,4},{8,10},{10,8},{12,14},{14,12},{16,18},{18,... | collective-permute-start | bytes 1572872 | tf_op jit(solution)/shard_map/ppermute | solution.py:847
  194.7 13.3 %collective-permute-start.34 = (bf16[2048,128]{1,0:T(8,128)(2,1)S(1)}, bf16[2048,128]{1,0:T(8,128)(2,1)S(1)}, u32[]{:S(2)}, u32[]{:S(2)}) collective-permute-start(bf16[2048,128]{1,0:T(8,128)(2,1)S(1)} %stack.21.refs_0_), channel_id=1, source_target_pairs={{0,4},{2,6},{4,0},{6,2},{8,12},{10,14},{12,8},{14,10},{16,20},{18,... | collective-permute-start | bytes 1572872 | tf_op jit(solution)/shard_map/ppermute | solution.py:847
  196.5 9.2 %collective-permute-start.30 = (bf16[576,128]{1,0:T(8,128)(2,1)S(1)}, bf16[576,128]{1,0:T(8,128)(2,1)S(1)}, u32[]{:S(2)}, u32[]{:S(2)}) collective-permute-start(bf16[576,128]{1,0:T(8,128)(2,1)S(1)} %last_add_sums.1.own_ref), channel_id=1, source_target_pairs={{0,16},{2,18},{4,20},{6,22},{8,24},{10,26},{12,28},{14,30},{16,0},... | collective-permute-start | bytes 442376 | tf_op jit(solution)/shard_map/ppermute | solution.py:847
  198.5 18.3 %collective-permute-start.18 = (bf16[320,1024]{1,0:T(8,128)(2,1)S(1)}, bf16[320,1024]{1,0:T(8,128)(2,1)S(1)}, u32[]{:S(2)}, u32[]{:S(2)}) collective-permute-start(bf16[320,1024]{1,0:T(8,128)(2,1)S(1)} %copy-done.16), channel_id=1, source_target_pairs={{0,1},{1,0},{2,3},{3,2},{4,5},{5,4},{6,7},{7,6},{8,9},{9,8},{10,11... | collective-permute-start | bytes 1966088 | tf_op jit(solution)/shard_map/ppermute | solution.py:847
  205.7 6.6 %collective-permute-start.32 = (bf16[1088,128]{1,0:T(8,128)(2,1)S(1)}, bf16[1088,128]{1,0:T(8,128)(2,1)S(1)}, u32[]{:S(2)}, u32[]{:S(2)}) collective-permute-start(bf16[1088,128]{1,0:T(8,128)(2,1)S(1)} %stack.22.own_ref), channel_id=1, source_target_pairs={{0,8},{2,10},{4,12},{6,14},{8,0},{10,2},{12,4},{14,6},{16,24},{18,... | collective-permute-start | bytes 835592 | tf_op jit(solution)/shard_map/ppermute | solution.py:847
  212.4 17.9 %collective-permute-start.35 = (bf16[2112,128]{1,0:T(8,128)(2,1)S(1)}, bf16[2112,128]{1,0:T(8,128)(2,1)S(1)}, u32[]{:S(2)}, u32[]{:S(2)}) collective-permute-start(bf16[2112,128]{1,0:T(8,128)(2,1)S(1)} %stack.23.refs_0_), channel_id=1, source_target_pairs={{0,2},{2,0},{4,6},{6,4},{8,10},{10,8},{12,14},{14,12},{16,18},{18,... | collective-permute-start | bytes 1622024 | tf_op jit(solution)/shard_map/ppermute | solution.py:847
  212.9 17.4 %collective-permute-start.36 = (bf16[2112,128]{1,0:T(8,128)(2,1)S(1)}, bf16[2112,128]{1,0:T(8,128)(2,1)S(1)}, u32[]{:S(2)}, u32[]{:S(2)}) collective-permute-start(bf16[2112,128]{1,0:T(8,128)(2,1)S(1)} %stack.23.refs_0_), channel_id=1, source_target_pairs={{0,4},{2,6},{4,0},{6,2},{8,12},{10,14},{12,8},{14,10},{16,20},{18,... | collective-permute-start | bytes 1622024 | tf_op jit(solution)/shard_map/ppermute | solution.py:847
  213.9 15.8 %collective-permute-start.37 = (bf16[1024,128]{1,0:T(8,128)(2,1)S(1)}, bf16[1024,128]{1,0:T(8,128)(2,1)S(1)}, u32[]{:S(2)}, u32[]{:S(2)}) collective-permute-start(bf16[1024,128]{1,0:T(8,128)(2,1)S(1)} %slice.16), channel_id=1, source_target_pairs={{0,2},{2,0},{4,6},{6,4},{8,10},{10,8},{12,14},{14,12},{16,18},{18,... | collective-permute-start | bytes 786440 | tf_op jit(solution)/shard_map/ppermute | solution.py:847
  215.0 15.3 %collective-permute-start.38 = (bf16[1024,128]{1,0:T(8,128)(2,1)S(1)}, bf16[1024,128]{1,0:T(8,128)(2,1)S(1)}, u32[]{:S(2)}, u32[]{:S(2)}) collective-permute-start(bf16[1024,128]{1,0:T(8,128)(2,1)S(1)} %slice.17), channel_id=1, source_target_pairs={{0,4},{2,6},{4,0},{6,2},{8,12},{10,14},{12,8},{14,10},{16,20},{18,... | collective-permute-start | bytes 786440 | tf_op jit(solution)/shard_map/ppermute | solution.py:847
  230.3 6.5 %collective-permute-start.39 = (bf16[1056,128]{1,0:T(8,128)(2,1)S(1)}, bf16[1056,128]{1,0:T(8,128)(2,1)S(1)}, u32[]{:S(2)}, u32[]{:S(2)}) collective-permute-start(bf16[1056,128]{1,0:T(8,128)(2,1)S(1)} %slice.18), channel_id=1, source_target_pairs={{0,2},{2,0},{4,6},{6,4},{8,10},{10,8},{12,14},{14,12},{16,18},{18,... | collective-permute-start | bytes 811016 | tf_op jit(solution)/shard_map/ppermute | solution.py:847
  231.5 6.5 %collective-permute-start.40 = (bf16[1056,128]{1,0:T(8,128)(2,1)S(1)}, bf16[1056,128]{1,0:T(8,128)(2,1)S(1)}, u32[]{:S(2)}, u32[]{:S(2)}) collective-permute-start(bf16[1056,128]{1,0:T(8,128)(2,1)S(1)} %slice.19), channel_id=1, source_target_pairs={{0,4},{2,6},{4,0},{6,2},{8,12},{10,14},{12,8},{14,10},{16,20},{18,... | collective-permute-start | bytes 811016 | tf_op jit(solution)/shard_map/ppermute | solution.py:847
